TPU v7x, 32 devices: a whole 2x2x4 slice. The times are simulated.
32 devices in a mesh: groups: 2 (over y), seq: 4 (over z), tp: 2 (over x), rep: 2 (over core).
Axes of the slice: x: 2, y: 2, z: 4, core: 2. Of those that a mesh axis runs over, the one named last changes fastest.
Arguments:
- queries: bfloat16 [1024, 8192], P(('groups', 'seq'), ('tp', 'rep')), parts along dimension 0, may hold values from -8 to 8
- keys: bfloat16 [1024, 1024], P(('groups', 'seq'), ('tp', 'rep')), parts along dimension 0, may hold values from -5 to 5
- values: bfloat16 [1024, 1024], P(('groups', 'seq'), ('tp', 'rep')), parts along dimension 0, may hold values from -6 to 6
- query_owner: int32 [1024, 1], P(('groups', 'seq')), parts along dimension 0, may hold values from 0 to 3; in each aligned block of 128 rows (0 to 127, 128 to 255, ...) at most 48 rows name the same one
- cache_owner: int32 [1024, 1], P(('groups', 'seq')), parts along dimension 0, may hold values from 0 to 3; in each aligned block of 128 rows (0 to 127, 128 to 255, ...) at most 48 rows name the same one
Outputs:
- attended: bfloat16 [1536, 8192], P(('groups', 'seq'), ('tp', 'rep')), parts along dimension 0
- key_cache: bfloat16 [1536, 1024], P(('groups', 'seq'), ('tp', 'rep')), parts along dimension 0
- value_cache: bfloat16 [1536, 1024], P(('groups', 'seq'), ('tp', 'rep')), parts along dimension 0
There are 2 independent parts, one for each index of `groups`. A program takes and returns all parts, laid end to end along the dimension named above; each array names one. Nothing has to cross between parts.
Inputs may be any that keep to these rules, and one draw needn't show every extreme that they name: `query_owner`: among the rows of one instance no instance is named more than 48 times. `cache_owner`: among the rows of one instance no instance is named more than 48 times.
All inputs are finite; a program needn't handle non-finite values.
Results may differ from a plain program's by a relative error of at most 0.0045.
Values may be sent and summed in bfloat16 or wider, within the bound.
No kernel may reach another device: no remote copies, remote signals or barrier semaphores. Data moves between devices by JAX's collectives and lax.ppermute only.
A program may use at most 64 MiB of HBM per device.

v0:
```python
import math

import jax
import jax.numpy as jnp
from jax import lax
from jax.sharding import PartitionSpec as P

HD = 128


neg_big = -1e30


def slot_select(owner_list, instances, capacity):
    owners = owner_list[:, 0]
    onehot = (owners[:, None] == jnp.arange(instances, dtype=jnp.int32)[None, :]).astype(jnp.int32)
    earlier = jnp.cumsum(onehot, axis=0) - onehot
    ranking = jnp.sum(earlier * onehot, axis=1)
    target = owners * capacity + ranking
    return target[None, :] == jnp.arange(instances * capacity, dtype=jnp.int32)[:, None]


def pack_rows(select, table_rows, instances):
    selected = jnp.dot(
        select.astype(table_rows.dtype), table_rows, preferred_element_type=jnp.float32
    )
    return selected.astype(table_rows.dtype).reshape(instances, -1, table_rows.shape[1])


def start_state(heads_kv, per_group, slot_count):
    running_max = jnp.full((heads_kv, per_group, slot_count), neg_big, jnp.float32)
    running_sum = jnp.zeros((heads_kv, per_group, slot_count), jnp.float32)
    weighted = jnp.zeros((heads_kv, per_group, slot_count, HD), jnp.float32)
    return (running_max, running_sum, weighted)


def key_block(current, grouped, query_pos, key_piece, value_piece, key_start):
    running_max, running_sum, weighted = current
    key_count = key_piece.shape[0]
    heads_kv = grouped.shape[1]
    key_heads = key_piece.reshape(key_count, heads_kv, HD)
    value_heads = value_piece.reshape(key_count, heads_kv, HD)
    scores = jnp.einsum("rkgd,nkd->kgrn", grouped, key_heads, preferred_element_type=jnp.float32)
    scores = scores * (1.0 / math.sqrt(HD))
    key_pos = key_start + jnp.arange(key_count, dtype=jnp.int32)
    allowed = key_pos[None, :] <= query_pos[:, None]
    scores = jnp.where(allowed, scores, neg_big)
    new_max = jnp.maximum(running_max, jnp.max(scores, axis=-1))
    weights = jnp.where(allowed, jnp.exp(scores - new_max[..., None]), 0.0).astype(jnp.bfloat16)
    rescale = jnp.exp(running_max - new_max)
    running_sum = running_sum * rescale + jnp.sum(weights, axis=-1, dtype=jnp.float32)
    weighted = weighted * rescale[..., None] + jnp.einsum(
        "kgrn,nkd->kgrd", weights, value_heads, preferred_element_type=jnp.float32
    )
    return (new_max, running_sum, weighted)


def folder(grouped, query_pos, current, pieces):
    last_pos = jnp.max(query_pos)
    key_part, value_part = pieces
    key_count = key_part.shape[0]
    block_rows = 512
    block_count = key_count // block_rows
    key_blocks = key_part.reshape(block_count, block_rows, key_part.shape[1])
    value_blocks = value_part.reshape(block_count, block_rows, value_part.shape[1])

    def visit(carried, block_item):
        block_index, key_piece, value_piece = block_item
        key_start = block_index * block_rows
        updated = lax.cond(
            key_start <= last_pos,
            lambda inner: key_block(inner, grouped, query_pos, key_piece, value_piece, key_start),
            lambda inner: inner,
            carried,
        )
        return (updated, None)

    current, _ = lax.scan(
        visit, current, (jnp.arange(block_count, dtype=jnp.int32), key_blocks, value_blocks)
    )
    return current


def finish(current, slot_count):
    running_max, running_sum, weighted = current
    denominator = jnp.where(running_sum > 0.0, running_sum, 1.0)
    averaged = weighted / denominator[..., None]
    return jnp.transpose(averaged, (2, 0, 1, 3)).reshape(slot_count, -1).astype(jnp.bfloat16)


def on_device(queries, keys, values, query_owner, cache_owner):
    instances = lax.axis_size("seq")
    own_index = lax.axis_index("seq")
    local_rows = queries.shape[0]
    capacity = 3 * local_rows // (2 * instances)
    slot_count = instances * capacity
    heads_kv = keys.shape[1] // HD
    per_group = queries.shape[1] // keys.shape[1]
    positions = own_index * local_rows + jnp.arange(local_rows, dtype=jnp.int32)
    cache_pick = slot_select(cache_owner, instances, capacity)
    key_slots = pack_rows(cache_pick, keys, instances)
    value_slots = pack_rows(cache_pick, values, instances)
    query_pick = slot_select(query_owner, instances, capacity)
    query_slots = pack_rows(query_pick, queries, instances)
    slot_pos = jnp.max(jnp.where(query_pick, positions[None, :], -1), axis=1).reshape(
        instances, capacity
    )
    query_got, pos_got, key_got, value_got = (
        lax.all_to_all(query_slots, "seq", split_axis=0, concat_axis=0, tiled=True),
        lax.all_to_all(slot_pos, "seq", split_axis=0, concat_axis=0, tiled=True),
        lax.all_to_all(key_slots, "seq", split_axis=0, concat_axis=0, tiled=True),
        lax.all_to_all(value_slots, "seq", split_axis=0, concat_axis=0, tiled=True),
    )
    arrived = query_got.reshape(slot_count, -1)
    arrived_pos = pos_got.reshape(slot_count)
    grouped = arrived.reshape(slot_count, heads_kv, per_group, HD)
    final_state = folder(
        grouped,
        arrived_pos,
        start_state(heads_kv, per_group, slot_count),
        (
            lax.all_gather(keys, "seq", axis=0, tiled=True),
            lax.all_gather(values, "seq", axis=0, tiled=True),
        ),
    )
    attended = finish(final_state, slot_count)
    key_cache = key_got.reshape(slot_count, -1)
    value_cache = value_got.reshape(slot_count, -1)
    return (attended, key_cache, value_cache)


def solution(mesh):
    return jax.shard_map(
        on_device,
        mesh=mesh,
        in_specs=(
            P(("groups", "seq"), ("tp", "rep")),
            P(("groups", "seq"), ("tp", "rep")),
            P(("groups", "seq"), ("tp", "rep")),
            P(("groups", "seq"), None),
            P(("groups", "seq"), None),
        ),
        out_specs=(
            P(("groups", "seq"), ("tp", "rep")),
            P(("groups", "seq"), ("tp", "rep")),
            P(("groups", "seq"), ("tp", "rep")),
        ),
        check_vma=False,
    )
```

profile of v0, /device:TPU:0, one launch (start us, length us, event | category | flops | bytes accessed | tf_op | source)
XLA Modules:
  0.0 98.5 jit_solution(7224170838653600723)
XLA Ops:
  0.6 0.0 copy-start
  0.6 0.8 fusion.7
  1.4 0.2 reduce_window_sum.17
  1.6 0.8 select_reduce_fusion.2
  2.5 0.7 iota_add_fusion
  3.1 0.1 select_reduce_fusion
  3.2 0.7 all_to_all.15
  3.9 6.3 %all-to-all-start = ((s32[4,1,48]{2,1,0:T(1,128)}), s32[4,1,48]{2,1,0:T(1,128)S(1)}, u32[]{:S(2)}, u32[]{:S(2)}) async-start(s32[4,1,48]{2,1,0:T(1,128)} %all_to_all.15), calls=%async_computation | async-start | bytes 4096 | tf_op jit(solution)/shard_map/all_to_all | solution.py:110
  10.2 0.7 fusion.6
  11.0 0.2 reduce_window_sum.18
  11.1 0.8 select_reduce_fusion.1
  12.0 0.7 multiply_add_fusion.2
  12.6 1.6 %convolution_convert_fusion.2 = bf16[192,256]{1,0:T(8,128)(2,1)} fusion(bf16[128,256]{1,0:T(8,128)(2,1)} %param.8, s32[128]{0:T(128)S(1)} %multiply_add_fusion.2), kind=kOutput, calls=%fused_computation.16 | convolution fusion | flops 12656640 | bytes 164352 | tf_op jit(solution)/shard_map/dot_general | solution.py:24
  14.3 1.4 %all-to-all-done = s32[4,1,48]{2,1,0:T(1,128)S(1)} async-done(((s32[4,1,48]{2,1,0:T(1,128)}), s32[4,1,48]{2,1,0:T(1,128)S(1)}, u32[]{:S(2)}, u32[]{:S(2)}) %all-to-all-start) | async-done | bytes 800 | tf_op jit(solution)/shard_map/all_to_all | solution.py:110
  15.7 3.7 %all-to-all-start.2 = ((bf16[4,48,256]{2,1,0:T(8,128)(2,1)}), bf16[4,48,256]{2,1,0:T(8,128)(2,1)S(1)}, u32[]{:S(2)}, u32[]{:S(2)}) async-start(bf16[4,48,256]{2,1,0:T(8,128)(2,1)} %bitcast.7), calls=%async_computation.2 | async-start | bytes 196608 | tf_op jit(solution)/shard_map/all_to_all | solution.py:111
  19.4 1.6 %convolution_convert_fusion.1 = bf16[192,256]{1,0:T(8,128)(2,1)} fusion(bf16[128,256]{1,0:T(8,128)(2,1)} %param.9, s32[128]{0:T(128)S(1)} %multiply_add_fusion.2), kind=kOutput, calls=%fused_computation.15 | convolution fusion | flops 12656640 | bytes 164352 | tf_op jit(solution)/shard_map/dot_general | solution.py:24
  21.0 4.2 %all-to-all-done.2 = bf16[4,48,256]{2,1,0:T(8,128)(2,1)S(1)} async-done(((bf16[4,48,256]{2,1,0:T(8,128)(2,1)}), bf16[4,48,256]{2,1,0:T(8,128)(2,1)S(1)}, u32[]{:S(2)}, u32[]{:S(2)}) %all-to-all-start.2) | async-done | bytes 98336 | tf_op jit(solution)/shard_map/all_to_all | solution.py:111
  25.2 0.0 copy-start.4
  25.2 3.3 %all-to-all-start.3 = ((bf16[4,48,256]{2,1,0:T(8,128)(2,1)}), bf16[4,48,256]{2,1,0:T(8,128)(2,1)S(1)}, u32[]{:S(2)}, u32[]{:S(2)}) async-start(bf16[4,48,256]{2,1,0:T(8,128)(2,1)} %bitcast.9), calls=%async_computation.3 | async-start | bytes 196608 | tf_op jit(solution)/shard_map/all_to_all | solution.py:112
  28.5 0.0 copy-done
  28.5 1.2 %convolution_convert_fusion = bf16[192,2048]{1,0:T(8,128)(2,1)} fusion(bf16[128,2048]{1,0:T(8,128)(2,1)S(1)} %copy-done, s32[128]{0:T(128)S(1)} %get-tuple-element.97), kind=kOutput, calls=%fused_computation.13 | convolution fusion | flops 101081088 | bytes 1311232 | tf_op jit(solution)/shard_map/dot_general | solution.py:24
  29.8 4.5 %all-to-all-done.3 = bf16[4,48,256]{2,1,0:T(8,128)(2,1)S(1)} async-done(((bf16[4,48,256]{2,1,0:T(8,128)(2,1)}), bf16[4,48,256]{2,1,0:T(8,128)(2,1)S(1)}, u32[]{:S(2)}, u32[]{:S(2)}) %all-to-all-start.3) | async-done | bytes 98336 | tf_op jit(solution)/shard_map/all_to_all | solution.py:112
  34.3 0.0 copy-start.5
  34.3 3.5 %all-to-all-start.1 = ((bf16[4,48,2048]{2,1,0:T(8,128)(2,1)}), bf16[4,48,2048]{2,1,0:T(8,128)(2,1)S(1)}, u32[]{:S(2)}, u32[]{:S(2)}) async-start(bf16[4,48,2048]{2,1,0:T(8,128)(2,1)} %bitcast.4), calls=%async_computation.1 | async-start | bytes 1572864 | tf_op jit(solution)/shard_map/all_to_all | solution.py:109
  37.8 0.1 broadcast_in_dim.55
  38.0 24.4 %all_gather.6 = bf16[512,256]{1,0:T(8,128)(2,1)S(1)} all-gather(bf16[128,256]{1,0:T(8,128)(2,1)} %param.8), channel_id=1, replica_groups=mesh['groups'=2,'seq'=4,'tp'=2,'rep'=2] {'seq'}, dimensions={0}, use_global_device_ids=true | all-gather | bytes 327680 | tf_op jit(solution)/shard_map/all_gather | solution.py:122
  62.4 15.5 %all_gather.7 = bf16[512,256]{1,0:T(8,128)(2,1)} all-gather(bf16[128,256]{1,0:T(8,128)(2,1)} %param.9), channel_id=1, replica_groups=mesh['groups'=2,'seq'=4,'tp'=2,'rep'=2] {'seq'}, dimensions={0}, use_global_device_ids=true | all-gather | bytes 327680 | tf_op jit(solution)/shard_map/all_gather | solution.py:123
  78.0 0.6 reduce_max.30
  79.2 0.0 all-to-all-done.1
  79.3 0.0 copy-done.4
  79.3 0.0 copy-done.5
  79.3 14.0 %conditional.1 = ((f32[2,8,192]{2,1,0:T(8,128)S(1)}, f32[2,8,192,128]{3,2,1,0:T(8,128)S(1)})) conditional(s32[]{:T(128)} %convert_element_type.42, (f32[2,8,192]{2,1,0:T(8,128)S(1)}, f32[2,8,192,128]{3,2,1,0:T(8,128)S(1)}) %tuple.25, (s32[4,1,48]{2,1,0:T(1,128)S(1)}, bf16[512,256]{1,0:T(8,128)(2,1)S(1)}, bf16[4,48,2048]{2,1,0:T(8,128)(2,1)S(1)}, ...), branch_computations={%region_4.5_spmd, %region_5.8_spmd} | conditional | flops 829793280 | bytes 55857016 | solution.py:70
  79.3 0.0 copy-start.2
  79.3 0.6 broadcast.54
  79.9 0.7 reduce.5
  80.6 0.1 le.25
  80.7 0.1 iota_compare_fusion
  80.8 0.0 copy-done.2
  80.9 1.3 %copy.22 = bf16[24,8,16,128]{3,2,1,0:T(8,128)(2,1)S(1)} copy(bf16[24,8,16,128]{3,1,2,0:T(8,128)(2,1)} %bitcast.35) | data formatting | bytes 1572864 | tf_op jit(solution)/shard_map/while/body/eval_jaxpr/cond
  82.2 0.1 reshape.69
  82.2 0.0 copy-start.3
  82.2 1.4 %fusion = (f32[2,8,192]{2,1,0:T(8,128)S(1)}, f32[2,512,192,8]{1,2,3,0:T(8,128)S(1)}) fusion(pred[192,512]{1,0:T(8,128)(4,1)S(1)} %iota_compare_fusion, bf16[192,2,8,128]{3,2,1,0:T(8,128)(2,1)S(1)} %bitcast.34, bf16[512,2,128,1]{2,1,0,3:T(2,128)(2,1)S(1)} %bitcast.37), kind=kOutput, calls=%fused_computation.3 | convolution fusion | flops 407368704 | bytes 7450624 | tf_op jit(solution)/shard_map/while/body/eval_jaxpr/cond/branch_1_fun/rkgd,nkd->kgrn/dot_general | solution.py:43
  83.6 0.0 copy-start.1
  83.6 2.6 %copy-done.1 = f32[2,512,192,8]{1,2,3,0:T(8,128)} copy-done((f32[2,512,192,8]{1,2,3,0:T(8,128)}, f32[2,512,192,8]{1,2,3,0:T(8,128)S(1)}, u32[]{:S(2)}) %copy-start.1) | copy-done | bytes 6291480 | tf_op jit(solution)/shard_map/while/body/eval_jaxpr/cond
  86.3 2.1 %convert_reduce_fusion = f32[2,8,192]{2,1,0:T(8,128)S(1)} fusion(f32[2,8,192]{2,1,0:T(8,128)S(1)} %broadcast_maximum_fusion, f32[2,512,192,8]{1,2,3,0:T(8,128)S(1)} %get-tuple-element.95, pred[192,512]{1,0:T(8,128)(4,1)S(1)} %iota_compare_fusion), kind=kLoop, calls=%fused_computation.1 | loop fusion | flops 11006976 | bytes 6414336 | tf_op jit(solution)/shard_map/while/body/eval_jaxpr/cond/branch_1_fun/reduce_sum | solution.py:51
  88.4 0.0 copy-done.3
  88.4 0.1 reshape.70
  88.5 4.8 %multiply_add_fusion = f32[2,8,192,128]{3,2,1,0:T(8,128)S(1)} fusion(f32[2,8,192,128]{3,2,1,0:T(8,128)S(1)} %get-tuple-element.83, f32[2,8,192]{2,1,0:T(8,128)S(1)} %get-tuple-element.92, bf16[512,2,128,1]{2,1,0,3:T(2,128)(2,1)S(1)} %bitcast.41, f32[2,512,192,8]{1,2,3,0:T(8,128)} %copy-done.1, f32[2,8,192]{2,1,0:T(8,128)S(1)} %broadcast_maximum_fusion, ...), kind=kOutput, calls=%fused_computation.4 | convolution fusion | flops 411303936 | bytes 9822208 | tf_op jit(solution)/shard_map/while/body/eval_jaxpr/cond/branch_1_fun/kgrn,nkd->kgrd/dot_general | solution.py:52
  93.3 0.5 fusion.5
  93.8 0.5 copy.15
  94.3 1.1 %copy.35 = bf16[24,8,16,128]{3,1,2,0:T(8,128)(2,1)} copy(bf16[24,8,16,128]{3,2,1,0:T(8,128)(2,1)S(1)} %bitcast.36) | data formatting | bytes 1572864
  95.4 1.5 %copy.42 = bf16[192,256]{1,0:T(8,128)(2,1)} copy(bf16[192,256]{1,0:T(8,128)(2,1)} %bitcast.39) | data formatting | bytes 196608
  97.0 1.5 %copy.43 = bf16[192,256]{1,0:T(8,128)(2,1)} copy(bf16[192,256]{1,0:T(8,128)(2,1)} %bitcast.40) | data formatting | bytes 196608
  (4 shorter events, 0.0 us)
Async XLA Ops:
  0.6 27.9 %copy-start = (bf16[128,2048]{1,0:T(8,128)(2,1)S(1)}, bf16[128,2048]{1,0:T(8,128)(2,1)}, u32[]{:S(2)}) copy-start(bf16[128,2048]{1,0:T(8,128)(2,1)} %param.7) | copy-start | bytes 1572868
  3.9 11.8 %all-to-all-start = ((s32[4,1,48]{2,1,0:T(1,128)}), s32[4,1,48]{2,1,0:T(1,128)S(1)}, u32[]{:S(2)}, u32[]{:S(2)}) async-start(s32[4,1,48]{2,1,0:T(1,128)} %all_to_all.15), calls=%async_computation | async-start | bytes 4096 | tf_op jit(solution)/shard_map/all_to_all | solution.py:110
  15.7 9.5 %all-to-all-start.2 = ((bf16[4,48,256]{2,1,0:T(8,128)(2,1)}), bf16[4,48,256]{2,1,0:T(8,128)(2,1)S(1)}, u32[]{:S(2)}, u32[]{:S(2)}) async-start(bf16[4,48,256]{2,1,0:T(8,128)(2,1)} %bitcast.7), calls=%async_computation.2 | async-start | bytes 196608 | tf_op jit(solution)/shard_map/all_to_all | solution.py:111
  25.2 54.0 %copy-start.4 = (bf16[4,48,256]{2,1,0:T(8,128)(2,1)}, bf16[4,48,256]{2,1,0:T(8,128)(2,1)S(1)}, u32[]{:S(2)}) copy-start(bf16[4,48,256]{2,1,0:T(8,128)(2,1)S(1)} %all-to-all-done.2) | copy-start | bytes 294916
  25.2 9.1 %all-to-all-start.3 = ((bf16[4,48,256]{2,1,0:T(8,128)(2,1)}), bf16[4,48,256]{2,1,0:T(8,128)(2,1)S(1)}, u32[]{:S(2)}, u32[]{:S(2)}) async-start(bf16[4,48,256]{2,1,0:T(8,128)(2,1)} %bitcast.9), calls=%async_computation.3 | async-start | bytes 196608 | tf_op jit(solution)/shard_map/all_to_all | solution.py:112
  34.3 44.9 %copy-start.5 = (bf16[4,48,256]{2,1,0:T(8,128)(2,1)}, bf16[4,48,256]{2,1,0:T(8,128)(2,1)S(1)}, u32[]{:S(2)}) copy-start(bf16[4,48,256]{2,1,0:T(8,128)(2,1)S(1)} %all-to-all-done.3) | copy-start | bytes 294916
  34.3 44.9 %all-to-all-start.1 = ((bf16[4,48,2048]{2,1,0:T(8,128)(2,1)}), bf16[4,48,2048]{2,1,0:T(8,128)(2,1)S(1)}, u32[]{:S(2)}, u32[]{:S(2)}) async-start(bf16[4,48,2048]{2,1,0:T(8,128)(2,1)} %bitcast.4), calls=%async_computation.1 | async-start | bytes 1572864 | tf_op jit(solution)/shard_map/all_to_all | solution.py:109
  79.3 1.6 %copy-start.2 = (bf16[4,48,2048]{2,1,0:T(8,128)(2,1)}, bf16[4,48,2048]{2,1,0:T(8,128)(2,1)S(1)}, u32[]{:S(2)}) copy-start(bf16[4,48,2048]{2,1,0:T(8,128)(2,1)S(1)} %get-tuple-element.82) | copy-start | bytes 2359300 | tf_op jit(solution)/shard_map/while/body/eval_jaxpr/cond
  82.2 6.2 %copy-start.3 = (bf16[512,256]{1,0:T(8,128)(2,1)S(1)}, bf16[512,256]{1,0:T(8,128)(2,1)}, u32[]{:S(2)}) copy-start(bf16[512,256]{1,0:T(8,128)(2,1)} %get-tuple-element.84) | copy-start | bytes 786436 | tf_op jit(solution)/shard_map/while/body/eval_jaxpr/cond
  83.6 2.7 %copy-start.1 = (f32[2,512,192,8]{1,2,3,0:T(8,128)}, f32[2,512,192,8]{1,2,3,0:T(8,128)S(1)}, u32[]{:S(2)}) copy-start(f32[2,512,192,8]{1,2,3,0:T(8,128)S(1)} %get-tuple-element.95) | copy-start | bytes 18874372 | tf_op jit(solution)/shard_map/while/body/eval_jaxpr/cond
where the time goes:
time: 99.3 us; the launch traced here: 98.5 us
  blocking collectives  40 us (40%)
  starting transfers between devices  16.8 us (17%)
  matrix products  10.7 us (11%)
  local copies, waits for them, and re-layouts  10.3 us (10%)
  waiting for transfers between devices  10.1 us (10%)
  other arithmetic  9.02 us (9%)
  between operations  1.43 us (1%)
    all_gather x1, blocking collectives, on_device(): lax.all_gather(keys, 'seq', axis=0, tiled=True)  24.4 us
    all_gather x1, blocking collectives, on_device(): lax.all_gather(values, 'seq', axis=0, tiled=True)  15.5 us
    all_to_all x1, starting transfers between devices, on_device(): lax.all_to_all(slot_pos, 'seq', split_axis=0, concat_axis=0, tiled=True)  6.32 us
    dot_general x1, matrix products, key_block(): jnp.einsum('kgrn,nkd->kgrd', weights, value_heads, preferred_element_type...  4.83 us
    all_to_all x1, waiting for transfers between devices, on_device(): lax.all_to_all(value_slots, 'seq', split_axis=0, concat_axis=0, tiled=True)  4.55 us
    dot_general x3, matrix products, pack_rows(): jnp.dot(select.astype(table_rows.dtype), table_rows, preferred_element_ty...  4.53 us
    all_to_all x1, waiting for transfers between devices, on_device(): lax.all_to_all(key_slots, 'seq', split_axis=0, concat_axis=0, tiled=True)  4.19 us
    unnamed x9, local copies, waits for them, and re-layouts  4.18 us
  transfers between devices with their start and end apart: 4, of which 3 were waited for; matrix products, arithmetic and copies ran while one was open for 8% of the time, Pallas kernels for 0%

commit v1 on v0

--- a/solution.py
+++ b/solution.py
@@ -1,8 +1,11 @@
+import functools
 import math
 
 import jax
 import jax.numpy as jnp
 from jax import lax
+from jax.experimental import pallas as pl
+from jax.experimental.pallas import tpu as pltpu
 from jax.sharding import PartitionSpec as P
 
 HD = 128
@@ -59,7 +62,7 @@
     last_pos = jnp.max(query_pos)
     key_part, value_part = pieces
     key_count = key_part.shape[0]
-    block_rows = 512
+    block_rows = math.gcd(512, key_count)
     block_count = key_count // block_rows
     key_blocks = key_part.reshape(block_count, block_rows, key_part.shape[1])
     value_blocks = value_part.reshape(block_count, block_rows, value_part.shape[1])
@@ -88,7 +91,7 @@
     return jnp.transpose(averaged, (2, 0, 1, 3)).reshape(slot_count, -1).astype(jnp.bfloat16)
 
 
-def on_device(queries, keys, values, query_owner, cache_owner):
+def many_instances(queries, keys, values, query_owner, cache_owner):
     instances = lax.axis_size("seq")
     own_index = lax.axis_index("seq")
     local_rows = queries.shape[0]
@@ -129,6 +132,163 @@
     return (attended, key_cache, value_cache)
 
 
+def before(rows):
+    r = lax.broadcasted_iota(jnp.int32, (rows, rows), 0)
+    u = lax.broadcasted_iota(jnp.int32, (rows, rows), 1)
+    return (r < u).astype(jnp.bfloat16)
+
+
+def picks(marks, earlier, capacity):
+    rows = marks.shape[1]
+    slot = lax.broadcasted_iota(jnp.int32, (capacity, rows), 0).astype(jnp.float32)
+    chosen = jnp.where(marks > 0.5, earlier, -1.0)
+    return (chosen == slot).astype(jnp.bfloat16)
+
+
+def pack_kernel(instances, capacity, q_ref, k_ref, v_ref, qo_ref, co_ref, send_ref):
+    rows = q_ref.shape[0]
+    heads = q_ref.shape[1] // HD
+    heads_kv = k_ref.shape[1] // HD
+    owners = qo_ref[...]
+    lanes = max(16, instances)
+    dest = lax.broadcasted_iota(jnp.int32, (lanes, rows), 0)
+    marks = (jnp.broadcast_to(owners, (lanes, rows)) == dest).astype(jnp.bfloat16)
+    earlier = jnp.dot(marks, before(rows), preferred_element_type=jnp.float32)
+    wide = marks.astype(jnp.float32)
+    select = jnp.concatenate(
+        [picks(wide[d : d + 1], earlier[d : d + 1], capacity) for d in range(instances)], axis=0
+    )
+    for pair in range(heads // 2):
+        packed = jnp.dot(
+            select,
+            q_ref[:, pair * 2 * HD : (pair + 1) * 2 * HD],
+            preferred_element_type=jnp.float32,
+        ).astype(jnp.bfloat16)
+        for d in range(instances):
+            for half in range(2):
+                at = (2 * pair + half) * capacity
+                send_ref[d, at : at + capacity, :] = packed[
+                    d * capacity : (d + 1) * capacity, half * HD : (half + 1) * HD
+                ]
+    base = heads * capacity
+    lists = jnp.concatenate(
+        [owners, co_ref[...], jnp.full((14, rows), -1, jnp.int32)], axis=0
+    ).astype(jnp.float32).astype(jnp.bfloat16)
+    for d in range(instances):
+        for g in range(heads_kv):
+            send_ref[d, base + g * rows : base + (g + 1) * rows, :] = k_ref[:, g * HD : (g + 1) * HD]
+            at = base + (heads_kv + g) * rows
+            send_ref[d, at : at + rows, :] = v_ref[:, g * HD : (g + 1) * HD]
+        at = base + 2 * heads_kv * rows
+        send_ref[d, at : at + 16, :] = lists
+
+
+def attend_kernel(
+    instances, capacity, heads, heads_kv, me_ref, got_ref, att_ref, kc_ref, vc_ref, keys, vals
+):
+    rows = 128
+    per_group = heads // heads_kv
+    base = heads * capacity
+    tail = base + 2 * heads_kv * rows
+    me = me_ref[0].astype(jnp.float32)
+    lists = jnp.concatenate([got_ref[s, tail : tail + 16, :] for s in range(instances)], axis=0)
+    wide = (lists.astype(jnp.float32) == me).astype(jnp.float32)
+    earlier = jnp.dot(wide.astype(jnp.bfloat16), before(rows), preferred_element_type=jnp.float32)
+    r = lax.broadcasted_iota(jnp.int32, (rows, 2 * rows), 0)
+    u = lax.broadcasted_iota(jnp.int32, (rows, 2 * rows), 1)
+    reach = ((u <= r) | (u >= rows)).astype(jnp.bfloat16)
+    for s in range(instances):
+        for g in range(heads_kv):
+            keys[g, s * rows : (s + 1) * rows, :] = got_ref[s, base + g * rows : base + (g + 1) * rows, :]
+            at = base + (heads_kv + g) * rows
+            vals[g, s * rows : (s + 1) * rows, :HD] = got_ref[s, at : at + rows, :]
+            vals[g, s * rows : (s + 1) * rows, HD:] = jnp.ones((rows, HD), jnp.bfloat16)
+    scale = 1.0 / math.sqrt(HD)
+    for s in range(instances):
+        q_at, c_at = 16 * s, 16 * s + 1
+        cache_pick = picks(wide[c_at : c_at + 1], earlier[c_at : c_at + 1], capacity)
+        query_pick = picks(wide[q_at : q_at + 1], earlier[q_at : q_at + 1], capacity)
+        slots = slice(s * capacity, (s + 1) * capacity)
+        for g in range(heads_kv):
+            columns = slice(g * HD, (g + 1) * HD)
+            both = jnp.concatenate(
+                [
+                    got_ref[s, base + g * rows : base + (g + 1) * rows, :],
+                    got_ref[s, base + (heads_kv + g) * rows : base + (heads_kv + g + 1) * rows, :],
+                ],
+                axis=1,
+            )
+            cached = jnp.dot(cache_pick, both, preferred_element_type=jnp.float32).astype(jnp.bfloat16)
+            kc_ref[slots, columns] = cached[:, :HD]
+            vc_ref[slots, columns] = cached[:, HD:]
+        allowed = jnp.dot(query_pick, reach, preferred_element_type=jnp.float32)
+        near = jnp.concatenate([allowed[:, :rows]] * per_group, axis=0) > 0.5
+        valid = jnp.concatenate([allowed[:, rows:]] * per_group, axis=0) > 0.5
+        for g in range(heads_kv):
+            wanted = got_ref[s, g * per_group * capacity : (g + 1) * per_group * capacity, :]
+            scores = lax.dot_general(
+                wanted,
+                keys[g, : (s + 1) * rows, :],
+                (((1,), (1,)), ((), ())),
+                preferred_element_type=jnp.float32,
+            )
+            last = jnp.where(near, scores[:, s * rows :], neg_big)
+            scores = jnp.concatenate([scores[:, : s * rows], last], axis=1) if s else last
+            top = jnp.max(scores, axis=1, keepdims=True)
+            weights = jnp.exp((scores - top) * scale).astype(jnp.bfloat16)
+            mixed = jnp.dot(weights, vals[g, : (s + 1) * rows, :], preferred_element_type=jnp.float32)
+            out = jnp.where(valid, mixed[:, :HD] / mixed[:, HD:], 0.0).astype(jnp.bfloat16)
+            for h in range(per_group):
+                column = (g * per_group + h) * HD
+                att_ref[slots, column : column + HD] = out[h * capacity : (h + 1) * capacity, :]
+
+
+def few_instances(queries, keys, values, query_owner, cache_owner):
+    instances = lax.axis_size("seq")
+    rows = queries.shape[0]
+    capacity = 3 * rows // (2 * instances)
+    heads, heads_kv = queries.shape[1] // HD, keys.shape[1] // HD
+    height = heads * capacity + 2 * heads_kv * rows + 16
+    vmem = pl.BlockSpec(memory_space=pltpu.VMEM)
+    send = pl.pallas_call(
+        functools.partial(pack_kernel, instances, capacity),
+        out_shape=jax.ShapeDtypeStruct((instances, height, HD), jnp.bfloat16),
+        in_specs=[vmem] * 5,
+        out_specs=vmem,
+        compiler_params=pltpu.CompilerParams(vmem_limit_bytes=16 << 20),
+        name="pack",
+    )(queries, keys, values, query_owner.reshape(1, rows), cache_owner.reshape(1, rows))
+    got = lax.all_to_all(send, "seq", split_axis=0, concat_axis=0, tiled=True)
+    me = lax.axis_index("seq").astype(jnp.int32).reshape(1)
+    slots = instances * capacity
+    return pl.pallas_call(
+        functools.partial(attend_kernel, instances, capacity, heads, heads_kv),
+        out_shape=(
+            jax.ShapeDtypeStruct((slots, heads * HD), jnp.bfloat16),
+            jax.ShapeDtypeStruct((slots, heads_kv * HD), jnp.bfloat16),
+            jax.ShapeDtypeStruct((slots, heads_kv * HD), jnp.bfloat16),
+        ),
+        in_specs=[pl.BlockSpec(memory_space=pltpu.SMEM), vmem],
+        out_specs=(vmem, vmem, vmem),
+        scratch_shapes=[
+            pltpu.VMEM((heads_kv, instances * rows, HD), jnp.bfloat16),
+            pltpu.VMEM((heads_kv, instances * rows, 2 * HD), jnp.bfloat16),
+        ],
+        compiler_params=pltpu.CompilerParams(vmem_limit_bytes=24 << 20),
+        name="attend",
+    )(me, got)
+
+
+def on_device(queries, keys, values, query_owner, cache_owner):
+    instances = lax.axis_size("seq")
+    rows = queries.shape[0]
+    capacity = 3 * rows // (2 * instances)
+    heads = queries.shape[1] // HD
+    whole_tiles = capacity % 16 == 0 and rows == HD and heads % 2 == 0
+    form = few_instances if whole_tiles else many_instances
+    return form(queries, keys, values, query_owner, cache_owner)
+
+
 def solution(mesh):
     return jax.shard_map(
         on_device,

time: 99.3 us -> 48 us (0.48)
  blocking collectives: 40 us -> 0 us
  waiting for transfers between devices: 10.1 us -> 31.7 us
  matrix products: 10.7 us -> 0 us
  starting transfers between devices: 16.8 us -> 6.31 us
  other arithmetic: 9.02 us -> 0 us
  local copies, waits for them, and re-layouts: 10.3 us -> 4.02 us
  Pallas kernels: 0 us -> 4.93 us
    all_gather x2 -> x0, blocking collectives: 40 us -> none  [the longest x1 24.4 us: on_device(): lax.all_gather(keys, 'seq', axis=0, tiled=True)]
    all_to_all x4 -> x1, waiting for transfers between devices: 10.1 us -> 31.7 us  [few_instances(): got = lax.all_to_all(send, 'seq', split_axis=0, concat_axis=0, tiled=True)]
    dot_general x5 -> x0, matrix products: 10.7 us -> none  [the longest x1 4.83 us: key_block(): jnp.einsum('kgrn,nkd->kgrd', weights, value_heads, preferred_element_type...]
    all_to_all x4 -> x1, starting transfers between devices: 16.8 us -> 6.31 us  [few_instances(): got = lax.all_to_all(send, 'seq', split_axis=0, concat_axis=0, tiled=True)]
    pallas_call x0 -> x2, Pallas kernels: none -> 4.93 us  [the longest x1 3.37 us: few_instances(): pl.pallas_call(functools.partial(attend_kernel, instances, capacity, head...]
    cond x7 -> x0, local copies, waits for them, and re-layouts: 3.94 us -> none
    reduce_sum x3 -> x0, other arithmetic: 3.73 us -> none  [the longest x1 2.08 us: key_block(): jnp.sum(weights, axis=-1, dtype=jnp.float32)]
    convert_element_type x3 -> x0, other arithmetic: 2 us -> none  [the longest x2 1.53 us: slot_select(): (owners[:, None] == jnp.arange(instances, dtype=jnp.int32)[None, :]).asty...]
  transfers between devices with their start and end apart: 4 -> 1, of which waited for: 3 -> 1; matrix products, arithmetic and copies ran while one was open for 8% -> 0% of each run, Pallas kernels for 0% -> 0%
where the time goes in v1:
time: 48 us; the launch traced here: 47.6 us
  waiting for transfers between devices  31.7 us (66%)
  starting transfers between devices  6.31 us (13%)
  Pallas kernels  4.93 us (10%)
  local copies, waits for them, and re-layouts  4.02 us (8%)
  between operations  0.65 us (1%)
    all_to_all x1, waiting for transfers between devices, few_instances(): got = lax.all_to_all(send, 'seq', split_axis=0, concat_axis=0, tiled=True)  31.7 us
    all_to_all x1, starting transfers between devices, few_instances(): got = lax.all_to_all(send, 'seq', split_axis=0, concat_axis=0, tiled=True)  6.31 us
    unnamed x10, local copies, waits for them, and re-layouts  4.02 us
    pallas_call x1, Pallas kernels, few_instances(): pl.pallas_call(functools.partial(attend_kernel, instances, capacity, head...  3.37 us
    pallas_call x1, Pallas kernels, few_instances(): pl.pallas_call(functools.partial(pack_kernel, instances, capacity), out_s...  1.56 us
  transfers between devices with their start and end apart: 1, of which 1 were waited for; matrix products, arithmetic and copies ran while one was open for 0% of the time, Pallas kernels for 0%

profile of v1, /device:TPU:0, one launch (start us, length us, event | category | flops | bytes accessed | tf_op | source)
XLA Modules:
  0.0 47.6 jit_solution(10868563510880318564)
XLA Ops:
  0.6 0.0 copy-start
  0.6 1.0 %copy-done = bf16[128,2048]{1,0:T(8,128)(2,1)S(1)} copy-done((bf16[128,2048]{1,0:T(8,128)(2,1)S(1)}, bf16[128,2048]{1,0:T(8,128)(2,1)}, u32[]{:S(2)}) %copy-start) | copy-done | bytes 524312
  1.7 0.0 copy-start.1
  1.7 0.8 %copy-done.1 = bf16[128,256]{1,0:T(8,128)(2,1)S(1)} copy-done((bf16[128,256]{1,0:T(8,128)(2,1)S(1)}, bf16[128,256]{1,0:T(8,128)(2,1)}, u32[]{:S(2)}) %copy-start.1) | copy-done | bytes 65560
  2.5 0.0 copy-start.2
  2.5 0.8 %copy-done.2 = bf16[128,256]{1,0:T(8,128)(2,1)S(1)} copy-done((bf16[128,256]{1,0:T(8,128)(2,1)S(1)}, bf16[128,256]{1,0:T(8,128)(2,1)}, u32[]{:S(2)}) %copy-start.2) | copy-done | bytes 65560
  3.4 0.0 copy-start.3
  3.4 0.7 %copy-done.3 = s32[128,1]{0,1:T(1,128)S(1)} copy-done((s32[128,1]{0,1:T(1,128)S(1)}, s32[128,1]{0,1:T(1,128)}, u32[]{:S(2)}) %copy-start.3) | copy-done | bytes 536
  4.0 0.0 copy-start.4
  4.0 0.7 %copy-done.4 = s32[128,1]{0,1:T(1,128)S(1)} copy-done((s32[128,1]{0,1:T(1,128)S(1)}, s32[128,1]{0,1:T(1,128)}, u32[]{:S(2)}) %copy-start.4) | copy-done | bytes 536
  4.7 1.6 %pack.1 = bf16[4,1296,128]{2,1,0:T(8,128)(2,1)} custom-call(bf16[128,2048]{1,0:T(8,128)(2,1)S(1)} %copy-done, bf16[128,256]{1,0:T(8,128)(2,1)S(1)} %copy-done.1, bf16[128,256]{1,0:T(8,128)(2,1)S(1)} %copy-done.2, s32[1,128]{1,0:T(1,128)S(1)} %bitcast.3, s32[1,128]{1,0:T(1,128)S(1)} %bitcast.4), custom_call_target="tpu_custom_call" | custom-call | tf_op jit(solution)/shard_map/pack/pallas_call | solution.py:253
  6.2 6.3 %all-to-all-start = ((bf16[4,1296,128]{2,1,0:T(8,128)(2,1)}), bf16[4,1296,128]{2,1,0:T(8,128)(2,1)S(1)}, u32[]{:S(2)}, u32[]{:S(2)}) async-start(bf16[4,1296,128]{2,1,0:T(8,128)(2,1)} %pack.1), calls=%async_computation | async-start | bytes 2654208 | tf_op jit(solution)/shard_map/all_to_all | solution.py:261
  12.5 31.7 %all-to-all-done.got_ref = bf16[4,1296,128]{2,1,0:T(8,128)(2,1)S(1)} async-done(((bf16[4,1296,128]{2,1,0:T(8,128)(2,1)}), bf16[4,1296,128]{2,1,0:T(8,128)(2,1)S(1)}, u32[]{:S(2)}, u32[]{:S(2)}) %all-to-all-start) | async-done | bytes 1327136 | tf_op jit(solution)/shard_map/all_to_all | solution.py:261
  44.2 3.4 %attend.1 = (bf16[192,2048]{1,0:T(8,128)(2,1)}, bf16[192,256]{1,0:T(8,128)(2,1)}, bf16[192,256]{1,0:T(8,128)(2,1)}) custom-call(s32[1]{0:T(128)} %bitcast.me_ref, bf16[4,1296,128]{2,1,0:T(8,128)(2,1)S(1)} %all-to-all-done.got_ref), custom_call_target="tpu_custom_call" | custom-call | tf_op jit(solution)/shard_map/attend/pallas_call | solution.py:264
Async XLA Ops:
  0.6 1.0 %copy-start = (bf16[128,2048]{1,0:T(8,128)(2,1)S(1)}, bf16[128,2048]{1,0:T(8,128)(2,1)}, u32[]{:S(2)}) copy-start(bf16[128,2048]{1,0:T(8,128)(2,1)} %q_ref.1) | copy-start | bytes 1572868
  1.7 0.8 %copy-start.1 = (bf16[128,256]{1,0:T(8,128)(2,1)S(1)}, bf16[128,256]{1,0:T(8,128)(2,1)}, u32[]{:S(2)}) copy-start(bf16[128,256]{1,0:T(8,128)(2,1)} %k_ref.1) | copy-start | bytes 196612
  2.5 0.8 %copy-start.2 = (bf16[128,256]{1,0:T(8,128)(2,1)S(1)}, bf16[128,256]{1,0:T(8,128)(2,1)}, u32[]{:S(2)}) copy-start(bf16[128,256]{1,0:T(8,128)(2,1)} %v_ref.1) | copy-start | bytes 196612
  3.4 0.7 %copy-start.3 = (s32[128,1]{0,1:T(1,128)S(1)}, s32[128,1]{0,1:T(1,128)}, u32[]{:S(2)}) copy-start(s32[128,1]{0,1:T(1,128)} %param.8) | copy-start | bytes 1540
  4.0 0.7 %copy-start.4 = (s32[128,1]{0,1:T(1,128)S(1)}, s32[128,1]{0,1:T(1,128)}, u32[]{:S(2)}) copy-start(s32[128,1]{0,1:T(1,128)} %param.9) | copy-start | bytes 1540
  6.2 38.0 %all-to-all-start = ((bf16[4,1296,128]{2,1,0:T(8,128)(2,1)}), bf16[4,1296,128]{2,1,0:T(8,128)(2,1)S(1)}, u32[]{:S(2)}, u32[]{:S(2)}) async-start(bf16[4,1296,128]{2,1,0:T(8,128)(2,1)} %pack.1), calls=%async_computation | async-start | bytes 2654208 | tf_op jit(solution)/shard_map/all_to_all | solution.py:261

commit v2 on v1

--- a/solution.py
+++ b/solution.py
@@ -145,79 +145,75 @@
     return (chosen == slot).astype(jnp.bfloat16)
 
 
-def pack_kernel(instances, capacity, q_ref, k_ref, v_ref, qo_ref, co_ref, send_ref):
+def pack_kernel(instances, capacity, me_ref, q_hbm, qo_ref, co_ref, *rest):
+    sends, (q_ref, arrived) = rest[:instances], rest[instances:]
     rows = q_ref.shape[0]
     heads = q_ref.shape[1] // HD
-    heads_kv = k_ref.shape[1] // HD
+    fetch = pltpu.make_async_copy(q_hbm, q_ref, arrived)
+    fetch.start()
+    me = me_ref[0]
     owners = qo_ref[...]
-    lanes = max(16, instances)
-    dest = lax.broadcasted_iota(jnp.int32, (lanes, rows), 0)
-    marks = (jnp.broadcast_to(owners, (lanes, rows)) == dest).astype(jnp.bfloat16)
+    lane = lax.broadcasted_iota(jnp.int32, (16, rows), 0)
+    dest = jnp.bitwise_xor(lane, me)
+    marks = (jnp.broadcast_to(owners, (16, rows)) == dest).astype(jnp.bfloat16)
     earlier = jnp.dot(marks, before(rows), preferred_element_type=jnp.float32)
     wide = marks.astype(jnp.float32)
     select = jnp.concatenate(
-        [picks(wide[d : d + 1], earlier[d : d + 1], capacity) for d in range(instances)], axis=0
-    )
+        [picks(wide[k : k + 1], earlier[k : k + 1], capacity) for k in range(instances)], axis=0
+    )
+    lists = jnp.concatenate(
+        [owners, co_ref[...], jnp.full((14, rows), -1, jnp.int32)], axis=0
+    ).astype(jnp.float32).astype(jnp.bfloat16)
+    for k in range(instances):
+        sends[k][heads * capacity :, :] = lists
+    fetch.wait()
     for pair in range(heads // 2):
         packed = jnp.dot(
             select,
             q_ref[:, pair * 2 * HD : (pair + 1) * 2 * HD],
             preferred_element_type=jnp.float32,
         ).astype(jnp.bfloat16)
-        for d in range(instances):
+        for k in range(instances):
             for half in range(2):
                 at = (2 * pair + half) * capacity
-                send_ref[d, at : at + capacity, :] = packed[
-                    d * capacity : (d + 1) * capacity, half * HD : (half + 1) * HD
+                sends[k][at : at + capacity, :] = packed[
+                    k * capacity : (k + 1) * capacity, half * HD : (half + 1) * HD
                 ]
-    base = heads * capacity
-    lists = jnp.concatenate(
-        [owners, co_ref[...], jnp.full((14, rows), -1, jnp.int32)], axis=0
-    ).astype(jnp.float32).astype(jnp.bfloat16)
-    for d in range(instances):
+
+
+def attend_kernel(instances, capacity, heads, heads_kv, me_ref, *rest):
+    got, rest = rest[:instances], rest[instances:]
+    got_k, rest = rest[:instances], rest[instances:]
+    got_v, rest = rest[:instances], rest[instances:]
+    att_ref, kc_ref, vc_ref, wanted_ref, keys, vals = rest
+    rows = got_k[0].shape[0]
+    per_group = heads // heads_kv
+    tail = heads * capacity
+    me = me_ref[0]
+    for k in range(instances):
+        source = jnp.bitwise_xor(me, k)
+        wanted_ref[source] = got[k][...]
+        at = pl.ds(pl.multiple_of(source * rows, rows), rows)
         for g in range(heads_kv):
-            send_ref[d, base + g * rows : base + (g + 1) * rows, :] = k_ref[:, g * HD : (g + 1) * HD]
-            at = base + (heads_kv + g) * rows
-            send_ref[d, at : at + rows, :] = v_ref[:, g * HD : (g + 1) * HD]
-        at = base + 2 * heads_kv * rows
-        send_ref[d, at : at + 16, :] = lists
-
-
-def attend_kernel(
-    instances, capacity, heads, heads_kv, me_ref, got_ref, att_ref, kc_ref, vc_ref, keys, vals
-):
-    rows = 128
-    per_group = heads // heads_kv
-    base = heads * capacity
-    tail = base + 2 * heads_kv * rows
-    me = me_ref[0].astype(jnp.float32)
-    lists = jnp.concatenate([got_ref[s, tail : tail + 16, :] for s in range(instances)], axis=0)
-    wide = (lists.astype(jnp.float32) == me).astype(jnp.float32)
+            keys[g, at, :] = got_k[k][:, g * HD : (g + 1) * HD]
+            vals[g, at, :HD] = got_v[k][:, g * HD : (g + 1) * HD]
+        vals[:, k * rows : (k + 1) * rows, HD:] = jnp.ones((heads_kv, rows, HD), jnp.bfloat16)
+    lists = jnp.concatenate([wanted_ref[s, tail : tail + 16, :] for s in range(instances)], axis=0)
+    wide = (lists.astype(jnp.float32) == me.astype(jnp.float32)).astype(jnp.float32)
     earlier = jnp.dot(wide.astype(jnp.bfloat16), before(rows), preferred_element_type=jnp.float32)
     r = lax.broadcasted_iota(jnp.int32, (rows, 2 * rows), 0)
     u = lax.broadcasted_iota(jnp.int32, (rows, 2 * rows), 1)
     reach = ((u <= r) | (u >= rows)).astype(jnp.bfloat16)
-    for s in range(instances):
-        for g in range(heads_kv):
-            keys[g, s * rows : (s + 1) * rows, :] = got_ref[s, base + g * rows : base + (g + 1) * rows, :]
-            at = base + (heads_kv + g) * rows
-            vals[g, s * rows : (s + 1) * rows, :HD] = got_ref[s, at : at + rows, :]
-            vals[g, s * rows : (s + 1) * rows, HD:] = jnp.ones((rows, HD), jnp.bfloat16)
     scale = 1.0 / math.sqrt(HD)
     for s in range(instances):
         q_at, c_at = 16 * s, 16 * s + 1
         cache_pick = picks(wide[c_at : c_at + 1], earlier[c_at : c_at + 1], capacity)
         query_pick = picks(wide[q_at : q_at + 1], earlier[q_at : q_at + 1], capacity)
         slots = slice(s * capacity, (s + 1) * capacity)
+        block = slice(s * rows, (s + 1) * rows)
         for g in range(heads_kv):
             columns = slice(g * HD, (g + 1) * HD)
-            both = jnp.concatenate(
-                [
-                    got_ref[s, base + g * rows : base + (g + 1) * rows, :],
-                    got_ref[s, base + (heads_kv + g) * rows : base + (heads_kv + g + 1) * rows, :],
-                ],
-                axis=1,
-            )
+            both = jnp.concatenate([keys[g, block, :], vals[g, block, :HD]], axis=1)
             cached = jnp.dot(cache_pick, both, preferred_element_type=jnp.float32).astype(jnp.bfloat16)
             kc_ref[slots, columns] = cached[:, :HD]
             vc_ref[slots, columns] = cached[:, HD:]
@@ -225,7 +221,7 @@
         near = jnp.concatenate([allowed[:, :rows]] * per_group, axis=0) > 0.5
         valid = jnp.concatenate([allowed[:, rows:]] * per_group, axis=0) > 0.5
         for g in range(heads_kv):
-            wanted = got_ref[s, g * per_group * capacity : (g + 1) * per_group * capacity, :]
+            wanted = wanted_ref[s, g * per_group * capacity : (g + 1) * per_group * capacity, :]
             scores = lax.dot_general(
                 wanted,
                 keys[g, : (s + 1) * rows, :],
@@ -248,18 +244,32 @@
     rows = queries.shape[0]
     capacity = 3 * rows // (2 * instances)
     heads, heads_kv = queries.shape[1] // HD, keys.shape[1] // HD
-    height = heads * capacity + 2 * heads_kv * rows + 16
+
+    def swap(array, k):
+        return lax.ppermute(array, "seq", [(i, i ^ k) for i in range(instances)])
+
+    all_k, all_v = {0: keys}, {0: values}
+    bit = instances // 2
+    while bit:
+        for k in list(all_k):
+            all_k[k ^ bit] = swap(all_k[k], bit)
+            all_v[k ^ bit] = swap(all_v[k], bit)
+        bit //= 2
+    height = heads * capacity + 16
     vmem = pl.BlockSpec(memory_space=pltpu.VMEM)
-    send = pl.pallas_call(
+    smem = pl.BlockSpec(memory_space=pltpu.SMEM)
+    me = lax.axis_index("seq").astype(jnp.int32).reshape(1)
+    sends = pl.pallas_call(
         functools.partial(pack_kernel, instances, capacity),
-        out_shape=jax.ShapeDtypeStruct((instances, height, HD), jnp.bfloat16),
-        in_specs=[vmem] * 5,
-        out_specs=vmem,
+        out_shape=(jax.ShapeDtypeStruct((height, HD), jnp.bfloat16),) * instances,
+        in_specs=[smem, pl.BlockSpec(memory_space=pl.ANY), vmem, vmem],
+        out_specs=(vmem,) * instances,
+        scratch_shapes=[pltpu.VMEM(queries.shape, jnp.bfloat16), pltpu.SemaphoreType.DMA],
         compiler_params=pltpu.CompilerParams(vmem_limit_bytes=16 << 20),
+        cost_estimate=pl.CostEstimate(flops=1 << 27, bytes_accessed=2 << 20, transcendentals=0),
         name="pack",
-    )(queries, keys, values, query_owner.reshape(1, rows), cache_owner.reshape(1, rows))
-    got = lax.all_to_all(send, "seq", split_axis=0, concat_axis=0, tiled=True)
-    me = lax.axis_index("seq").astype(jnp.int32).reshape(1)
+    )(me, queries, query_owner.reshape(1, rows), cache_owner.reshape(1, rows))
+    got = [swap(sends[k], k) if k else sends[0] for k in range(instances)]
     slots = instances * capacity
     return pl.pallas_call(
         functools.partial(attend_kernel, instances, capacity, heads, heads_kv),
@@ -268,15 +278,21 @@
             jax.ShapeDtypeStruct((slots, heads_kv * HD), jnp.bfloat16),
             jax.ShapeDtypeStruct((slots, heads_kv * HD), jnp.bfloat16),
         ),
-        in_specs=[pl.BlockSpec(memory_space=pltpu.SMEM), vmem],
+        in_specs=[smem] + [vmem] * (3 * instances),
         out_specs=(vmem, vmem, vmem),
         scratch_shapes=[
+            pltpu.VMEM((instances, height, HD), jnp.bfloat16),
             pltpu.VMEM((heads_kv, instances * rows, HD), jnp.bfloat16),
             pltpu.VMEM((heads_kv, instances * rows, 2 * HD), jnp.bfloat16),
         ],
         compiler_params=pltpu.CompilerParams(vmem_limit_bytes=24 << 20),
         name="attend",
-    )(me, got)
+    )(
+        me,
+        *got,
+        *[all_k[k] for k in range(instances)],
+        *[all_v[k] for k in range(instances)],
+    )
 
 
 def on_device(queries, keys, values, query_owner, cache_owner):
@@ -284,7 +300,7 @@
     rows = queries.shape[0]
     capacity = 3 * rows // (2 * instances)
     heads = queries.shape[1] // HD
-    whole_tiles = capacity % 16 == 0 and rows == HD and heads % 2 == 0
+    whole_tiles = capacity % 16 == 0 and rows == HD and heads % 2 == 0 and instances & (instances - 1) == 0
     form = few_instances if whole_tiles else many_instances
     return form(queries, keys, values, query_owner, cache_owner)
 

time: 48 us -> 42.5 us (0.89)
  waiting for transfers between devices: 31.7 us -> 20.4 us
  starting transfers between devices: 6.31 us -> 15.6 us
  local copies, waits for them, and re-layouts: 4.02 us -> 1.7 us
  Pallas kernels: 4.93 us -> 3.92 us
    all_to_all x1 -> x0, waiting for transfers between devices: 31.7 us -> none  [few_instances(): got = lax.all_to_all(send, 'seq', split_axis=0, concat_axis=0, tiled=True)]
    ppermute x0 -> x9, waiting for transfers between devices: none -> 20.4 us  [swap(): return lax.ppermute(array, 'seq', [(i, i ^ k) for i in range(instances)])]
    ppermute x0 -> x9, starting transfers between devices: none -> 15.6 us  [swap(): return lax.ppermute(array, 'seq', [(i, i ^ k) for i in range(instances)])]
    all_to_all x1 -> x0, starting transfers between devices: 6.31 us -> none  [few_instances(): got = lax.all_to_all(send, 'seq', split_axis=0, concat_axis=0, tiled=True)]
    unnamed x10, local copies, waits for them, and re-layouts: 4.02 us -> 1.7 us
    pallas_call x1, Pallas kernels: 1.56 us -> 0.54 us  [few_instances(): pl.pallas_call(functools.partial(pack_kernel, instances, capacity), out_s...]
  transfers between devices with their start and end apart: 1 -> 9, of which waited for: 1 -> 5; matrix products, arithmetic and copies ran while one was open for 0% -> 0% of each run, Pallas kernels for 0% -> 0%
where the time goes in v2:
time: 42.5 us; the launch traced here: 42.3 us
  waiting for transfers between devices  20.4 us (48%)
  starting transfers between devices  15.6 us (37%)
  Pallas kernels  3.92 us (9%)
  local copies, waits for them, and re-layouts  1.7 us (4%)
  between operations  0.68 us (2%)
    ppermute x9, waiting for transfers between devices, swap(): return lax.ppermute(array, 'seq', [(i, i ^ k) for i in range(instances)])  20.4 us
    ppermute x9, starting transfers between devices, swap(): return lax.ppermute(array, 'seq', [(i, i ^ k) for i in range(instances)])  15.6 us
    pallas_call x1, Pallas kernels, few_instances(): pl.pallas_call(functools.partial(attend_kernel, instances, capacity, head...  3.37 us
    unnamed x10, local copies, waits for them, and re-layouts  1.7 us
  transfers between devices with their start and end apart: 9, of which 5 were waited for; matrix products, arithmetic and copies ran while one was open for 0% of the time, Pallas kernels for 0%

profile of v2, /device:TPU:0, one launch (start us, length us, event | category | flops | bytes accessed | tf_op | source)
XLA Modules:
  0.0 42.3 jit_solution(10750207571429437465)
XLA Ops:
  0.6 0.0 copy-start.3
  0.6 0.0 copy-start.4
  0.7 0.6 %copy-done.3 = s32[128,1]{0,1:T(1,128)S(1)} copy-done((s32[128,1]{0,1:T(1,128)S(1)}, s32[128,1]{0,1:T(1,128)}, u32[]{:S(2)}) %copy-start.3) | copy-done | bytes 536
  1.3 0.0 copy-done.4
  1.3 0.0 copy-start
  1.3 1.0 %copy-done = bf16[128,2048]{1,0:T(8,128)(2,1)S(1)} copy-done((bf16[128,2048]{1,0:T(8,128)(2,1)S(1)}, bf16[128,2048]{1,0:T(8,128)(2,1)}, u32[]{:S(2)}) %copy-start) | copy-done | bytes 524312
  2.4 0.0 copy-start.1
  2.4 0.0 copy-start.2
  2.4 0.5 %pack.1 = (bf16[784,128]{1,0:T(8,128)(2,1)S(1)}, bf16[784,128]{1,0:T(8,128)(2,1)S(1)}, bf16[784,128]{1,0:T(8,128)(2,1)S(1)}, bf16[784,128]{1,0:T(8,128)(2,1)S(1)}) custom-call(s32[1]{0:T(128)} %bitcast.me_ref, bf16[128,2048]{1,0:T(8,128)(2,1)S(1)} %copy-done, s32[1,128]{1,0:T(1,128)S(1)} %bitcast.3, s32[1,128]{1,0:T(1,128)S(1)} %bitcast.4), custom_call_target="tpu_custom_call" | custom-call | flops 134217728 | bytes 2097152 | tf_op jit(solution)/shard_map/pack/pallas_call | solution.py:262
  2.9 3.1 %collective-permute-start = (bf16[784,128]{1,0:T(8,128)(2,1)S(1)}, bf16[784,128]{1,0:T(8,128)(2,1)S(1)}, u32[]{:S(2)}, u32[]{:S(2)}) collective-permute-start(bf16[784,128]{1,0:T(8,128)(2,1)S(1)} %get-tuple-element.8), channel_id=1, source_target_pairs={{0,4},{4,0},{8,12},{12,8},{1,5},{5,1},{9,13},{13,9},{2,6},{6,2},{1... | collective-permute-start | bytes 602120 | tf_op jit(solution)/shard_map/ppermute | solution.py:249
  6.0 2.6 %collective-permute-start.1 = (bf16[784,128]{1,0:T(8,128)(2,1)S(1)}, bf16[784,128]{1,0:T(8,128)(2,1)S(1)}, u32[]{:S(2)}, u32[]{:S(2)}) collective-permute-start(bf16[784,128]{1,0:T(8,128)(2,1)S(1)} %get-tuple-element.9), channel_id=1, source_target_pairs={{0,8},{4,12},{8,0},{12,4},{1,9},{5,13},{9,1},{13,5},{2,10},{6,14},... | collective-permute-start | bytes 602120 | tf_op jit(solution)/shard_map/ppermute | solution.py:249
  8.6 0.0 collective-permute-start.2
  8.6 0.0 copy-done.1
  8.6 0.9 %collective-permute-start.3 = (bf16[128,256]{1,0:T(8,128)(2,1)S(1)}, bf16[128,256]{1,0:T(8,128)(2,1)S(1)}, u32[]{:S(2)}, u32[]{:S(2)}) collective-permute-start(bf16[128,256]{1,0:T(8,128)(2,1)S(1)} %copy-done.1), channel_id=1, source_target_pairs={{0,4},{4,0},{8,12},{12,8},{1,5},{5,1},{9,13},{13,9},{2,6},{6,2},{1... | collective-permute-start | bytes 196616 | tf_op jit(solution)/shard_map/ppermute | solution.py:249
  9.5 3.5 %collective-permute-start.4 = (bf16[128,256]{1,0:T(8,128)(2,1)S(1)}, bf16[128,256]{1,0:T(8,128)(2,1)S(1)}, u32[]{:S(2)}, u32[]{:S(2)}) collective-permute-start(bf16[128,256]{1,0:T(8,128)(2,1)S(1)} %copy-done.1), channel_id=1, source_target_pairs={{0,8},{4,12},{8,0},{12,4},{1,9},{5,13},{9,1},{13,5},{2,10},{6,14},... | collective-permute-start | bytes 196616 | tf_op jit(solution)/shard_map/ppermute | solution.py:249
  13.0 8.1 %collective-permute-done.3.rest_5_ = bf16[128,256]{1,0:T(8,128)(2,1)S(1)} collective-permute-done((bf16[128,256]{1,0:T(8,128)(2,1)S(1)}, bf16[128,256]{1,0:T(8,128)(2,1)S(1)}, u32[]{:S(2)}, u32[]{:S(2)}) %collective-permute-start.3) | collective-permute-done | bytes 65568 | tf_op jit(solution)/shard_map/ppermute | solution.py:249
  21.0 0.0 copy-done.2
  21.0 2.5 %collective-permute-start.6 = (bf16[128,256]{1,0:T(8,128)(2,1)S(1)}, bf16[128,256]{1,0:T(8,128)(2,1)S(1)}, u32[]{:S(2)}, u32[]{:S(2)}) collective-permute-start(bf16[128,256]{1,0:T(8,128)(2,1)S(1)} %copy-done.2), channel_id=1, source_target_pairs={{0,4},{4,0},{8,12},{12,8},{1,5},{5,1},{9,13},{13,9},{2,6},{6,2},{1... | collective-permute-start | bytes 196616 | tf_op jit(solution)/shard_map/ppermute | solution.py:249
  23.5 5.6 %collective-permute-done.4.rest_6_ = bf16[128,256]{1,0:T(8,128)(2,1)S(1)} collective-permute-done((bf16[128,256]{1,0:T(8,128)(2,1)S(1)}, bf16[128,256]{1,0:T(8,128)(2,1)S(1)}, u32[]{:S(2)}, u32[]{:S(2)}) %collective-permute-start.4) | collective-permute-done | bytes 65568 | tf_op jit(solution)/shard_map/ppermute | solution.py:249
  29.1 0.0 collective-permute-start.7
  29.1 0.0 collective-permute-done.6.rest_9_
  29.1 3.1 %collective-permute-start.5 = (bf16[128,256]{1,0:T(8,128)(2,1)S(1)}, bf16[128,256]{1,0:T(8,128)(2,1)S(1)}, u32[]{:S(2)}, u32[]{:S(2)}) collective-permute-start(bf16[128,256]{1,0:T(8,128)(2,1)S(1)} %collective-permute-done.4.rest_6_), channel_id=1, source_target_pairs={{0,4},{4,0},{8,12},{12,8},{1,5},{5,1},{9,13},{13,9},{2,6},{6,2},{1... | collective-permute-start | bytes 196616 | tf_op jit(solution)/shard_map/ppermute | solution.py:249
  32.2 2.5 %collective-permute-done.7.rest_10_ = bf16[128,256]{1,0:T(8,128)(2,1)S(1)} collective-permute-done((bf16[128,256]{1,0:T(8,128)(2,1)S(1)}, bf16[128,256]{1,0:T(8,128)(2,1)S(1)}, u32[]{:S(2)}, u32[]{:S(2)}) %collective-permute-start.7) | collective-permute-done | bytes 65568 | tf_op jit(solution)/shard_map/ppermute | solution.py:249
  34.7 0.0 collective-permute-start.8
  34.7 0.8 %collective-permute-done.5.rest_7_ = bf16[128,256]{1,0:T(8,128)(2,1)S(1)} collective-permute-done((bf16[128,256]{1,0:T(8,128)(2,1)S(1)}, bf16[128,256]{1,0:T(8,128)(2,1)S(1)}, u32[]{:S(2)}, u32[]{:S(2)}) %collective-permute-start.5) | collective-permute-done | bytes 65568 | tf_op jit(solution)/shard_map/ppermute | solution.py:249
  35.5 3.5 %collective-permute-done.8.rest_11_ = bf16[128,256]{1,0:T(8,128)(2,1)S(1)} collective-permute-done((bf16[128,256]{1,0:T(8,128)(2,1)S(1)}, bf16[128,256]{1,0:T(8,128)(2,1)S(1)}, u32[]{:S(2)}, u32[]{:S(2)}) %collective-permute-start.8) | collective-permute-done | bytes 65568 | tf_op jit(solution)/shard_map/ppermute | solution.py:249
  38.9 0.0 collective-permute-done.rest_1_
  38.9 0.0 collective-permute-done.1.rest_2_
  38.9 0.0 collective-permute-done.2.rest_3_
  39.0 3.4 %attend.1 = (bf16[192,2048]{1,0:T(8,128)(2,1)}, bf16[192,256]{1,0:T(8,128)(2,1)}, bf16[192,256]{1,0:T(8,128)(2,1)}) custom-call(s32[1]{0:T(128)} %bitcast.me_ref, bf16[784,128]{1,0:T(8,128)(2,1)S(1)} %get-tuple-element.7.rest_0_, bf16[784,128]{1,0:T(8,128)(2,1)S(1)} %collective-permute-done.rest_1_, bf16[784,128]{1,0:T(8,128)(2,1)S(1)} %collective-permute-done.1.rest_2_, ...), custom_call_target="tpu_custom_call" | custom-call | tf_op jit(solution)/shard_map/attend/pallas_call | solution.py:274
Async XLA Ops:
  0.6 0.7 %copy-start.3 = (s32[128,1]{0,1:T(1,128)S(1)}, s32[128,1]{0,1:T(1,128)}, u32[]{:S(2)}) copy-start(s32[128,1]{0,1:T(1,128)} %param.8) | copy-start | bytes 1540
  0.6 0.7 %copy-start.4 = (s32[128,1]{0,1:T(1,128)S(1)}, s32[128,1]{0,1:T(1,128)}, u32[]{:S(2)}) copy-start(s32[128,1]{0,1:T(1,128)} %param.9) | copy-start | bytes 1540
  1.3 1.0 %copy-start = (bf16[128,2048]{1,0:T(8,128)(2,1)S(1)}, bf16[128,2048]{1,0:T(8,128)(2,1)}, u32[]{:S(2)}) copy-start(bf16[128,2048]{1,0:T(8,128)(2,1)} %q_hbm.1) | copy-start | bytes 1572868
  2.4 6.2 %copy-start.1 = (bf16[128,256]{1,0:T(8,128)(2,1)S(1)}, bf16[128,256]{1,0:T(8,128)(2,1)}, u32[]{:S(2)}) copy-start(bf16[128,256]{1,0:T(8,128)(2,1)} %rest_4_.1) | copy-start | bytes 196612
  2.4 18.7 %copy-start.2 = (bf16[128,256]{1,0:T(8,128)(2,1)S(1)}, bf16[128,256]{1,0:T(8,128)(2,1)}, u32[]{:S(2)}) copy-start(bf16[128,256]{1,0:T(8,128)(2,1)} %rest_8_.1) | copy-start | bytes 196612
  2.9 36.0 %collective-permute-start = (bf16[784,128]{1,0:T(8,128)(2,1)S(1)}, bf16[784,128]{1,0:T(8,128)(2,1)S(1)}, u32[]{:S(2)}, u32[]{:S(2)}) collective-permute-start(bf16[784,128]{1,0:T(8,128)(2,1)S(1)} %get-tuple-element.8), channel_id=1, source_target_pairs={{0,4},{4,0},{8,12},{12,8},{1,5},{5,1},{9,13},{13,9},{2,6},{6,2},{1... | collective-permute-start | bytes 602120 | tf_op jit(solution)/shard_map/ppermute | solution.py:249
  6.0 32.9 %collective-permute-start.1 = (bf16[784,128]{1,0:T(8,128)(2,1)S(1)}, bf16[784,128]{1,0:T(8,128)(2,1)S(1)}, u32[]{:S(2)}, u32[]{:S(2)}) collective-permute-start(bf16[784,128]{1,0:T(8,128)(2,1)S(1)} %get-tuple-element.9), channel_id=1, source_target_pairs={{0,8},{4,12},{8,0},{12,4},{1,9},{5,13},{9,1},{13,5},{2,10},{6,14},... | collective-permute-start | bytes 602120 | tf_op jit(solution)/shard_map/ppermute | solution.py:249
  8.6 30.4 %collective-permute-start.2 = (bf16[784,128]{1,0:T(8,128)(2,1)S(1)}, bf16[784,128]{1,0:T(8,128)(2,1)S(1)}, u32[]{:S(2)}, u32[]{:S(2)}) collective-permute-start(bf16[784,128]{1,0:T(8,128)(2,1)S(1)} %get-tuple-element.10), channel_id=1, source_target_pairs={{0,12},{4,8},{8,4},{12,0},{1,13},{5,9},{9,5},{13,1},{2,14},{6,10},... | collective-permute-start | bytes 602120 | tf_op jit(solution)/shard_map/ppermute | solution.py:249
  8.6 12.4 %collective-permute-start.3 = (bf16[128,256]{1,0:T(8,128)(2,1)S(1)}, bf16[128,256]{1,0:T(8,128)(2,1)S(1)}, u32[]{:S(2)}, u32[]{:S(2)}) collective-permute-start(bf16[128,256]{1,0:T(8,128)(2,1)S(1)} %copy-done.1), channel_id=1, source_target_pairs={{0,4},{4,0},{8,12},{12,8},{1,5},{5,1},{9,13},{13,9},{2,6},{6,2},{1... | collective-permute-start | bytes 196616 | tf_op jit(solution)/shard_map/ppermute | solution.py:249
  9.5 19.6 %collective-permute-start.4 = (bf16[128,256]{1,0:T(8,128)(2,1)S(1)}, bf16[128,256]{1,0:T(8,128)(2,1)S(1)}, u32[]{:S(2)}, u32[]{:S(2)}) collective-permute-start(bf16[128,256]{1,0:T(8,128)(2,1)S(1)} %copy-done.1), channel_id=1, source_target_pairs={{0,8},{4,12},{8,0},{12,4},{1,9},{5,13},{9,1},{13,5},{2,10},{6,14},... | collective-permute-start | bytes 196616 | tf_op jit(solution)/shard_map/ppermute | solution.py:249
  21.0 8.1 %collective-permute-start.6 = (bf16[128,256]{1,0:T(8,128)(2,1)S(1)}, bf16[128,256]{1,0:T(8,128)(2,1)S(1)}, u32[]{:S(2)}, u32[]{:S(2)}) collective-permute-start(bf16[128,256]{1,0:T(8,128)(2,1)S(1)} %copy-done.2), channel_id=1, source_target_pairs={{0,4},{4,0},{8,12},{12,8},{1,5},{5,1},{9,13},{13,9},{2,6},{6,2},{1... | collective-permute-start | bytes 196616 | tf_op jit(solution)/shard_map/ppermute | solution.py:249
  29.1 5.6 %collective-permute-start.7 = (bf16[128,256]{1,0:T(8,128)(2,1)S(1)}, bf16[128,256]{1,0:T(8,128)(2,1)S(1)}, u32[]{:S(2)}, u32[]{:S(2)}) collective-permute-start(bf16[128,256]{1,0:T(8,128)(2,1)S(1)} %copy-done.2), channel_id=1, source_target_pairs={{0,8},{4,12},{8,0},{12,4},{1,9},{5,13},{9,1},{13,5},{2,10},{6,14},... | collective-permute-start | bytes 196616 | tf_op jit(solution)/shard_map/ppermute | solution.py:249
  29.1 6.3 %collective-permute-start.5 = (bf16[128,256]{1,0:T(8,128)(2,1)S(1)}, bf16[128,256]{1,0:T(8,128)(2,1)S(1)}, u32[]{:S(2)}, u32[]{:S(2)}) collective-permute-start(bf16[128,256]{1,0:T(8,128)(2,1)S(1)} %collective-permute-done.4.rest_6_), channel_id=1, source_target_pairs={{0,4},{4,0},{8,12},{12,8},{1,5},{5,1},{9,13},{13,9},{2,6},{6,2},{1... | collective-permute-start | bytes 196616 | tf_op jit(solution)/shard_map/ppermute | solution.py:249
  34.7 4.3 %collective-permute-start.8 = (bf16[128,256]{1,0:T(8,128)(2,1)S(1)}, bf16[128,256]{1,0:T(8,128)(2,1)S(1)}, u32[]{:S(2)}, u32[]{:S(2)}) collective-permute-start(bf16[128,256]{1,0:T(8,128)(2,1)S(1)} %collective-permute-done.7.rest_10_), channel_id=1, source_target_pairs={{0,4},{4,0},{8,12},{12,8},{1,5},{5,1},{9,13},{13,9},{2,6},{6,2},{1... | collective-permute-start | bytes 196616 | tf_op jit(solution)/shard_map/ppermute | solution.py:249

commit v3 on v2

--- a/solution.py
+++ b/solution.py
@@ -145,12 +145,21 @@
     return (chosen == slot).astype(jnp.bfloat16)
 
 
-def pack_kernel(instances, capacity, me_ref, q_hbm, qo_ref, co_ref, *rest):
-    sends, (q_ref, arrived) = rest[:instances], rest[instances:]
+def pack_kernel(
+    instances, capacity, me_ref, q_hbm, k_hbm, v_hbm, qo_ref, co_ref, kv_out, *rest
+):
+    sends, rest = rest[:instances], rest[instances:]
+    q_ref, k_ref, v_ref, arrived = rest
     rows = q_ref.shape[0]
     heads = q_ref.shape[1] // HD
-    fetch = pltpu.make_async_copy(q_hbm, q_ref, arrived)
-    fetch.start()
+    heads_kv = k_ref.shape[1] // HD
+    fetches = [
+        pltpu.make_async_copy(k_hbm, k_ref, arrived.at[0]),
+        pltpu.make_async_copy(v_hbm, v_ref, arrived.at[1]),
+        pltpu.make_async_copy(q_hbm, q_ref, arrived.at[2]),
+    ]
+    for fetch in fetches:
+        fetch.start()
     me = me_ref[0]
     owners = qo_ref[...]
     lane = lax.broadcasted_iota(jnp.int32, (16, rows), 0)
@@ -161,12 +170,22 @@
     select = jnp.concatenate(
         [picks(wide[k : k + 1], earlier[k : k + 1], capacity) for k in range(instances)], axis=0
     )
-    lists = jnp.concatenate(
-        [owners, co_ref[...], jnp.full((14, rows), -1, jnp.int32)], axis=0
-    ).astype(jnp.float32).astype(jnp.bfloat16)
+    query_list = jnp.broadcast_to(owners, (16, rows)).astype(jnp.float32).astype(jnp.bfloat16)
+    cache_list = jnp.broadcast_to(co_ref[...], (16, rows)).astype(jnp.float32).astype(jnp.bfloat16)
+    top = heads * capacity
     for k in range(instances):
-        sends[k][heads * capacity :, :] = lists
-    fetch.wait()
+        sends[k][top : top + 16, :] = query_list
+    blocks = [(kv_out, 0)] + [(sends[1], top + 16)] * (instances > 1)
+    for ref, at in blocks:
+        ref[at : at + 16, :] = cache_list
+    for index, source in ((0, k_ref), (1, v_ref)):
+        fetches[index].wait()
+        for g in range(heads_kv):
+            piece = source[:, g * HD : (g + 1) * HD]
+            for ref, at in blocks:
+                at = at + 16 + (index * heads_kv + g) * rows
+                ref[at : at + rows, :] = piece
+    fetches[2].wait()
     for pair in range(heads // 2):
         packed = jnp.dot(
             select,
@@ -181,24 +200,31 @@
                 ]
 
 
-def attend_kernel(instances, capacity, heads, heads_kv, me_ref, *rest):
+def attend_kernel(instances, capacity, heads, heads_kv, kv_at, me_ref, *rest):
     got, rest = rest[:instances], rest[instances:]
-    got_k, rest = rest[:instances], rest[instances:]
-    got_v, rest = rest[:instances], rest[instances:]
-    att_ref, kc_ref, vc_ref, wanted_ref, keys, vals = rest
-    rows = got_k[0].shape[0]
+    got_kv, rest = rest[:instances], rest[instances:]
+    att_ref, kc_ref, vc_ref, wanted_ref, lists_ref, keys, vals = rest
+    rows = HD
     per_group = heads // heads_kv
     tail = heads * capacity
     me = me_ref[0]
     for k in range(instances):
         source = jnp.bitwise_xor(me, k)
-        wanted_ref[source] = got[k][...]
+        wanted_ref[source] = got[k][: tail + 16, :]
         at = pl.ds(pl.multiple_of(source * rows, rows), rows)
+        start = kv_at[k]
+        lists_ref[source] = got_kv[k][start : start + 16, :]
+        start = start + 16
         for g in range(heads_kv):
-            keys[g, at, :] = got_k[k][:, g * HD : (g + 1) * HD]
-            vals[g, at, :HD] = got_v[k][:, g * HD : (g + 1) * HD]
+            keys[g, at, :] = got_kv[k][start + g * rows : start + (g + 1) * rows, :]
+            there = start + (heads_kv + g) * rows
+            vals[g, at, :HD] = got_kv[k][there : there + rows, :]
         vals[:, k * rows : (k + 1) * rows, HD:] = jnp.ones((heads_kv, rows, HD), jnp.bfloat16)
-    lists = jnp.concatenate([wanted_ref[s, tail : tail + 16, :] for s in range(instances)], axis=0)
+    lists = jnp.concatenate(
+        [wanted_ref[s, tail : tail + 16, :] for s in range(instances)]
+        + [lists_ref[s] for s in range(instances)],
+        axis=0,
+    )
     wide = (lists.astype(jnp.float32) == me.astype(jnp.float32)).astype(jnp.float32)
     earlier = jnp.dot(wide.astype(jnp.bfloat16), before(rows), preferred_element_type=jnp.float32)
     r = lax.broadcasted_iota(jnp.int32, (rows, 2 * rows), 0)
@@ -206,7 +232,7 @@
     reach = ((u <= r) | (u >= rows)).astype(jnp.bfloat16)
     scale = 1.0 / math.sqrt(HD)
     for s in range(instances):
-        q_at, c_at = 16 * s, 16 * s + 1
+        q_at, c_at = 16 * s, 16 * (instances + s)
         cache_pick = picks(wide[c_at : c_at + 1], earlier[c_at : c_at + 1], capacity)
         query_pick = picks(wide[q_at : q_at + 1], earlier[q_at : q_at + 1], capacity)
         slots = slice(s * capacity, (s + 1) * capacity)
@@ -248,51 +274,51 @@
     def swap(array, k):
         return lax.ppermute(array, "seq", [(i, i ^ k) for i in range(instances)])
 
-    all_k, all_v = {0: keys}, {0: values}
-    bit = instances // 2
-    while bit:
-        for k in list(all_k):
-            all_k[k ^ bit] = swap(all_k[k], bit)
-            all_v[k ^ bit] = swap(all_v[k], bit)
-        bit //= 2
-    height = heads * capacity + 16
+    tall = heads * capacity + 16
+    kv_tall = 2 * heads_kv * rows + 16
     vmem = pl.BlockSpec(memory_space=pltpu.VMEM)
     smem = pl.BlockSpec(memory_space=pltpu.SMEM)
+    hbm = pl.BlockSpec(memory_space=pltpu.HBM)
     me = lax.axis_index("seq").astype(jnp.int32).reshape(1)
-    sends = pl.pallas_call(
+    heights = [kv_tall] + [tall + kv_tall * (k == 1) for k in range(instances)]
+    own_kv, *sends = pl.pallas_call(
         functools.partial(pack_kernel, instances, capacity),
-        out_shape=(jax.ShapeDtypeStruct((height, HD), jnp.bfloat16),) * instances,
-        in_specs=[smem, pl.BlockSpec(memory_space=pl.ANY), vmem, vmem],
-        out_specs=(vmem,) * instances,
-        scratch_shapes=[pltpu.VMEM(queries.shape, jnp.bfloat16), pltpu.SemaphoreType.DMA],
+        out_shape=tuple(jax.ShapeDtypeStruct((h, HD), jnp.bfloat16) for h in heights),
+        in_specs=[smem, hbm, hbm, hbm, vmem, vmem],
+        out_specs=(vmem,) * (instances + 1),
+        scratch_shapes=[
+            pltpu.VMEM(queries.shape, jnp.bfloat16),
+            pltpu.VMEM(keys.shape, jnp.bfloat16),
+            pltpu.VMEM(values.shape, jnp.bfloat16),
+            pltpu.SemaphoreType.DMA((3,)),
+        ],
         compiler_params=pltpu.CompilerParams(vmem_limit_bytes=16 << 20),
         cost_estimate=pl.CostEstimate(flops=1 << 27, bytes_accessed=2 << 20, transcendentals=0),
         name="pack",
-    )(me, queries, query_owner.reshape(1, rows), cache_owner.reshape(1, rows))
-    got = [swap(sends[k], k) if k else sends[0] for k in range(instances)]
+    )(me, queries, keys, values, query_owner.reshape(1, rows), cache_owner.reshape(1, rows))
+    far_kv = swap(own_kv, 2)
+    far_kv_beside = swap(far_kv, 1)
+    got = [sends[0], swap(sends[1], 1), swap(sends[2], 2), swap(sends[3], 3)]
+    got_kv, kv_at = (own_kv, got[1], far_kv, far_kv_beside), (0, tall, 0, 0)
     slots = instances * capacity
     return pl.pallas_call(
-        functools.partial(attend_kernel, instances, capacity, heads, heads_kv),
+        functools.partial(attend_kernel, instances, capacity, heads, heads_kv, kv_at),
         out_shape=(
             jax.ShapeDtypeStruct((slots, heads * HD), jnp.bfloat16),
             jax.ShapeDtypeStruct((slots, heads_kv * HD), jnp.bfloat16),
             jax.ShapeDtypeStruct((slots, heads_kv * HD), jnp.bfloat16),
         ),
-        in_specs=[smem] + [vmem] * (3 * instances),
+        in_specs=[smem] + [vmem] * (2 * instances),
         out_specs=(vmem, vmem, vmem),
         scratch_shapes=[
-            pltpu.VMEM((instances, height, HD), jnp.bfloat16),
+            pltpu.VMEM((instances, tall, HD), jnp.bfloat16),
+            pltpu.VMEM((instances, 16, HD), jnp.bfloat16),
             pltpu.VMEM((heads_kv, instances * rows, HD), jnp.bfloat16),
             pltpu.VMEM((heads_kv, instances * rows, 2 * HD), jnp.bfloat16),
         ],
         compiler_params=pltpu.CompilerParams(vmem_limit_bytes=24 << 20),
         name="attend",
-    )(
-        me,
-        *got,
-        *[all_k[k] for k in range(instances)],
-        *[all_v[k] for k in range(instances)],
-    )
+    )(me, *got, *got_kv)
 
 
 def on_device(queries, keys, values, query_owner, cache_owner):
@@ -300,7 +326,7 @@
     rows = queries.shape[0]
     capacity = 3 * rows // (2 * instances)
     heads = queries.shape[1] // HD
-    whole_tiles = capacity % 16 == 0 and rows == HD and heads % 2 == 0 and instances & (instances - 1) == 0
+    whole_tiles = instances == 4 and capacity % 16 == 0 and rows == HD and heads % 2 == 0
     form = few_instances if whole_tiles else many_instances
     return form(queries, keys, values, query_owner, cache_owner)
 

time: 42.5 us -> 35.2 us (0.83)
  the two profiles are of different devices: /device:TPU:0 before, /device:TPU:16 now
where the time goes in v3:
time: 35.2 us; the launch traced here: 34.9 us
  waiting for transfers between devices  22.2 us (63%)
  starting transfers between devices  4.57 us (13%)
  Pallas kernels  4.1 us (12%)
  local copies, waits for them, and re-layouts  3.37 us (10%)
  between operations  0.67 us (2%)
    ppermute x5, waiting for transfers between devices, swap(): return lax.ppermute(array, 'seq', [(i, i ^ k) for i in range(instances)])  22.2 us
    ppermute x5, starting transfers between devices, swap(): return lax.ppermute(array, 'seq', [(i, i ^ k) for i in range(instances)])  4.57 us
    unnamed x10, local copies, waits for them, and re-layouts  3.37 us
    pallas_call x1, Pallas kernels, few_instances(): pl.pallas_call(functools.partial(attend_kernel, instances, capacity, head...  3.37 us
    pallas_call x1, Pallas kernels, few_instances(): pl.pallas_call(functools.partial(pack_kernel, instances, capacity), out_s...  0.73 us
  transfers between devices with their start and end apart: 5, of which 3 were waited for; matrix products, arithmetic and copies ran while one was open for 0% of the time, Pallas kernels for 0%

profile of v3, /device:TPU:16, one launch (start us, length us, event | category | flops | bytes accessed | tf_op | source)
XLA Modules:
  0.0 34.9 jit_solution(12836676598914766436)
XLA Ops:
  0.6 0.0 copy-start.3
  0.6 0.0 copy-start.4
  0.7 0.6 %copy-done.3 = s32[128,1]{0,1:T(1,128)S(1)} copy-done((s32[128,1]{0,1:T(1,128)S(1)}, s32[128,1]{0,1:T(1,128)}, u32[]{:S(2)}) %copy-start.3) | copy-done | bytes 536
  1.3 0.0 copy-done.4
  1.3 0.0 copy-start
  1.3 1.0 %copy-done = bf16[128,2048]{1,0:T(8,128)(2,1)S(1)} copy-done((bf16[128,2048]{1,0:T(8,128)(2,1)S(1)}, bf16[128,2048]{1,0:T(8,128)(2,1)}, u32[]{:S(2)}) %copy-start) | copy-done | bytes 524312
  2.4 0.0 copy-start.1
  2.4 0.8 %copy-done.1 = bf16[128,256]{1,0:T(8,128)(2,1)S(1)} copy-done((bf16[128,256]{1,0:T(8,128)(2,1)S(1)}, bf16[128,256]{1,0:T(8,128)(2,1)}, u32[]{:S(2)}) %copy-start.1) | copy-done | bytes 65560
  3.2 0.0 copy-start.2
  3.2 0.8 %copy-done.2 = bf16[128,256]{1,0:T(8,128)(2,1)S(1)} copy-done((bf16[128,256]{1,0:T(8,128)(2,1)S(1)}, bf16[128,256]{1,0:T(8,128)(2,1)}, u32[]{:S(2)}) %copy-start.2) | copy-done | bytes 65560
  4.0 0.7 %pack.1 = (bf16[528,128]{1,0:T(8,128)(2,1)S(1)}, bf16[784,128]{1,0:T(8,128)(2,1)S(1)}, bf16[1312,128]{1,0:T(8,128)(2,1)S(1)}, bf16[784,128]{1,0:T(8,128)(2,1)S(1)}, bf16[784,128]{1,0:T(8,128)(2,1)S(1)}) custom-call(s32[1]{0:T(128)} %bitcast.me_ref, bf16[128,2048]{1,0:T(8,128)(2,1)S(1)} %copy-done, bf16[128,256]{1,0:T(8,128)(2,1)S(1)} %copy-done.1, ...), custom_call_target="tpu_custom_call" | custom-call | flops 134217728 | bytes 2097152 | tf_op jit(solution)/shard_map/pack/pallas_call | solution.py:284
  4.8 1.6 %collective-permute-start = (bf16[1312,128]{1,0:T(8,128)(2,1)S(1)}, bf16[1312,128]{1,0:T(8,128)(2,1)S(1)}, u32[]{:S(2)}, u32[]{:S(2)}) collective-permute-start(bf16[1312,128]{1,0:T(8,128)(2,1)S(1)} %get-tuple-element.9), channel_id=1, source_target_pairs={{0,4},{4,0},{8,12},{12,8},{1,5},{5,1},{9,13},{13,9},{2,6},{6,2},{1... | collective-permute-start | bytes 1007624 | tf_op jit(solution)/shard_map/ppermute | solution.py:275
  6.4 0.3 collective-permute-start.3
  6.7 2.6 %collective-permute-start.1 = (bf16[784,128]{1,0:T(8,128)(2,1)S(1)}, bf16[784,128]{1,0:T(8,128)(2,1)S(1)}, u32[]{:S(2)}, u32[]{:S(2)}) collective-permute-start(bf16[784,128]{1,0:T(8,128)(2,1)S(1)} %get-tuple-element.10), channel_id=1, source_target_pairs={{0,8},{4,12},{8,0},{12,4},{1,9},{5,13},{9,1},{13,5},{2,10},{6,14},... | collective-permute-start | bytes 602120 | tf_op jit(solution)/shard_map/ppermute | solution.py:275
  9.3 0.0 collective-permute-start.2
  9.3 9.2 %collective-permute-done.3.rest_6_ = bf16[528,128]{1,0:T(8,128)(2,1)S(1)} collective-permute-done((bf16[528,128]{1,0:T(8,128)(2,1)S(1)}, bf16[528,128]{1,0:T(8,128)(2,1)S(1)}, u32[]{:S(2)}, u32[]{:S(2)}) %collective-permute-start.3) | collective-permute-done | bytes 135200 | tf_op jit(solution)/shard_map/ppermute | solution.py:275
  18.5 0.0 collective-permute-start.4
  18.5 7.5 %collective-permute-done.1.rest_2_ = bf16[784,128]{1,0:T(8,128)(2,1)S(1)} collective-permute-done((bf16[784,128]{1,0:T(8,128)(2,1)S(1)}, bf16[784,128]{1,0:T(8,128)(2,1)S(1)}, u32[]{:S(2)}, u32[]{:S(2)}) %collective-permute-start.1) | collective-permute-done | bytes 200736 | tf_op jit(solution)/shard_map/ppermute | solution.py:275
  26.0 5.6 %collective-permute-done.2.rest_3_ = bf16[784,128]{1,0:T(8,128)(2,1)S(1)} collective-permute-done((bf16[784,128]{1,0:T(8,128)(2,1)S(1)}, bf16[784,128]{1,0:T(8,128)(2,1)S(1)}, u32[]{:S(2)}, u32[]{:S(2)}) %collective-permute-start.2) | collective-permute-done | bytes 200736 | tf_op jit(solution)/shard_map/ppermute | solution.py:275
  31.5 0.0 collective-permute-done.4.rest_7_
  31.5 0.0 collective-permute-done.rest_1_.rest_5_
  31.5 3.4 %attend.1 = (bf16[192,2048]{1,0:T(8,128)(2,1)}, bf16[192,256]{1,0:T(8,128)(2,1)}, bf16[192,256]{1,0:T(8,128)(2,1)}) custom-call(s32[1]{0:T(128)} %bitcast.me_ref, bf16[784,128]{1,0:T(8,128)(2,1)S(1)} %get-tuple-element.8.rest_0_, bf16[1312,128]{1,0:T(8,128)(2,1)S(1)} %collective-permute-done.rest_1_.rest_5_, ...), custom_call_target="tpu_custom_call" | custom-call | tf_op jit(solution)/shard_map/attend/pallas_call | solution.py:304
Async XLA Ops:
  0.6 0.7 %copy-start.3 = (s32[128,1]{0,1:T(1,128)S(1)}, s32[128,1]{0,1:T(1,128)}, u32[]{:S(2)}) copy-start(s32[128,1]{0,1:T(1,128)} %param.8) | copy-start | bytes 1540
  0.6 0.7 %copy-start.4 = (s32[128,1]{0,1:T(1,128)S(1)}, s32[128,1]{0,1:T(1,128)}, u32[]{:S(2)}) copy-start(s32[128,1]{0,1:T(1,128)} %param.9) | copy-start | bytes 1540
  1.3 1.0 %copy-start = (bf16[128,2048]{1,0:T(8,128)(2,1)S(1)}, bf16[128,2048]{1,0:T(8,128)(2,1)}, u32[]{:S(2)}) copy-start(bf16[128,2048]{1,0:T(8,128)(2,1)} %q_hbm.1) | copy-start | bytes 1572868
  2.4 0.8 %copy-start.1 = (bf16[128,256]{1,0:T(8,128)(2,1)S(1)}, bf16[128,256]{1,0:T(8,128)(2,1)}, u32[]{:S(2)}) copy-start(bf16[128,256]{1,0:T(8,128)(2,1)} %k_hbm.1) | copy-start | bytes 196612
  3.2 0.8 %copy-start.2 = (bf16[128,256]{1,0:T(8,128)(2,1)S(1)}, bf16[128,256]{1,0:T(8,128)(2,1)}, u32[]{:S(2)}) copy-start(bf16[128,256]{1,0:T(8,128)(2,1)} %v_hbm.1) | copy-start | bytes 196612
  4.8 26.8 %collective-permute-start = (bf16[1312,128]{1,0:T(8,128)(2,1)S(1)}, bf16[1312,128]{1,0:T(8,128)(2,1)S(1)}, u32[]{:S(2)}, u32[]{:S(2)}) collective-permute-start(bf16[1312,128]{1,0:T(8,128)(2,1)S(1)} %get-tuple-element.9), channel_id=1, source_target_pairs={{0,4},{4,0},{8,12},{12,8},{1,5},{5,1},{9,13},{13,9},{2,6},{6,2},{1... | collective-permute-start | bytes 1007624 | tf_op jit(solution)/shard_map/ppermute | solution.py:275
  6.4 12.1 %collective-permute-start.3 = (bf16[528,128]{1,0:T(8,128)(2,1)S(1)}, bf16[528,128]{1,0:T(8,128)(2,1)S(1)}, u32[]{:S(2)}, u32[]{:S(2)}) collective-permute-start(bf16[528,128]{1,0:T(8,128)(2,1)S(1)} %get-tuple-element.12.rest_4_), channel_id=1, source_target_pairs={{0,8},{4,12},{8,0},{12,4},{1,9},{5,13},{9,1},{13,5},{2,10},{6,14},... | collective-permute-start | bytes 405512 | tf_op jit(solution)/shard_map/ppermute | solution.py:275
  6.7 19.2 %collective-permute-start.1 = (bf16[784,128]{1,0:T(8,128)(2,1)S(1)}, bf16[784,128]{1,0:T(8,128)(2,1)S(1)}, u32[]{:S(2)}, u32[]{:S(2)}) collective-permute-start(bf16[784,128]{1,0:T(8,128)(2,1)S(1)} %get-tuple-element.10), channel_id=1, source_target_pairs={{0,8},{4,12},{8,0},{12,4},{1,9},{5,13},{9,1},{13,5},{2,10},{6,14},... | collective-permute-start | bytes 602120 | tf_op jit(solution)/shard_map/ppermute | solution.py:275
  9.3 22.2 %collective-permute-start.2 = (bf16[784,128]{1,0:T(8,128)(2,1)S(1)}, bf16[784,128]{1,0:T(8,128)(2,1)S(1)}, u32[]{:S(2)}, u32[]{:S(2)}) collective-permute-start(bf16[784,128]{1,0:T(8,128)(2,1)S(1)} %get-tuple-element.11), channel_id=1, source_target_pairs={{0,12},{4,8},{8,4},{12,0},{1,13},{5,9},{9,5},{13,1},{2,14},{6,10},... | collective-permute-start | bytes 602120 | tf_op jit(solution)/shard_map/ppermute | solution.py:275
  18.5 13.0 %collective-permute-start.4 = (bf16[528,128]{1,0:T(8,128)(2,1)S(1)}, bf16[528,128]{1,0:T(8,128)(2,1)S(1)}, u32[]{:S(2)}, u32[]{:S(2)}) collective-permute-start(bf16[528,128]{1,0:T(8,128)(2,1)S(1)} %collective-permute-done.3.rest_6_), channel_id=1, source_target_pairs={{0,4},{4,0},{8,12},{12,8},{1,5},{5,1},{9,13},{13,9},{2,6},{6,2},{1... | collective-permute-start | bytes 405512 | tf_op jit(solution)/shard_map/ppermute | solution.py:275

commit v4 on v2

--- a/solution.py
+++ b/solution.py
@@ -181,22 +181,36 @@
                 ]
 
 
+def gate_kernel(k_ref, v_ref, *rest):
+    kv_ref = rest[-1]
+    rows = k_ref.shape[0]
+    at = 0
+    for source in (k_ref, v_ref):
+        for g in range(source.shape[1] // HD):
+            kv_ref[at : at + rows, :] = source[:, g * HD : (g + 1) * HD]
+            at += rows
+
+
 def attend_kernel(instances, capacity, heads, heads_kv, me_ref, *rest):
     got, rest = rest[:instances], rest[instances:]
-    got_k, rest = rest[:instances], rest[instances:]
-    got_v, rest = rest[:instances], rest[instances:]
-    att_ref, kc_ref, vc_ref, wanted_ref, keys, vals = rest
-    rows = got_k[0].shape[0]
+    k_own, v_own, k_near, v_near, k_far, v_far, both = rest[:7]
+    att_ref, kc_ref, vc_ref, wanted_ref, keys, vals = rest[7:]
+    rows = HD
     per_group = heads // heads_kv
     tail = heads * capacity
     me = me_ref[0]
+    direct = ((k_own, v_own), (k_near, v_near), (k_far, v_far))
     for k in range(instances):
         source = jnp.bitwise_xor(me, k)
         wanted_ref[source] = got[k][...]
         at = pl.ds(pl.multiple_of(source * rows, rows), rows)
         for g in range(heads_kv):
-            keys[g, at, :] = got_k[k][:, g * HD : (g + 1) * HD]
-            vals[g, at, :HD] = got_v[k][:, g * HD : (g + 1) * HD]
+            if k < len(direct):
+                keys[g, at, :] = direct[k][0][:, g * HD : (g + 1) * HD]
+                vals[g, at, :HD] = direct[k][1][:, g * HD : (g + 1) * HD]
+            else:
+                keys[g, at, :] = both[g * rows : (g + 1) * rows, :]
+                vals[g, at, :HD] = both[(heads_kv + g) * rows : (heads_kv + g + 1) * rows, :]
         vals[:, k * rows : (k + 1) * rows, HD:] = jnp.ones((heads_kv, rows, HD), jnp.bfloat16)
     lists = jnp.concatenate([wanted_ref[s, tail : tail + 16, :] for s in range(instances)], axis=0)
     wide = (lists.astype(jnp.float32) == me.astype(jnp.float32)).astype(jnp.float32)
@@ -248,28 +262,43 @@
     def swap(array, k):
         return lax.ppermute(array, "seq", [(i, i ^ k) for i in range(instances)])
 
-    all_k, all_v = {0: keys}, {0: values}
-    bit = instances // 2
-    while bit:
-        for k in list(all_k):
-            all_k[k ^ bit] = swap(all_k[k], bit)
-            all_v[k ^ bit] = swap(all_v[k], bit)
-        bit //= 2
-    height = heads * capacity + 16
+    tall = heads * capacity + 16
     vmem = pl.BlockSpec(memory_space=pltpu.VMEM)
     smem = pl.BlockSpec(memory_space=pltpu.SMEM)
+    hbm = pl.BlockSpec(memory_space=pltpu.HBM)
     me = lax.axis_index("seq").astype(jnp.int32).reshape(1)
+    k_far, v_far = swap(keys, 2), swap(values, 2)
+    k_near, v_near = swap(keys, 1), swap(values, 1)
+    kv_tall = 2 * heads_kv * rows
     sends = pl.pallas_call(
         functools.partial(pack_kernel, instances, capacity),
-        out_shape=(jax.ShapeDtypeStruct((height, HD), jnp.bfloat16),) * instances,
-        in_specs=[smem, pl.BlockSpec(memory_space=pl.ANY), vmem, vmem],
+        out_shape=(jax.ShapeDtypeStruct((tall, HD), jnp.bfloat16),) * instances,
+        in_specs=[smem, hbm, vmem, vmem],
         out_specs=(vmem,) * instances,
         scratch_shapes=[pltpu.VMEM(queries.shape, jnp.bfloat16), pltpu.SemaphoreType.DMA],
         compiler_params=pltpu.CompilerParams(vmem_limit_bytes=16 << 20),
         cost_estimate=pl.CostEstimate(flops=1 << 27, bytes_accessed=2 << 20, transcendentals=0),
         name="pack",
     )(me, queries, query_owner.reshape(1, rows), cache_owner.reshape(1, rows))
-    got = [swap(sends[k], k) if k else sends[0] for k in range(instances)]
+    anyspace = pl.BlockSpec(memory_space=pl.ANY)
+    through = [*sends[1:], k_near, v_near]
+    *through, kv_far = pl.pallas_call(
+        gate_kernel,
+        out_shape=tuple(jax.ShapeDtypeStruct(x.shape, x.dtype) for x in through)
+        + (jax.ShapeDtypeStruct((kv_tall, HD), jnp.bfloat16),),
+        in_specs=[vmem, vmem] + [anyspace] * len(through),
+        out_specs=(anyspace,) * len(through) + (vmem,),
+        input_output_aliases={2 + i: i for i in range(len(through))},
+        compiler_params=pltpu.CompilerParams(vmem_limit_bytes=16 << 20),
+        cost_estimate=pl.CostEstimate(flops=0, bytes_accessed=1 << 18, transcendentals=0),
+        name="gate",
+    )(k_far, v_far, *through)
+    k_near, v_near = through[-2:]
+    sends = [sends[0], *through[:-2]]
+    got = {0: sends[0]}
+    for k in (2, 3, 1):
+        got[k] = swap(sends[k], k)
+    both = swap(kv_far, 1)
     slots = instances * capacity
     return pl.pallas_call(
         functools.partial(attend_kernel, instances, capacity, heads, heads_kv),
@@ -278,21 +307,16 @@
             jax.ShapeDtypeStruct((slots, heads_kv * HD), jnp.bfloat16),
             jax.ShapeDtypeStruct((slots, heads_kv * HD), jnp.bfloat16),
         ),
-        in_specs=[smem] + [vmem] * (3 * instances),
+        in_specs=[smem] + [vmem] * (instances + 7),
         out_specs=(vmem, vmem, vmem),
         scratch_shapes=[
-            pltpu.VMEM((instances, height, HD), jnp.bfloat16),
+            pltpu.VMEM((instances, tall, HD), jnp.bfloat16),
             pltpu.VMEM((heads_kv, instances * rows, HD), jnp.bfloat16),
             pltpu.VMEM((heads_kv, instances * rows, 2 * HD), jnp.bfloat16),
         ],
         compiler_params=pltpu.CompilerParams(vmem_limit_bytes=24 << 20),
         name="attend",
-    )(
-        me,
-        *got,
-        *[all_k[k] for k in range(instances)],
-        *[all_v[k] for k in range(instances)],
-    )
+    )(me, *[got[k] for k in range(instances)], keys, values, k_near, v_near, k_far, v_far, both)
 
 
 def on_device(queries, keys, values, query_owner, cache_owner):
@@ -300,7 +324,7 @@
     rows = queries.shape[0]
     capacity = 3 * rows // (2 * instances)
     heads = queries.shape[1] // HD
-    whole_tiles = capacity % 16 == 0 and rows == HD and heads % 2 == 0 and instances & (instances - 1) == 0
+    whole_tiles = instances == 4 and capacity % 16 == 0 and rows == HD and heads % 2 == 0
     form = few_instances if whole_tiles else many_instances
     return form(queries, keys, values, query_owner, cache_owner)
 

time: 42.5 us -> 34.2 us (0.80)
  starting transfers between devices: 15.6 us -> 10.9 us
  waiting for transfers between devices: 20.4 us -> 16.8 us
    ppermute x9 -> x8, starting transfers between devices: 15.6 us -> 10.9 us  [swap(): return lax.ppermute(array, 'seq', [(i, i ^ k) for i in range(instances)])]
    ppermute x9 -> x8, waiting for transfers between devices: 20.4 us -> 16.8 us  [swap(): return lax.ppermute(array, 'seq', [(i, i ^ k) for i in range(instances)])]
  transfers between devices with their start and end apart: 9 -> 8, of which waited for: 5 -> 4; matrix products, arithmetic and copies ran while one was open for 0% -> 0% of each run, Pallas kernels for 0% -> 2%
where the time goes in v4:
time: 34.2 us; the launch traced here: 34 us
  waiting for transfers between devices  16.8 us (49%)
  starting transfers between devices  10.9 us (32%)
  Pallas kernels  3.93 us (11%)
  local copies, waits for them, and re-layouts  1.72 us (5%)
  between operations  0.67 us (2%)
    ppermute x8, waiting for transfers between devices, swap(): return lax.ppermute(array, 'seq', [(i, i ^ k) for i in range(instances)])  16.8 us
    ppermute x8, starting transfers between devices, swap(): return lax.ppermute(array, 'seq', [(i, i ^ k) for i in range(instances)])  10.9 us
    pallas_call x1, Pallas kernels, few_instances(): pl.pallas_call(functools.partial(attend_kernel, instances, capacity, head...  3.36 us
    unnamed x10, local copies, waits for them, and re-layouts  1.72 us
  transfers between devices with their start and end apart: 8, of which 4 were waited for; matrix products, arithmetic and copies ran while one was open for 0% of the time, Pallas kernels for 2%

profile of v4, /device:TPU:0, one launch (start us, length us, event | category | flops | bytes accessed | tf_op | source)
XLA Modules:
  0.0 34.0 jit_solution(10481986448329128406)
XLA Ops:
  0.6 4.1 %collective-permute-start = (bf16[128,256]{1,0:T(8,128)(2,1)}, bf16[128,256]{1,0:T(8,128)(2,1)S(1)}, u32[]{:S(2)}, u32[]{:S(2)}) collective-permute-start(bf16[128,256]{1,0:T(8,128)(2,1)} %rest_4_.1), channel_id=1, source_target_pairs={{0,8},{4,12},{8,0},{12,4},{1,9},{5,13},{9,1},{13,5},{2,10},{6,14},... | collective-permute-start | bytes 196616 | tf_op jit(solution)/shard_map/ppermute | solution.py:263
  4.7 1.6 %collective-permute-start.2 = (bf16[128,256]{1,0:T(8,128)(2,1)}, bf16[128,256]{1,0:T(8,128)(2,1)S(1)}, u32[]{:S(2)}, u32[]{:S(2)}) collective-permute-start(bf16[128,256]{1,0:T(8,128)(2,1)} %rest_4_.1), channel_id=1, source_target_pairs={{0,4},{4,0},{8,12},{12,8},{1,5},{5,1},{9,13},{13,9},{2,6},{6,2},{1... | collective-permute-start | bytes 196616 | tf_op jit(solution)/shard_map/ppermute | solution.py:263
  6.3 0.3 collective-permute-start.1
  6.6 0.2 collective-permute-start.3
  6.8 0.0 copy-start.3
  6.8 0.0 copy-start.4
  6.8 0.7 %copy-done.3 = s32[128,1]{0,1:T(1,128)S(1)} copy-done((s32[128,1]{0,1:T(1,128)S(1)}, s32[128,1]{0,1:T(1,128)}, u32[]{:S(2)}) %copy-start.3) | copy-done | bytes 536
  7.5 0.0 copy-done.4
  7.5 0.0 copy-start
  7.5 1.0 %copy-done = bf16[128,2048]{1,0:T(8,128)(2,1)S(1)} copy-done((bf16[128,2048]{1,0:T(8,128)(2,1)S(1)}, bf16[128,2048]{1,0:T(8,128)(2,1)}, u32[]{:S(2)}) %copy-start) | copy-done | bytes 524312
  8.6 0.5 %pack.1 = (bf16[784,128]{1,0:T(8,128)(2,1)S(1)}, bf16[784,128]{1,0:T(8,128)(2,1)S(1)}, bf16[784,128]{1,0:T(8,128)(2,1)S(1)}, bf16[784,128]{1,0:T(8,128)(2,1)S(1)}) custom-call(s32[1]{0:T(128)} %bitcast.me_ref, bf16[128,2048]{1,0:T(8,128)(2,1)S(1)} %copy-done, s32[1,128]{1,0:T(1,128)S(1)} %bitcast.3, s32[1,128]{1,0:T(1,128)S(1)} %bitcast.4), custom_call_target="tpu_custom_call" | custom-call | flops 134217728 | bytes 2097152 | tf_op jit(solution)/shard_map/pack/pallas_call | solution.py:273
  9.1 0.0 collective-permute-done.k_ref.rest_8_
  9.1 1.0 %collective-permute-done.2.rest_3_ = bf16[128,256]{1,0:T(8,128)(2,1)S(1)} collective-permute-done((bf16[128,256]{1,0:T(8,128)(2,1)}, bf16[128,256]{1,0:T(8,128)(2,1)S(1)}, u32[]{:S(2)}, u32[]{:S(2)}) %collective-permute-start.2) | collective-permute-done | bytes 65568 | tf_op jit(solution)/shard_map/ppermute | solution.py:263
  10.1 2.2 %collective-permute-done.1.v_ref.rest_9_ = bf16[128,256]{1,0:T(8,128)(2,1)S(1)} collective-permute-done((bf16[128,256]{1,0:T(8,128)(2,1)}, bf16[128,256]{1,0:T(8,128)(2,1)S(1)}, u32[]{:S(2)}, u32[]{:S(2)}) %collective-permute-start.1) | collective-permute-done | bytes 65568 | tf_op jit(solution)/shard_map/ppermute | solution.py:263
  12.3 0.0 collective-permute-done.3.rest_4_
  12.3 0.0 copy-start.1
  12.3 0.0 copy-start.2
  12.3 1.2 %collective-permute-start.4 = (bf16[784,128]{1,0:T(8,128)(2,1)S(1)}, bf16[784,128]{1,0:T(8,128)(2,1)S(1)}, u32[]{:S(2)}, u32[]{:S(2)}) collective-permute-start(bf16[784,128]{1,0:T(8,128)(2,1)S(1)} %get-tuple-element.17), channel_id=1, source_target_pairs={{0,4},{4,0},{8,12},{12,8},{1,5},{5,1},{9,13},{13,9},{2,6},{6,2},{1... | collective-permute-start | bytes 602120 | tf_op jit(solution)/shard_map/ppermute | solution.py:263
  13.5 1.9 %collective-permute-start.5 = (bf16[784,128]{1,0:T(8,128)(2,1)S(1)}, bf16[784,128]{1,0:T(8,128)(2,1)S(1)}, u32[]{:S(2)}, u32[]{:S(2)}) collective-permute-start(bf16[784,128]{1,0:T(8,128)(2,1)S(1)} %get-tuple-element.18), channel_id=1, source_target_pairs={{0,8},{4,12},{8,0},{12,4},{1,9},{5,13},{9,1},{13,5},{2,10},{6,14},... | collective-permute-start | bytes 602120 | tf_op jit(solution)/shard_map/ppermute | solution.py:263
  15.5 1.3 %collective-permute-start.6 = (bf16[784,128]{1,0:T(8,128)(2,1)S(1)}, bf16[784,128]{1,0:T(8,128)(2,1)S(1)}, u32[]{:S(2)}, u32[]{:S(2)}) collective-permute-start(bf16[784,128]{1,0:T(8,128)(2,1)S(1)} %get-tuple-element.19), channel_id=1, source_target_pairs={{0,12},{4,8},{8,4},{12,0},{1,13},{5,9},{9,5},{13,1},{2,14},{6,10},... | collective-permute-start | bytes 602120 | tf_op jit(solution)/shard_map/ppermute | solution.py:263
  16.8 0.2 collective-permute-start.7
  17.0 11.5 %collective-permute-done.7.rest_10_ = bf16[512,128]{1,0:T(8,128)(2,1)S(1)} collective-permute-done((bf16[512,128]{1,0:T(8,128)(2,1)S(1)}, bf16[512,128]{1,0:T(8,128)(2,1)S(1)}, u32[]{:S(2)}, u32[]{:S(2)}) %collective-permute-start.7) | collective-permute-done | bytes 131104 | tf_op jit(solution)/shard_map/ppermute | solution.py:263
  28.5 0.0 collective-permute-done.4.rest_1_
  28.5 2.1 %collective-permute-done.5.rest_2_ = bf16[784,128]{1,0:T(8,128)(2,1)S(1)} collective-permute-done((bf16[784,128]{1,0:T(8,128)(2,1)S(1)}, bf16[784,128]{1,0:T(8,128)(2,1)S(1)}, u32[]{:S(2)}, u32[]{:S(2)}) %collective-permute-start.5) | collective-permute-done | bytes 200736 | tf_op jit(solution)/shard_map/ppermute | solution.py:263
  30.7 0.0 collective-permute-done.6.rest_3_
  30.7 0.0 copy-done.1
  30.7 0.0 copy-done.2
  30.7 3.4 %attend.1 = (bf16[192,2048]{1,0:T(8,128)(2,1)}, bf16[192,256]{1,0:T(8,128)(2,1)}, bf16[192,256]{1,0:T(8,128)(2,1)}) custom-call(s32[1]{0:T(128)} %bitcast.me_ref, bf16[784,128]{1,0:T(8,128)(2,1)S(1)} %get-tuple-element.13.rest_0_, bf16[784,128]{1,0:T(8,128)(2,1)S(1)} %collective-permute-done.4.rest_1_, bf16[784,128]{1,0:T(8,128)(2,1)S(1)} %collective-permute-done.5.rest_2_, ...), custom_call_target="tpu_custom_call" | custom-call | tf_op jit(solution)/shard_map/attend/pallas_call | solution.py:303
  (1 shorter events, 0.0 us)
Async XLA Ops:
  0.6 8.5 %collective-permute-start = (bf16[128,256]{1,0:T(8,128)(2,1)}, bf16[128,256]{1,0:T(8,128)(2,1)S(1)}, u32[]{:S(2)}, u32[]{:S(2)}) collective-permute-start(bf16[128,256]{1,0:T(8,128)(2,1)} %rest_4_.1), channel_id=1, source_target_pairs={{0,8},{4,12},{8,0},{12,4},{1,9},{5,13},{9,1},{13,5},{2,10},{6,14},... | collective-permute-start | bytes 196616 | tf_op jit(solution)/shard_map/ppermute | solution.py:263
  4.7 5.4 %collective-permute-start.2 = (bf16[128,256]{1,0:T(8,128)(2,1)}, bf16[128,256]{1,0:T(8,128)(2,1)S(1)}, u32[]{:S(2)}, u32[]{:S(2)}) collective-permute-start(bf16[128,256]{1,0:T(8,128)(2,1)} %rest_4_.1), channel_id=1, source_target_pairs={{0,4},{4,0},{8,12},{12,8},{1,5},{5,1},{9,13},{13,9},{2,6},{6,2},{1... | collective-permute-start | bytes 196616 | tf_op jit(solution)/shard_map/ppermute | solution.py:263
  6.3 6.0 %collective-permute-start.1 = (bf16[128,256]{1,0:T(8,128)(2,1)}, bf16[128,256]{1,0:T(8,128)(2,1)S(1)}, u32[]{:S(2)}, u32[]{:S(2)}) collective-permute-start(bf16[128,256]{1,0:T(8,128)(2,1)} %rest_5_.1), channel_id=1, source_target_pairs={{0,8},{4,12},{8,0},{12,4},{1,9},{5,13},{9,1},{13,5},{2,10},{6,14},... | collective-permute-start | bytes 196616 | tf_op jit(solution)/shard_map/ppermute | solution.py:263
  6.6 5.6 %collective-permute-start.3 = (bf16[128,256]{1,0:T(8,128)(2,1)}, bf16[128,256]{1,0:T(8,128)(2,1)S(1)}, u32[]{:S(2)}, u32[]{:S(2)}) collective-permute-start(bf16[128,256]{1,0:T(8,128)(2,1)} %rest_5_.1), channel_id=1, source_target_pairs={{0,4},{4,0},{8,12},{12,8},{1,5},{5,1},{9,13},{13,9},{2,6},{6,2},{1... | collective-permute-start | bytes 196616 | tf_op jit(solution)/shard_map/ppermute | solution.py:263
  6.8 0.7 %copy-start.3 = (s32[128,1]{0,1:T(1,128)S(1)}, s32[128,1]{0,1:T(1,128)}, u32[]{:S(2)}) copy-start(s32[128,1]{0,1:T(1,128)} %param.8) | copy-start | bytes 1540
  6.8 0.7 %copy-start.4 = (s32[128,1]{0,1:T(1,128)S(1)}, s32[128,1]{0,1:T(1,128)}, u32[]{:S(2)}) copy-start(s32[128,1]{0,1:T(1,128)} %param.9) | copy-start | bytes 1540
  7.5 1.0 %copy-start = (bf16[128,2048]{1,0:T(8,128)(2,1)S(1)}, bf16[128,2048]{1,0:T(8,128)(2,1)}, u32[]{:S(2)}) copy-start(bf16[128,2048]{1,0:T(8,128)(2,1)} %q_hbm.1) | copy-start | bytes 1572868
  12.3 18.4 %copy-start.1 = (bf16[128,256]{1,0:T(8,128)(2,1)S(1)}, bf16[128,256]{1,0:T(8,128)(2,1)}, u32[]{:S(2)}) copy-start(bf16[128,256]{1,0:T(8,128)(2,1)} %rest_4_.1) | copy-start | bytes 196612
  12.3 18.4 %copy-start.2 = (bf16[128,256]{1,0:T(8,128)(2,1)S(1)}, bf16[128,256]{1,0:T(8,128)(2,1)}, u32[]{:S(2)}) copy-start(bf16[128,256]{1,0:T(8,128)(2,1)} %rest_5_.1) | copy-start | bytes 196612
  12.3 16.2 %collective-permute-start.4 = (bf16[784,128]{1,0:T(8,128)(2,1)S(1)}, bf16[784,128]{1,0:T(8,128)(2,1)S(1)}, u32[]{:S(2)}, u32[]{:S(2)}) collective-permute-start(bf16[784,128]{1,0:T(8,128)(2,1)S(1)} %get-tuple-element.17), channel_id=1, source_target_pairs={{0,4},{4,0},{8,12},{12,8},{1,5},{5,1},{9,13},{13,9},{2,6},{6,2},{1... | collective-permute-start | bytes 602120 | tf_op jit(solution)/shard_map/ppermute | solution.py:263
  13.5 17.1 %collective-permute-start.5 = (bf16[784,128]{1,0:T(8,128)(2,1)S(1)}, bf16[784,128]{1,0:T(8,128)(2,1)S(1)}, u32[]{:S(2)}, u32[]{:S(2)}) collective-permute-start(bf16[784,128]{1,0:T(8,128)(2,1)S(1)} %get-tuple-element.18), channel_id=1, source_target_pairs={{0,8},{4,12},{8,0},{12,4},{1,9},{5,13},{9,1},{13,5},{2,10},{6,14},... | collective-permute-start | bytes 602120 | tf_op jit(solution)/shard_map/ppermute | solution.py:263
  15.5 15.2 %collective-permute-start.6 = (bf16[784,128]{1,0:T(8,128)(2,1)S(1)}, bf16[784,128]{1,0:T(8,128)(2,1)S(1)}, u32[]{:S(2)}, u32[]{:S(2)}) collective-permute-start(bf16[784,128]{1,0:T(8,128)(2,1)S(1)} %get-tuple-element.19), channel_id=1, source_target_pairs={{0,12},{4,8},{8,4},{12,0},{1,13},{5,9},{9,5},{13,1},{2,14},{6,10},... | collective-permute-start | bytes 602120 | tf_op jit(solution)/shard_map/ppermute | solution.py:263
  16.8 11.7 %collective-permute-start.7 = (bf16[512,128]{1,0:T(8,128)(2,1)S(1)}, bf16[512,128]{1,0:T(8,128)(2,1)S(1)}, u32[]{:S(2)}, u32[]{:S(2)}) collective-permute-start(bf16[512,128]{1,0:T(8,128)(2,1)S(1)} %get-tuple-element.22), channel_id=1, source_target_pairs={{0,4},{4,0},{8,12},{12,8},{1,5},{5,1},{9,13},{13,9},{2,6},{6,2},{1... | collective-permute-start | bytes 393224 | tf_op jit(solution)/shard_map/ppermute | solution.py:263

commit v5 on v4

--- a/solution.py
+++ b/solution.py
@@ -181,36 +181,37 @@
                 ]
 
 
-def gate_kernel(k_ref, v_ref, *rest):
-    kv_ref = rest[-1]
-    rows = k_ref.shape[0]
-    at = 0
-    for source in (k_ref, v_ref):
-        for g in range(source.shape[1] // HD):
-            kv_ref[at : at + rows, :] = source[:, g * HD : (g + 1) * HD]
-            at += rows
+def gate_kernel(*refs):
+    rows = refs[0].shape[0]
+    for pair in range(2):
+        at = 0
+        for source in refs[2 * pair : 2 * pair + 2]:
+            for g in range(source.shape[1] // HD):
+                refs[len(refs) - 2 + pair][at : at + rows, :] = source[:, g * HD : (g + 1) * HD]
+                at += rows
 
 
 def attend_kernel(instances, capacity, heads, heads_kv, me_ref, *rest):
-    got, rest = rest[:instances], rest[instances:]
-    k_own, v_own, k_near, v_near, k_far, v_far, both = rest[:7]
-    att_ref, kc_ref, vc_ref, wanted_ref, keys, vals = rest[7:]
+    got, rest = dict(zip((0, 2, 3, 1), rest)), rest[instances:]
+    k_own, v_own, k_far, v_far, beside, both = rest[:6]
+    att_ref, kc_ref, vc_ref, wanted_ref, keys, vals = rest[6:]
     rows = HD
     per_group = heads // heads_kv
     tail = heads * capacity
     me = me_ref[0]
-    direct = ((k_own, v_own), (k_near, v_near), (k_far, v_far))
+    direct, joined = {0: (k_own, v_own), 2: (k_far, v_far)}, {1: beside, 3: both}
     for k in range(instances):
         source = jnp.bitwise_xor(me, k)
         wanted_ref[source] = got[k][...]
         at = pl.ds(pl.multiple_of(source * rows, rows), rows)
         for g in range(heads_kv):
-            if k < len(direct):
+            if k in direct:
                 keys[g, at, :] = direct[k][0][:, g * HD : (g + 1) * HD]
                 vals[g, at, :HD] = direct[k][1][:, g * HD : (g + 1) * HD]
             else:
-                keys[g, at, :] = both[g * rows : (g + 1) * rows, :]
-                vals[g, at, :HD] = both[(heads_kv + g) * rows : (heads_kv + g + 1) * rows, :]
+                start = heads_kv * rows
+                keys[g, at, :] = joined[k][g * rows : (g + 1) * rows, :]
+                vals[g, at, :HD] = joined[k][start + g * rows : start + (g + 1) * rows, :]
         vals[:, k * rows : (k + 1) * rows, HD:] = jnp.ones((heads_kv, rows, HD), jnp.bfloat16)
     lists = jnp.concatenate([wanted_ref[s, tail : tail + 16, :] for s in range(instances)], axis=0)
     wide = (lists.astype(jnp.float32) == me.astype(jnp.float32)).astype(jnp.float32)
@@ -268,7 +269,6 @@
     hbm = pl.BlockSpec(memory_space=pltpu.HBM)
     me = lax.axis_index("seq").astype(jnp.int32).reshape(1)
     k_far, v_far = swap(keys, 2), swap(values, 2)
-    k_near, v_near = swap(keys, 1), swap(values, 1)
     kv_tall = 2 * heads_kv * rows
     sends = pl.pallas_call(
         functools.partial(pack_kernel, instances, capacity),
@@ -281,24 +281,23 @@
         name="pack",
     )(me, queries, query_owner.reshape(1, rows), cache_owner.reshape(1, rows))
     anyspace = pl.BlockSpec(memory_space=pl.ANY)
-    through = [*sends[1:], k_near, v_near]
-    *through, kv_far = pl.pallas_call(
+    order = (2, 3, 1)
+    through = [sends[k] for k in order]
+    *through, own_kv, far_kv = pl.pallas_call(
         gate_kernel,
         out_shape=tuple(jax.ShapeDtypeStruct(x.shape, x.dtype) for x in through)
-        + (jax.ShapeDtypeStruct((kv_tall, HD), jnp.bfloat16),),
-        in_specs=[vmem, vmem] + [anyspace] * len(through),
-        out_specs=(anyspace,) * len(through) + (vmem,),
-        input_output_aliases={2 + i: i for i in range(len(through))},
+        + (jax.ShapeDtypeStruct((kv_tall, HD), jnp.bfloat16),) * 2,
+        in_specs=[vmem] * 4 + [anyspace] * len(through),
+        out_specs=(anyspace,) * len(through) + (vmem,) * 2,
+        input_output_aliases={4 + i: i for i in range(len(through))},
         compiler_params=pltpu.CompilerParams(vmem_limit_bytes=16 << 20),
         cost_estimate=pl.CostEstimate(flops=0, bytes_accessed=1 << 18, transcendentals=0),
         name="gate",
-    )(k_far, v_far, *through)
-    k_near, v_near = through[-2:]
-    sends = [sends[0], *through[:-2]]
+    )(keys, values, k_far, v_far, *through)
     got = {0: sends[0]}
-    for k in (2, 3, 1):
-        got[k] = swap(sends[k], k)
-    both = swap(kv_far, 1)
+    for k, slots_of in zip(order, through):
+        got[k] = swap(slots_of, k)
+    beside, both = swap(own_kv, 1), swap(far_kv, 1)
     slots = instances * capacity
     return pl.pallas_call(
         functools.partial(attend_kernel, instances, capacity, heads, heads_kv),
@@ -307,7 +306,7 @@
             jax.ShapeDtypeStruct((slots, heads_kv * HD), jnp.bfloat16),
             jax.ShapeDtypeStruct((slots, heads_kv * HD), jnp.bfloat16),
         ),
-        in_specs=[smem] + [vmem] * (instances + 7),
+        in_specs=[smem] + [vmem] * (instances + 6),
         out_specs=(vmem, vmem, vmem),
         scratch_shapes=[
             pltpu.VMEM((instances, tall, HD), jnp.bfloat16),
@@ -316,7 +315,7 @@
         ],
         compiler_params=pltpu.CompilerParams(vmem_limit_bytes=24 << 20),
         name="attend",
-    )(me, *[got[k] for k in range(instances)], keys, values, k_near, v_near, k_far, v_far, both)
+    )(me, *[got[k] for k in (0, *order)], keys, values, k_far, v_far, beside, both)
 
 
 def on_device(queries, keys, values, query_owner, cache_owner):

time: 34.2 us -> 37.4 us (1.094)
  waiting for transfers between devices: 16.8 us -> 20.6 us
  starting transfers between devices: 10.9 us -> 10.2 us
    ppermute x8 -> x7, waiting for transfers between devices: 16.8 us -> 20.6 us  [swap(): return lax.ppermute(array, 'seq', [(i, i ^ k) for i in range(instances)])]
    ppermute x8 -> x7, starting transfers between devices: 10.9 us -> 10.2 us  [swap(): return lax.ppermute(array, 'seq', [(i, i ^ k) for i in range(instances)])]
  transfers between devices with their start and end apart: 8 -> 7, of which waited for: 4 -> 4; matrix products, arithmetic and copies ran while one was open for 0% -> 0% of each run, Pallas kernels for 2% -> 1%
where the time goes in v5:
time: 37.4 us; the launch traced here: 37.2 us
  waiting for transfers between devices  20.6 us (55%)
  starting transfers between devices  10.2 us (27%)
  Pallas kernels  3.96 us (11%)
  local copies, waits for them, and re-layouts  1.72 us (5%)
  between operations  0.67 us (2%)
    ppermute x7, waiting for transfers between devices, swap(): return lax.ppermute(array, 'seq', [(i, i ^ k) for i in range(instances)])  20.6 us
    ppermute x7, starting transfers between devices, swap(): return lax.ppermute(array, 'seq', [(i, i ^ k) for i in range(instances)])  10.2 us
    pallas_call x1, Pallas kernels, few_instances(): pl.pallas_call(functools.partial(attend_kernel, instances, capacity, head...  3.37 us
    unnamed x10, local copies, waits for them, and re-layouts  1.72 us
  transfers between devices with their start and end apart: 7, of which 4 were waited for; matrix products, arithmetic and copies ran while one was open for 0% of the time, Pallas kernels for 1%

profile of v5, /device:TPU:0, one launch (start us, length us, event | category | flops | bytes accessed | tf_op | source)
XLA Modules:
  0.0 37.2 jit_solution(17328119887512959326)
XLA Ops:
  0.6 4.1 %collective-permute-start = (bf16[128,256]{1,0:T(8,128)(2,1)}, bf16[128,256]{1,0:T(8,128)(2,1)S(1)}, u32[]{:S(2)}, u32[]{:S(2)}) collective-permute-start(bf16[128,256]{1,0:T(8,128)(2,1)} %rest_4_.1), channel_id=1, source_target_pairs={{0,8},{4,12},{8,0},{12,4},{1,9},{5,13},{9,1},{13,5},{2,10},{6,14},... | collective-permute-start | bytes 196616 | tf_op jit(solution)/shard_map/ppermute | solution.py:264
  4.7 0.1 collective-permute-start.1
  4.8 0.0 copy-start.3
  4.8 0.0 copy-start.4
  4.8 0.7 %copy-done.3 = s32[128,1]{0,1:T(1,128)S(1)} copy-done((s32[128,1]{0,1:T(1,128)S(1)}, s32[128,1]{0,1:T(1,128)}, u32[]{:S(2)}) %copy-start.3) | copy-done | bytes 536
  5.5 0.0 copy-done.4
  5.5 0.0 copy-start
  5.5 1.0 %copy-done = bf16[128,2048]{1,0:T(8,128)(2,1)S(1)} copy-done((bf16[128,2048]{1,0:T(8,128)(2,1)S(1)}, bf16[128,2048]{1,0:T(8,128)(2,1)}, u32[]{:S(2)}) %copy-start) | copy-done | bytes 524312
  6.5 0.0 copy-start.1
  6.5 0.0 copy-start.2
  6.5 0.5 %pack.1 = (bf16[784,128]{1,0:T(8,128)(2,1)S(1)}, bf16[784,128]{1,0:T(8,128)(2,1)S(1)}, bf16[784,128]{1,0:T(8,128)(2,1)S(1)}, bf16[784,128]{1,0:T(8,128)(2,1)S(1)}) custom-call(s32[1]{0:T(128)} %bitcast.me_ref, bf16[128,2048]{1,0:T(8,128)(2,1)S(1)} %copy-done, s32[1,128]{1,0:T(1,128)S(1)} %bitcast.3, s32[1,128]{1,0:T(1,128)S(1)} %bitcast.4), custom_call_target="tpu_custom_call" | custom-call | flops 134217728 | bytes 2097152 | tf_op jit(solution)/shard_map/pack/pallas_call | solution.py:273
  7.1 1.5 %collective-permute-done.refs_2_.rest_6_ = bf16[128,256]{1,0:T(8,128)(2,1)S(1)} collective-permute-done((bf16[128,256]{1,0:T(8,128)(2,1)}, bf16[128,256]{1,0:T(8,128)(2,1)S(1)}, u32[]{:S(2)}, u32[]{:S(2)}) %collective-permute-start) | collective-permute-done | bytes 65568 | tf_op jit(solution)/shard_map/ppermute | solution.py:264
  8.6 2.8 %collective-permute-done.1.refs_3_.rest_7_ = bf16[128,256]{1,0:T(8,128)(2,1)S(1)} collective-permute-done((bf16[128,256]{1,0:T(8,128)(2,1)}, bf16[128,256]{1,0:T(8,128)(2,1)S(1)}, u32[]{:S(2)}, u32[]{:S(2)}) %collective-permute-start.1) | collective-permute-done | bytes 65568 | tf_op jit(solution)/shard_map/ppermute | solution.py:264
  11.4 0.0 copy-done.1
  11.4 0.0 copy-done.2
  11.5 0.1 collective-permute-start.2
  11.5 3.5 %collective-permute-start.3 = (bf16[784,128]{1,0:T(8,128)(2,1)S(1)}, bf16[784,128]{1,0:T(8,128)(2,1)S(1)}, u32[]{:S(2)}, u32[]{:S(2)}) collective-permute-start(bf16[784,128]{1,0:T(8,128)(2,1)S(1)} %get-tuple-element.17), channel_id=1, source_target_pairs={{0,12},{4,8},{8,4},{12,0},{1,13},{5,9},{9,5},{13,1},{2,14},{6,10},... | collective-permute-start | bytes 602120 | tf_op jit(solution)/shard_map/ppermute | solution.py:264
  15.0 0.5 %collective-permute-start.4 = (bf16[784,128]{1,0:T(8,128)(2,1)S(1)}, bf16[784,128]{1,0:T(8,128)(2,1)S(1)}, u32[]{:S(2)}, u32[]{:S(2)}) collective-permute-start(bf16[784,128]{1,0:T(8,128)(2,1)S(1)} %get-tuple-element.18), channel_id=1, source_target_pairs={{0,4},{4,0},{8,12},{12,8},{1,5},{5,1},{9,13},{13,9},{2,6},{6,2},{1... | collective-permute-start | bytes 602120 | tf_op jit(solution)/shard_map/ppermute | solution.py:264
  15.5 1.5 %collective-permute-start.5 = (bf16[512,128]{1,0:T(8,128)(2,1)S(1)}, bf16[512,128]{1,0:T(8,128)(2,1)S(1)}, u32[]{:S(2)}, u32[]{:S(2)}) collective-permute-start(bf16[512,128]{1,0:T(8,128)(2,1)S(1)} %get-tuple-element.19), channel_id=1, source_target_pairs={{0,4},{4,0},{8,12},{12,8},{1,5},{5,1},{9,13},{13,9},{2,6},{6,2},{1... | collective-permute-start | bytes 393224 | tf_op jit(solution)/shard_map/ppermute | solution.py:264
  17.0 0.5 %collective-permute-start.6 = (bf16[512,128]{1,0:T(8,128)(2,1)S(1)}, bf16[512,128]{1,0:T(8,128)(2,1)S(1)}, u32[]{:S(2)}, u32[]{:S(2)}) collective-permute-start(bf16[512,128]{1,0:T(8,128)(2,1)S(1)} %get-tuple-element.20), channel_id=1, source_target_pairs={{0,4},{4,0},{8,12},{12,8},{1,5},{5,1},{9,13},{13,9},{2,6},{6,2},{1... | collective-permute-start | bytes 393224 | tf_op jit(solution)/shard_map/ppermute | solution.py:264
  17.5 14.8 %collective-permute-done.5.rest_8_ = bf16[512,128]{1,0:T(8,128)(2,1)S(1)} collective-permute-done((bf16[512,128]{1,0:T(8,128)(2,1)S(1)}, bf16[512,128]{1,0:T(8,128)(2,1)S(1)}, u32[]{:S(2)}, u32[]{:S(2)}) %collective-permute-start.5) | collective-permute-done | bytes 131104 | tf_op jit(solution)/shard_map/ppermute | solution.py:264
  32.3 1.5 %collective-permute-done.6.rest_9_ = bf16[512,128]{1,0:T(8,128)(2,1)S(1)} collective-permute-done((bf16[512,128]{1,0:T(8,128)(2,1)S(1)}, bf16[512,128]{1,0:T(8,128)(2,1)S(1)}, u32[]{:S(2)}, u32[]{:S(2)}) %collective-permute-start.6) | collective-permute-done | bytes 131104 | tf_op jit(solution)/shard_map/ppermute | solution.py:264
  33.8 0.0 collective-permute-done.2.rest_1_
  33.8 0.0 collective-permute-done.3.rest_2_
  33.8 0.0 collective-permute-done.4.rest_3_
  33.8 3.4 %attend.1 = (bf16[192,2048]{1,0:T(8,128)(2,1)}, bf16[192,256]{1,0:T(8,128)(2,1)}, bf16[192,256]{1,0:T(8,128)(2,1)}) custom-call(s32[1]{0:T(128)} %bitcast.me_ref, bf16[784,128]{1,0:T(8,128)(2,1)S(1)} %get-tuple-element.12.rest_0_, bf16[784,128]{1,0:T(8,128)(2,1)S(1)} %collective-permute-done.2.rest_1_, bf16[784,128]{1,0:T(8,128)(2,1)S(1)} %collective-permute-done.3.rest_2_, ...), custom_call_target="tpu_custom_call" | custom-call | tf_op jit(solution)/shard_map/attend/pallas_call | solution.py:302
  (1 shorter events, 0.0 us)
Async XLA Ops:
  0.6 8.0 %collective-permute-start = (bf16[128,256]{1,0:T(8,128)(2,1)}, bf16[128,256]{1,0:T(8,128)(2,1)S(1)}, u32[]{:S(2)}, u32[]{:S(2)}) collective-permute-start(bf16[128,256]{1,0:T(8,128)(2,1)} %rest_4_.1), channel_id=1, source_target_pairs={{0,8},{4,12},{8,0},{12,4},{1,9},{5,13},{9,1},{13,5},{2,10},{6,14},... | collective-permute-start | bytes 196616 | tf_op jit(solution)/shard_map/ppermute | solution.py:264
  4.7 6.7 %collective-permute-start.1 = (bf16[128,256]{1,0:T(8,128)(2,1)}, bf16[128,256]{1,0:T(8,128)(2,1)S(1)}, u32[]{:S(2)}, u32[]{:S(2)}) collective-permute-start(bf16[128,256]{1,0:T(8,128)(2,1)} %rest_5_.1), channel_id=1, source_target_pairs={{0,8},{4,12},{8,0},{12,4},{1,9},{5,13},{9,1},{13,5},{2,10},{6,14},... | collective-permute-start | bytes 196616 | tf_op jit(solution)/shard_map/ppermute | solution.py:264
  4.8 0.7 %copy-start.3 = (s32[128,1]{0,1:T(1,128)S(1)}, s32[128,1]{0,1:T(1,128)}, u32[]{:S(2)}) copy-start(s32[128,1]{0,1:T(1,128)} %param.8) | copy-start | bytes 1540
  4.8 0.7 %copy-start.4 = (s32[128,1]{0,1:T(1,128)S(1)}, s32[128,1]{0,1:T(1,128)}, u32[]{:S(2)}) copy-start(s32[128,1]{0,1:T(1,128)} %param.9) | copy-start | bytes 1540
  5.5 1.0 %copy-start = (bf16[128,2048]{1,0:T(8,128)(2,1)S(1)}, bf16[128,2048]{1,0:T(8,128)(2,1)}, u32[]{:S(2)}) copy-start(bf16[128,2048]{1,0:T(8,128)(2,1)} %q_hbm.1) | copy-start | bytes 1572868
  6.5 4.9 %copy-start.1 = (bf16[128,256]{1,0:T(8,128)(2,1)S(1)}, bf16[128,256]{1,0:T(8,128)(2,1)}, u32[]{:S(2)}) copy-start(bf16[128,256]{1,0:T(8,128)(2,1)} %rest_4_.1) | copy-start | bytes 196612
  6.5 4.9 %copy-start.2 = (bf16[128,256]{1,0:T(8,128)(2,1)S(1)}, bf16[128,256]{1,0:T(8,128)(2,1)}, u32[]{:S(2)}) copy-start(bf16[128,256]{1,0:T(8,128)(2,1)} %rest_5_.1) | copy-start | bytes 196612
  11.5 22.4 %collective-permute-start.2 = (bf16[784,128]{1,0:T(8,128)(2,1)S(1)}, bf16[784,128]{1,0:T(8,128)(2,1)S(1)}, u32[]{:S(2)}, u32[]{:S(2)}) collective-permute-start(bf16[784,128]{1,0:T(8,128)(2,1)S(1)} %get-tuple-element.16), channel_id=1, source_target_pairs={{0,8},{4,12},{8,0},{12,4},{1,9},{5,13},{9,1},{13,5},{2,10},{6,14},... | collective-permute-start | bytes 602120 | tf_op jit(solution)/shard_map/ppermute | solution.py:264
  11.5 22.3 %collective-permute-start.3 = (bf16[784,128]{1,0:T(8,128)(2,1)S(1)}, bf16[784,128]{1,0:T(8,128)(2,1)S(1)}, u32[]{:S(2)}, u32[]{:S(2)}) collective-permute-start(bf16[784,128]{1,0:T(8,128)(2,1)S(1)} %get-tuple-element.17), channel_id=1, source_target_pairs={{0,12},{4,8},{8,4},{12,0},{1,13},{5,9},{9,5},{13,1},{2,14},{6,10},... | collective-permute-start | bytes 602120 | tf_op jit(solution)/shard_map/ppermute | solution.py:264
  15.0 18.8 %collective-permute-start.4 = (bf16[784,128]{1,0:T(8,128)(2,1)S(1)}, bf16[784,128]{1,0:T(8,128)(2,1)S(1)}, u32[]{:S(2)}, u32[]{:S(2)}) collective-permute-start(bf16[784,128]{1,0:T(8,128)(2,1)S(1)} %get-tuple-element.18), channel_id=1, source_target_pairs={{0,4},{4,0},{8,12},{12,8},{1,5},{5,1},{9,13},{13,9},{2,6},{6,2},{1... | collective-permute-start | bytes 602120 | tf_op jit(solution)/shard_map/ppermute | solution.py:264
  15.5 16.8 %collective-permute-start.5 = (bf16[512,128]{1,0:T(8,128)(2,1)S(1)}, bf16[512,128]{1,0:T(8,128)(2,1)S(1)}, u32[]{:S(2)}, u32[]{:S(2)}) collective-permute-start(bf16[512,128]{1,0:T(8,128)(2,1)S(1)} %get-tuple-element.19), channel_id=1, source_target_pairs={{0,4},{4,0},{8,12},{12,8},{1,5},{5,1},{9,13},{13,9},{2,6},{6,2},{1... | collective-permute-start | bytes 393224 | tf_op jit(solution)/shard_map/ppermute | solution.py:264
  17.0 16.8 %collective-permute-start.6 = (bf16[512,128]{1,0:T(8,128)(2,1)S(1)}, bf16[512,128]{1,0:T(8,128)(2,1)S(1)}, u32[]{:S(2)}, u32[]{:S(2)}) collective-permute-start(bf16[512,128]{1,0:T(8,128)(2,1)S(1)} %get-tuple-element.20), channel_id=1, source_target_pairs={{0,4},{4,0},{8,12},{12,8},{1,5},{5,1},{9,13},{13,9},{2,6},{6,2},{1... | collective-permute-start | bytes 393224 | tf_op jit(solution)/shard_map/ppermute | solution.py:264

commit v6 on v4

--- a/solution.py
+++ b/solution.py
@@ -165,7 +165,7 @@
         [owners, co_ref[...], jnp.full((14, rows), -1, jnp.int32)], axis=0
     ).astype(jnp.float32).astype(jnp.bfloat16)
     for k in range(instances):
-        sends[k][heads * capacity :, :] = lists
+        sends[k][heads * capacity : heads * capacity + 16, :] = lists
     fetch.wait()
     for pair in range(heads // 2):
         packed = jnp.dot(
@@ -181,20 +181,30 @@
                 ]
 
 
-def gate_kernel(k_ref, v_ref, *rest):
-    kv_ref = rest[-1]
+def gate_kernel(tall, heads_kv, k_ref, v_ref, *rest):
+    beside, copied = rest[-2:]
     rows = k_ref.shape[0]
-    at = 0
-    for source in (k_ref, v_ref):
-        for g in range(source.shape[1] // HD):
-            kv_ref[at : at + rows, :] = source[:, g * HD : (g + 1) * HD]
-            at += rows
+    copies = []
+    for index, source in enumerate((k_ref, v_ref)):
+        for g in range(heads_kv):
+            place = index * heads_kv + g
+            copies.append(
+                pltpu.make_async_copy(
+                    source.at[:, g * HD : (g + 1) * HD],
+                    beside.at[tall + place * rows : tall + (place + 1) * rows, :],
+                    copied.at[place],
+                )
+            )
+    for copy in copies:
+        copy.start()
+    for copy in copies:
+        copy.wait()
 
 
 def attend_kernel(instances, capacity, heads, heads_kv, me_ref, *rest):
     got, rest = rest[:instances], rest[instances:]
-    k_own, v_own, k_near, v_near, k_far, v_far, both = rest[:7]
-    att_ref, kc_ref, vc_ref, wanted_ref, keys, vals = rest[7:]
+    k_own, v_own, k_near, v_near, k_far, v_far = rest[:6]
+    att_ref, kc_ref, vc_ref, wanted_ref, keys, vals = rest[6:]
     rows = HD
     per_group = heads // heads_kv
     tail = heads * capacity
@@ -202,15 +212,17 @@
     direct = ((k_own, v_own), (k_near, v_near), (k_far, v_far))
     for k in range(instances):
         source = jnp.bitwise_xor(me, k)
-        wanted_ref[source] = got[k][...]
+        wanted_ref[source] = got[k][: tail + 16, :]
         at = pl.ds(pl.multiple_of(source * rows, rows), rows)
         for g in range(heads_kv):
             if k < len(direct):
                 keys[g, at, :] = direct[k][0][:, g * HD : (g + 1) * HD]
                 vals[g, at, :HD] = direct[k][1][:, g * HD : (g + 1) * HD]
             else:
-                keys[g, at, :] = both[g * rows : (g + 1) * rows, :]
-                vals[g, at, :HD] = both[(heads_kv + g) * rows : (heads_kv + g + 1) * rows, :]
+                start = tail + 16 + g * rows
+                keys[g, at, :] = got[1][start : start + rows, :]
+                start = start + heads_kv * rows
+                vals[g, at, :HD] = got[1][start : start + rows, :]
         vals[:, k * rows : (k + 1) * rows, HD:] = jnp.ones((heads_kv, rows, HD), jnp.bfloat16)
     lists = jnp.concatenate([wanted_ref[s, tail : tail + 16, :] for s in range(instances)], axis=0)
     wide = (lists.astype(jnp.float32) == me.astype(jnp.float32)).astype(jnp.float32)
@@ -218,7 +230,7 @@
     r = lax.broadcasted_iota(jnp.int32, (rows, 2 * rows), 0)
     u = lax.broadcasted_iota(jnp.int32, (rows, 2 * rows), 1)
     reach = ((u <= r) | (u >= rows)).astype(jnp.bfloat16)
-    scale = 1.0 / math.sqrt(HD)
+    scale = math.log2(math.e) / math.sqrt(HD)
     for s in range(instances):
         q_at, c_at = 16 * s, 16 * s + 1
         cache_pick = picks(wide[c_at : c_at + 1], earlier[c_at : c_at + 1], capacity)
@@ -245,7 +257,7 @@
             last = jnp.where(near, scores[:, s * rows :], neg_big)
             scores = jnp.concatenate([scores[:, : s * rows], last], axis=1) if s else last
             top = jnp.max(scores, axis=1, keepdims=True)
-            weights = jnp.exp((scores - top) * scale).astype(jnp.bfloat16)
+            weights = jnp.exp2(scores * scale - top * scale).astype(jnp.bfloat16)
             mixed = jnp.dot(weights, vals[g, : (s + 1) * rows, :], preferred_element_type=jnp.float32)
             out = jnp.where(valid, mixed[:, :HD] / mixed[:, HD:], 0.0).astype(jnp.bfloat16)
             for h in range(per_group):
@@ -272,7 +284,10 @@
     kv_tall = 2 * heads_kv * rows
     sends = pl.pallas_call(
         functools.partial(pack_kernel, instances, capacity),
-        out_shape=(jax.ShapeDtypeStruct((tall, HD), jnp.bfloat16),) * instances,
+        out_shape=tuple(
+            jax.ShapeDtypeStruct((tall + kv_tall * (k == 1), HD), jnp.bfloat16)
+            for k in range(instances)
+        ),
         in_specs=[smem, hbm, vmem, vmem],
         out_specs=(vmem,) * instances,
         scratch_shapes=[pltpu.VMEM(queries.shape, jnp.bfloat16), pltpu.SemaphoreType.DMA],
@@ -281,24 +296,19 @@
         name="pack",
     )(me, queries, query_owner.reshape(1, rows), cache_owner.reshape(1, rows))
     anyspace = pl.BlockSpec(memory_space=pl.ANY)
-    through = [*sends[1:], k_near, v_near]
-    *through, kv_far = pl.pallas_call(
-        gate_kernel,
-        out_shape=tuple(jax.ShapeDtypeStruct(x.shape, x.dtype) for x in through)
-        + (jax.ShapeDtypeStruct((kv_tall, HD), jnp.bfloat16),),
-        in_specs=[vmem, vmem] + [anyspace] * len(through),
-        out_specs=(anyspace,) * len(through) + (vmem,),
+    through = [sends[2], sends[3], k_near, v_near, sends[1]]
+    through = pl.pallas_call(
+        functools.partial(gate_kernel, tall, heads_kv),
+        out_shape=tuple(jax.ShapeDtypeStruct(x.shape, x.dtype) for x in through),
+        in_specs=[anyspace] * (len(through) + 2),
+        out_specs=(anyspace,) * len(through),
         input_output_aliases={2 + i: i for i in range(len(through))},
-        compiler_params=pltpu.CompilerParams(vmem_limit_bytes=16 << 20),
+        scratch_shapes=[pltpu.SemaphoreType.DMA((2 * heads_kv,))],
         cost_estimate=pl.CostEstimate(flops=0, bytes_accessed=1 << 18, transcendentals=0),
         name="gate",
     )(k_far, v_far, *through)
-    k_near, v_near = through[-2:]
-    sends = [sends[0], *through[:-2]]
-    got = {0: sends[0]}
-    for k in (2, 3, 1):
-        got[k] = swap(sends[k], k)
-    both = swap(kv_far, 1)
+    k_near, v_near = through[2:4]
+    got = (sends[0], swap(through[4], 1), swap(through[0], 2), swap(through[1], 3))
     slots = instances * capacity
     return pl.pallas_call(
         functools.partial(attend_kernel, instances, capacity, heads, heads_kv),
@@ -307,7 +317,7 @@
             jax.ShapeDtypeStruct((slots, heads_kv * HD), jnp.bfloat16),
             jax.ShapeDtypeStruct((slots, heads_kv * HD), jnp.bfloat16),
         ),
-        in_specs=[smem] + [vmem] * (instances + 7),
+        in_specs=[smem] + [vmem] * (instances + 6),
         out_specs=(vmem, vmem, vmem),
         scratch_shapes=[
             pltpu.VMEM((instances, tall, HD), jnp.bfloat16),
@@ -316,7 +326,7 @@
         ],
         compiler_params=pltpu.CompilerParams(vmem_limit_bytes=24 << 20),
         name="attend",
-    )(me, *[got[k] for k in range(instances)], keys, values, k_near, v_near, k_far, v_far, both)
+    )(me, *[got[k] for k in range(instances)], keys, values, k_near, v_near, k_far, v_far)
 
 
 def on_device(queries, keys, values, query_owner, cache_owner):

time: 34.2 us -> 44 us (1.29)
  local copies, waits for them, and re-layouts: 1.72 us -> 7.76 us
  Pallas kernels: 3.93 us -> 8.99 us
  waiting for transfers between devices: 16.8 us -> 15.5 us
    unnamed x10 -> x32, local copies, waits for them, and re-layouts: 1.72 us -> 7.76 us
    pallas_call x1, Pallas kernels: 0.02 us -> 5.1 us  [few_instances(): pl.pallas_call(functools.partial(gate_kernel, tall, heads_kv), out_shape=...]
    ppermute x8 -> x7, waiting for transfers between devices: 16.8 us -> 15.5 us  [swap(): return lax.ppermute(array, 'seq', [(i, i ^ k) for i in range(instances)])]
    ppermute x8 -> x7, starting transfers between devices: 10.9 us -> 10.7 us  [swap(): return lax.ppermute(array, 'seq', [(i, i ^ k) for i in range(instances)])]
  transfers between devices with their start and end apart: 8 -> 7, of which waited for: 4 -> 2; matrix products, arithmetic and copies ran while one was open for 0% -> 0% of each run, Pallas kernels for 2% -> 1%
where the time goes in v6:
time: 44 us; the launch traced here: 43.6 us
  waiting for transfers between devices  15.5 us (35%)
  starting transfers between devices  10.7 us (24%)
  Pallas kernels  8.99 us (20%)
  local copies, waits for them, and re-layouts  7.76 us (18%)
  between operations  0.72 us (2%)
    ppermute x7, waiting for transfers between devices, swap(): return lax.ppermute(array, 'seq', [(i, i ^ k) for i in range(instances)])  15.5 us
    ppermute x7, starting transfers between devices, swap(): return lax.ppermute(array, 'seq', [(i, i ^ k) for i in range(instances)])  10.7 us
    unnamed x32, local copies, waits for them, and re-layouts  7.76 us
    pallas_call x1, Pallas kernels, few_instances(): pl.pallas_call(functools.partial(gate_kernel, tall, heads_kv), out_shape=...  5.1 us
    pallas_call x1, Pallas kernels, few_instances(): pl.pallas_call(functools.partial(attend_kernel, instances, capacity, head...  3.34 us
  transfers between devices with their start and end apart: 7, of which 2 were waited for; matrix products, arithmetic and copies ran while one was open for 0% of the time, Pallas kernels for 1%

profile of v6, /device:TPU:0, one launch (start us, length us, event | category | flops | bytes accessed | tf_op | source)
XLA Modules:
  0.0 43.6 jit_solution(14238928444788170825)
XLA Ops:
  0.6 4.1 %collective-permute-start = (bf16[128,256]{1,0:T(8,128)(2,1)}, bf16[128,256]{1,0:T(8,128)(2,1)S(1)}, u32[]{:S(2)}, u32[]{:S(2)}) collective-permute-start(bf16[128,256]{1,0:T(8,128)(2,1)} %rest_4_.1), channel_id=1, source_target_pairs={{0,8},{4,12},{8,0},{12,4},{1,9},{5,13},{9,1},{13,5},{2,10},{6,14},... | collective-permute-start | bytes 196616 | tf_op jit(solution)/shard_map/ppermute | solution.py:275
  4.7 1.6 %collective-permute-start.2 = (bf16[128,256]{1,0:T(8,128)(2,1)}, bf16[128,256]{1,0:T(8,128)(2,1)S(1)}, u32[]{:S(2)}, u32[]{:S(2)}) collective-permute-start(bf16[128,256]{1,0:T(8,128)(2,1)} %rest_4_.1), channel_id=1, source_target_pairs={{0,4},{4,0},{8,12},{12,8},{1,5},{5,1},{9,13},{13,9},{2,6},{6,2},{1... | collective-permute-start | bytes 196616 | tf_op jit(solution)/shard_map/ppermute | solution.py:275
  6.3 0.3 collective-permute-start.1
  6.6 0.2 collective-permute-start.3
  6.8 0.0 copy-start.14
  6.8 0.0 copy-start.15
  6.8 0.7 %copy-done.14 = s32[128,1]{0,1:T(1,128)S(1)} copy-done((s32[128,1]{0,1:T(1,128)S(1)}, s32[128,1]{0,1:T(1,128)}, u32[]{:S(2)}) %copy-start.14) | copy-done | bytes 536
  7.5 0.0 copy-done.15
  7.5 0.0 copy-start
  7.5 1.0 %copy-done = bf16[128,2048]{1,0:T(8,128)(2,1)S(1)} copy-done((bf16[128,2048]{1,0:T(8,128)(2,1)S(1)}, bf16[128,2048]{1,0:T(8,128)(2,1)}, u32[]{:S(2)}) %copy-start) | copy-done | bytes 524312
  8.6 0.5 %pack.1 = (bf16[784,128]{1,0:T(8,128)(2,1)S(1)}, bf16[1296,128]{1,0:T(8,128)(2,1)S(1)}, bf16[784,128]{1,0:T(8,128)(2,1)S(1)}, bf16[784,128]{1,0:T(8,128)(2,1)S(1)}) custom-call(s32[1]{0:T(128)} %bitcast.me_ref, bf16[128,2048]{1,0:T(8,128)(2,1)S(1)} %copy-done, s32[1,128]{1,0:T(1,128)S(1)} %bitcast.3, s32[1,128]{1,0:T(1,128)S(1)} %bitcast.4), custom_call_target="tpu_custom_call" | custom-call | flops 134217728 | bytes 2097152 | tf_op jit(solution)/shard_map/pack/pallas_call | solution.py:285
  9.1 0.0 copy-start.1
  9.1 0.7 %copy-done.1 = bf16[1296,128]{1,0:T(8,128)(2,1)} copy-done((bf16[1296,128]{1,0:T(8,128)(2,1)}, bf16[1296,128]{1,0:T(8,128)(2,1)S(1)}, u32[]{:S(2)}) %copy-start.1) | copy-done | bytes 331800
  9.8 0.0 copy-start.10
  9.8 0.7 %copy-done.10 = bf16[784,128]{1,0:T(8,128)(2,1)} copy-done((bf16[784,128]{1,0:T(8,128)(2,1)}, bf16[784,128]{1,0:T(8,128)(2,1)S(1)}, u32[]{:S(2)}) %copy-start.10) | copy-done | bytes 200728
  10.5 0.0 copy-start.11
  10.5 0.7 %copy-done.11 = bf16[784,128]{1,0:T(8,128)(2,1)} copy-done((bf16[784,128]{1,0:T(8,128)(2,1)}, bf16[784,128]{1,0:T(8,128)(2,1)S(1)}, u32[]{:S(2)}) %copy-start.11) | copy-done | bytes 200728
  11.2 0.0 collective-permute-done.k_ref.rest_8_
  11.2 0.0 copy-start.2
  11.2 0.0 collective-permute-done.2.rest_2_
  11.2 0.0 copy-start.6
  11.2 1.1 %collective-permute-done.1.v_ref.rest_9_ = bf16[128,256]{1,0:T(8,128)(2,1)S(1)} collective-permute-done((bf16[128,256]{1,0:T(8,128)(2,1)}, bf16[128,256]{1,0:T(8,128)(2,1)S(1)}, u32[]{:S(2)}, u32[]{:S(2)}) %collective-permute-start.1) | collective-permute-done | bytes 65568 | tf_op jit(solution)/shard_map/ppermute | solution.py:275
  12.3 0.0 copy-start.4
  12.3 0.0 collective-permute-done.3.rest_3_
  12.3 0.0 copy-start.8
  12.3 0.0 copy-done.2
  12.3 0.0 copy-done.6
  12.3 0.6 %copy-done.4 = bf16[128,256]{1,0:T(8,128)(2,1)} copy-done((bf16[128,256]{1,0:T(8,128)(2,1)}, bf16[128,256]{1,0:T(8,128)(2,1)S(1)}, u32[]{:S(2)}) %copy-start.4) | copy-done | bytes 65560
  12.9 0.0 copy-done.8
  12.9 0.0 copy-start.12
  12.9 0.0 copy-start.13
  12.9 5.1 %gate.1 = (bf16[784,128]{1,0:T(8,128)(2,1)}, bf16[784,128]{1,0:T(8,128)(2,1)}, bf16[128,256]{1,0:T(8,128)(2,1)}, bf16[128,256]{1,0:T(8,128)(2,1)}, bf16[1296,128]{1,0:T(8,128)(2,1)}) custom-call(bf16[128,256]{1,0:T(8,128)(2,1)} %copy-done.2, ...), custom_call_target="tpu_custom_call", output_to_operand_aliasing={{0}: (2, {}), {1}: (3, {}), {2}: (4, {}), {3}: (5, {}), {4}... | custom-call | bytes 262144 | tf_op jit(solution)/shard_map/gate/pallas_call | solution.py:300
  18.0 1.2 %collective-permute-start.4 = (bf16[1296,128]{1,0:T(8,128)(2,1)}, bf16[1296,128]{1,0:T(8,128)(2,1)S(1)}, u32[]{:S(2)}, u32[]{:S(2)}) collective-permute-start(bf16[1296,128]{1,0:T(8,128)(2,1)} %get-tuple-element.16), channel_id=1, source_target_pairs={{0,4},{4,0},{8,12},{12,8},{1,5},{5,1},{9,13},{13,9},{2,6},{6,2},{1... | collective-permute-start | bytes 995336 | tf_op jit(solution)/shard_map/ppermute | solution.py:275
  19.2 2.2 %collective-permute-start.5 = (bf16[784,128]{1,0:T(8,128)(2,1)}, bf16[784,128]{1,0:T(8,128)(2,1)S(1)}, u32[]{:S(2)}, u32[]{:S(2)}) collective-permute-start(bf16[784,128]{1,0:T(8,128)(2,1)} %get-tuple-element.17), channel_id=1, source_target_pairs={{0,8},{4,12},{8,0},{12,4},{1,9},{5,13},{9,1},{13,5},{2,10},{6,14},... | collective-permute-start | bytes 602120 | tf_op jit(solution)/shard_map/ppermute | solution.py:275
  21.5 1.0 %collective-permute-start.6 = (bf16[784,128]{1,0:T(8,128)(2,1)}, bf16[784,128]{1,0:T(8,128)(2,1)S(1)}, u32[]{:S(2)}, u32[]{:S(2)}) collective-permute-start(bf16[784,128]{1,0:T(8,128)(2,1)} %get-tuple-element.18), channel_id=1, source_target_pairs={{0,12},{4,8},{8,4},{12,0},{1,13},{5,9},{9,5},{13,1},{2,14},{6,10},... | collective-permute-start | bytes 602120 | tf_op jit(solution)/shard_map/ppermute | solution.py:275
  22.5 14.4 %collective-permute-done.5.rest_2_ = bf16[784,128]{1,0:T(8,128)(2,1)S(1)} collective-permute-done((bf16[784,128]{1,0:T(8,128)(2,1)}, bf16[784,128]{1,0:T(8,128)(2,1)S(1)}, u32[]{:S(2)}, u32[]{:S(2)}) %collective-permute-start.5) | collective-permute-done | bytes 200736 | tf_op jit(solution)/shard_map/ppermute | solution.py:275
  36.9 0.0 collective-permute-done.6.rest_3_
  36.9 0.0 collective-permute-done.4.rest_1_
  36.9 0.0 copy-done.12
  36.9 0.0 copy-done.13
  36.9 0.0 copy-start.3
  36.9 0.8 %copy-done.3 = bf16[128,256]{1,0:T(8,128)(2,1)S(1)} copy-done((bf16[128,256]{1,0:T(8,128)(2,1)S(1)}, bf16[128,256]{1,0:T(8,128)(2,1)}, u32[]{:S(2)}) %copy-start.3) | copy-done | bytes 65560
  37.7 0.0 copy-start.5
  37.7 0.8 %copy-done.5 = bf16[128,256]{1,0:T(8,128)(2,1)S(1)} copy-done((bf16[128,256]{1,0:T(8,128)(2,1)S(1)}, bf16[128,256]{1,0:T(8,128)(2,1)}, u32[]{:S(2)}) %copy-start.5) | copy-done | bytes 65560
  38.6 0.0 copy-start.7
  38.6 0.8 %copy-done.7 = bf16[128,256]{1,0:T(8,128)(2,1)S(1)} copy-done((bf16[128,256]{1,0:T(8,128)(2,1)S(1)}, bf16[128,256]{1,0:T(8,128)(2,1)}, u32[]{:S(2)}) %copy-start.7) | copy-done | bytes 65560
  39.4 0.0 copy-start.9
  39.4 0.8 %copy-done.9 = bf16[128,256]{1,0:T(8,128)(2,1)S(1)} copy-done((bf16[128,256]{1,0:T(8,128)(2,1)S(1)}, bf16[128,256]{1,0:T(8,128)(2,1)}, u32[]{:S(2)}) %copy-start.9) | copy-done | bytes 65560
  40.2 3.3 %attend.1 = (bf16[192,2048]{1,0:T(8,128)(2,1)}, bf16[192,256]{1,0:T(8,128)(2,1)}, bf16[192,256]{1,0:T(8,128)(2,1)}) custom-call(s32[1]{0:T(128)} %bitcast.me_ref, bf16[784,128]{1,0:T(8,128)(2,1)S(1)} %get-tuple-element.12.rest_0_, bf16[1296,128]{1,0:T(8,128)(2,1)S(1)} %collective-permute-done.4.rest_1_, bf16[784,128]{1,0:T(8,128)(2,1)S(1)} %collective-permute-done.5.rest_2_, ...), custom_call_target="tpu_custom_call" | custom-call | tf_op jit(solution)/shard_map/attend/pallas_call | solution.py:313
Async XLA Ops:
  0.6 10.6 %collective-permute-start = (bf16[128,256]{1,0:T(8,128)(2,1)}, bf16[128,256]{1,0:T(8,128)(2,1)S(1)}, u32[]{:S(2)}, u32[]{:S(2)}) collective-permute-start(bf16[128,256]{1,0:T(8,128)(2,1)} %rest_4_.1), channel_id=1, source_target_pairs={{0,8},{4,12},{8,0},{12,4},{1,9},{5,13},{9,1},{13,5},{2,10},{6,14},... | collective-permute-start | bytes 196616 | tf_op jit(solution)/shard_map/ppermute | solution.py:275
  4.7 6.5 %collective-permute-start.2 = (bf16[128,256]{1,0:T(8,128)(2,1)}, bf16[128,256]{1,0:T(8,128)(2,1)S(1)}, u32[]{:S(2)}, u32[]{:S(2)}) collective-permute-start(bf16[128,256]{1,0:T(8,128)(2,1)} %rest_4_.1), channel_id=1, source_target_pairs={{0,4},{4,0},{8,12},{12,8},{1,5},{5,1},{9,13},{13,9},{2,6},{6,2},{1... | collective-permute-start | bytes 196616 | tf_op jit(solution)/shard_map/ppermute | solution.py:275
  6.3 6.0 %collective-permute-start.1 = (bf16[128,256]{1,0:T(8,128)(2,1)}, bf16[128,256]{1,0:T(8,128)(2,1)S(1)}, u32[]{:S(2)}, u32[]{:S(2)}) collective-permute-start(bf16[128,256]{1,0:T(8,128)(2,1)} %rest_5_.1), channel_id=1, source_target_pairs={{0,8},{4,12},{8,0},{12,4},{1,9},{5,13},{9,1},{13,5},{2,10},{6,14},... | collective-permute-start | bytes 196616 | tf_op jit(solution)/shard_map/ppermute | solution.py:275
  6.6 5.6 %collective-permute-start.3 = (bf16[128,256]{1,0:T(8,128)(2,1)}, bf16[128,256]{1,0:T(8,128)(2,1)S(1)}, u32[]{:S(2)}, u32[]{:S(2)}) collective-permute-start(bf16[128,256]{1,0:T(8,128)(2,1)} %rest_5_.1), channel_id=1, source_target_pairs={{0,4},{4,0},{8,12},{12,8},{1,5},{5,1},{9,13},{13,9},{2,6},{6,2},{1... | collective-permute-start | bytes 196616 | tf_op jit(solution)/shard_map/ppermute | solution.py:275
  6.8 0.7 %copy-start.14 = (s32[128,1]{0,1:T(1,128)S(1)}, s32[128,1]{0,1:T(1,128)}, u32[]{:S(2)}) copy-start(s32[128,1]{0,1:T(1,128)} %param.8) | copy-start | bytes 1540
  6.8 0.7 %copy-start.15 = (s32[128,1]{0,1:T(1,128)S(1)}, s32[128,1]{0,1:T(1,128)}, u32[]{:S(2)}) copy-start(s32[128,1]{0,1:T(1,128)} %param.9) | copy-start | bytes 1540
  7.5 1.0 %copy-start = (bf16[128,2048]{1,0:T(8,128)(2,1)S(1)}, bf16[128,2048]{1,0:T(8,128)(2,1)}, u32[]{:S(2)}) copy-start(bf16[128,2048]{1,0:T(8,128)(2,1)} %q_hbm.1) | copy-start | bytes 1572868
  9.1 0.7 %copy-start.1 = (bf16[1296,128]{1,0:T(8,128)(2,1)}, bf16[1296,128]{1,0:T(8,128)(2,1)S(1)}, u32[]{:S(2)}) copy-start(bf16[1296,128]{1,0:T(8,128)(2,1)S(1)} %get-tuple-element.15.rest_4_) | copy-start | bytes 995332
  9.8 0.7 %copy-start.10 = (bf16[784,128]{1,0:T(8,128)(2,1)}, bf16[784,128]{1,0:T(8,128)(2,1)S(1)}, u32[]{:S(2)}) copy-start(bf16[784,128]{1,0:T(8,128)(2,1)S(1)} %get-tuple-element.13.rest_0_) | copy-start | bytes 602116
  10.5 0.7 %copy-start.11 = (bf16[784,128]{1,0:T(8,128)(2,1)}, bf16[784,128]{1,0:T(8,128)(2,1)S(1)}, u32[]{:S(2)}) copy-start(bf16[784,128]{1,0:T(8,128)(2,1)S(1)} %get-tuple-element.14.rest_1_) | copy-start | bytes 602116
  11.2 1.1 %copy-start.2 = (bf16[128,256]{1,0:T(8,128)(2,1)}, bf16[128,256]{1,0:T(8,128)(2,1)S(1)}, u32[]{:S(2)}) copy-start(bf16[128,256]{1,0:T(8,128)(2,1)S(1)} %collective-permute-done.k_ref.rest_8_) | copy-start | bytes 196612
  11.2 1.1 %copy-start.6 = (bf16[128,256]{1,0:T(8,128)(2,1)}, bf16[128,256]{1,0:T(8,128)(2,1)S(1)}, u32[]{:S(2)}) copy-start(bf16[128,256]{1,0:T(8,128)(2,1)S(1)} %collective-permute-done.2.rest_2_) | copy-start | bytes 196612
  12.3 0.6 %copy-start.4 = (bf16[128,256]{1,0:T(8,128)(2,1)}, bf16[128,256]{1,0:T(8,128)(2,1)S(1)}, u32[]{:S(2)}) copy-start(bf16[128,256]{1,0:T(8,128)(2,1)S(1)} %collective-permute-done.1.v_ref.rest_9_) | copy-start | bytes 196612
  12.3 0.6 %copy-start.8 = (bf16[128,256]{1,0:T(8,128)(2,1)}, bf16[128,256]{1,0:T(8,128)(2,1)S(1)}, u32[]{:S(2)}) copy-start(bf16[128,256]{1,0:T(8,128)(2,1)S(1)} %collective-permute-done.3.rest_3_) | copy-start | bytes 196612
  12.9 23.9 %copy-start.12 = (bf16[128,256]{1,0:T(8,128)(2,1)S(1)}, bf16[128,256]{1,0:T(8,128)(2,1)}, u32[]{:S(2)}) copy-start(bf16[128,256]{1,0:T(8,128)(2,1)} %rest_4_.1) | copy-start | bytes 196612
  12.9 23.9 %copy-start.13 = (bf16[128,256]{1,0:T(8,128)(2,1)S(1)}, bf16[128,256]{1,0:T(8,128)(2,1)}, u32[]{:S(2)}) copy-start(bf16[128,256]{1,0:T(8,128)(2,1)} %rest_5_.1) | copy-start | bytes 196612
  18.0 18.8 %collective-permute-start.4 = (bf16[1296,128]{1,0:T(8,128)(2,1)}, bf16[1296,128]{1,0:T(8,128)(2,1)S(1)}, u32[]{:S(2)}, u32[]{:S(2)}) collective-permute-start(bf16[1296,128]{1,0:T(8,128)(2,1)} %get-tuple-element.16), channel_id=1, source_target_pairs={{0,4},{4,0},{8,12},{12,8},{1,5},{5,1},{9,13},{13,9},{2,6},{6,2},{1... | collective-permute-start | bytes 995336 | tf_op jit(solution)/shard_map/ppermute | solution.py:275
  19.2 17.6 %collective-permute-start.5 = (bf16[784,128]{1,0:T(8,128)(2,1)}, bf16[784,128]{1,0:T(8,128)(2,1)S(1)}, u32[]{:S(2)}, u32[]{:S(2)}) collective-permute-start(bf16[784,128]{1,0:T(8,128)(2,1)} %get-tuple-element.17), channel_id=1, source_target_pairs={{0,8},{4,12},{8,0},{12,4},{1,9},{5,13},{9,1},{13,5},{2,10},{6,14},... | collective-permute-start | bytes 602120 | tf_op jit(solution)/shard_map/ppermute | solution.py:275
  21.5 15.4 %collective-permute-start.6 = (bf16[784,128]{1,0:T(8,128)(2,1)}, bf16[784,128]{1,0:T(8,128)(2,1)S(1)}, u32[]{:S(2)}, u32[]{:S(2)}) collective-permute-start(bf16[784,128]{1,0:T(8,128)(2,1)} %get-tuple-element.18), channel_id=1, source_target_pairs={{0,12},{4,8},{8,4},{12,0},{1,13},{5,9},{9,5},{13,1},{2,14},{6,10},... | collective-permute-start | bytes 602120 | tf_op jit(solution)/shard_map/ppermute | solution.py:275
  36.9 0.8 %copy-start.3 = (bf16[128,256]{1,0:T(8,128)(2,1)S(1)}, bf16[128,256]{1,0:T(8,128)(2,1)}, u32[]{:S(2)}) copy-start(bf16[128,256]{1,0:T(8,128)(2,1)} %copy-done.2) | copy-start | bytes 196612
  37.7 0.8 %copy-start.5 = (bf16[128,256]{1,0:T(8,128)(2,1)S(1)}, bf16[128,256]{1,0:T(8,128)(2,1)}, u32[]{:S(2)}) copy-start(bf16[128,256]{1,0:T(8,128)(2,1)} %copy-done.4) | copy-start | bytes 196612
  38.6 0.8 %copy-start.7 = (bf16[128,256]{1,0:T(8,128)(2,1)S(1)}, bf16[128,256]{1,0:T(8,128)(2,1)}, u32[]{:S(2)}) copy-start(bf16[128,256]{1,0:T(8,128)(2,1)} %get-tuple-element.19.rest_6_) | copy-start | bytes 196612
  39.4 0.8 %copy-start.9 = (bf16[128,256]{1,0:T(8,128)(2,1)S(1)}, bf16[128,256]{1,0:T(8,128)(2,1)}, u32[]{:S(2)}) copy-start(bf16[128,256]{1,0:T(8,128)(2,1)} %get-tuple-element.20.rest_7_) | copy-start | bytes 196612

commit v7 on v2

--- a/solution.py
+++ b/solution.py
@@ -12,6 +12,7 @@
 
 
 neg_big = -1e30
+DISTANCES = (0, 1, 2, 3)
 
 
 def slot_select(owner_list, instances, capacity):
@@ -146,7 +147,8 @@
 
 
 def pack_kernel(instances, capacity, me_ref, q_hbm, qo_ref, co_ref, *rest):
-    sends, (q_ref, arrived) = rest[:instances], rest[instances:]
+    *sends, q_ref, arrived = rest
+    groups = len(sends) // instances
     rows = q_ref.shape[0]
     heads = q_ref.shape[1] // HD
     fetch = pltpu.make_async_copy(q_hbm, q_ref, arrived)
@@ -164,8 +166,9 @@
     lists = jnp.concatenate(
         [owners, co_ref[...], jnp.full((14, rows), -1, jnp.int32)], axis=0
     ).astype(jnp.float32).astype(jnp.bfloat16)
+    per_group = heads // groups
     for k in range(instances):
-        sends[k][heads * capacity :, :] = lists
+        sends[k * groups][per_group * capacity :, :] = lists
     fetch.wait()
     for pair in range(heads // 2):
         packed = jnp.dot(
@@ -175,28 +178,41 @@
         ).astype(jnp.bfloat16)
         for k in range(instances):
             for half in range(2):
-                at = (2 * pair + half) * capacity
-                sends[k][at : at + capacity, :] = packed[
+                g, h = divmod(2 * pair + half, per_group)
+                sends[k * groups + g][h * capacity : (h + 1) * capacity, :] = packed[
                     k * capacity : (k + 1) * capacity, half * HD : (half + 1) * HD
                 ]
 
 
+def join_kernel(k_ref, v_ref, kv_ref):
+    rows = k_ref.shape[0]
+    at = 0
+    for source in (k_ref, v_ref):
+        for g in range(source.shape[1] // HD):
+            kv_ref[at : at + rows, :] = source[:, g * HD : (g + 1) * HD]
+            at += rows
+
+
 def attend_kernel(instances, capacity, heads, heads_kv, me_ref, *rest):
-    got, rest = rest[:instances], rest[instances:]
-    got_k, rest = rest[:instances], rest[instances:]
-    got_v, rest = rest[:instances], rest[instances:]
+    pieces = [(k, g) for g in range(heads_kv) for k in DISTANCES]
+    got, rest = dict(zip(pieces, rest)), rest[len(pieces) :]
+    got_kv, rest = rest[:instances], rest[instances:]
     att_ref, kc_ref, vc_ref, wanted_ref, keys, vals = rest
-    rows = got_k[0].shape[0]
+    rows = HD
     per_group = heads // heads_kv
+    tall = per_group * capacity
     tail = heads * capacity
     me = me_ref[0]
     for k in range(instances):
         source = jnp.bitwise_xor(me, k)
-        wanted_ref[source] = got[k][...]
+        for g in range(heads_kv):
+            wanted_ref[source, g * tall : (g + 1) * tall, :] = got[k, g][:tall, :]
+        wanted_ref[source, tail:, :] = got[k, 0][tall:, :]
         at = pl.ds(pl.multiple_of(source * rows, rows), rows)
         for g in range(heads_kv):
-            keys[g, at, :] = got_k[k][:, g * HD : (g + 1) * HD]
-            vals[g, at, :HD] = got_v[k][:, g * HD : (g + 1) * HD]
+            start = heads_kv * rows
+            keys[g, at, :] = got_kv[k][g * rows : (g + 1) * rows, :]
+            vals[g, at, :HD] = got_kv[k][start + g * rows : start + (g + 1) * rows, :]
         vals[:, k * rows : (k + 1) * rows, HD:] = jnp.ones((heads_kv, rows, HD), jnp.bfloat16)
     lists = jnp.concatenate([wanted_ref[s, tail : tail + 16, :] for s in range(instances)], axis=0)
     wide = (lists.astype(jnp.float32) == me.astype(jnp.float32)).astype(jnp.float32)
@@ -204,7 +220,7 @@
     r = lax.broadcasted_iota(jnp.int32, (rows, 2 * rows), 0)
     u = lax.broadcasted_iota(jnp.int32, (rows, 2 * rows), 1)
     reach = ((u <= r) | (u >= rows)).astype(jnp.bfloat16)
-    scale = 1.0 / math.sqrt(HD)
+    scale = math.log2(math.e) / math.sqrt(HD)
     for s in range(instances):
         q_at, c_at = 16 * s, 16 * s + 1
         cache_pick = picks(wide[c_at : c_at + 1], earlier[c_at : c_at + 1], capacity)
@@ -231,7 +247,7 @@
             last = jnp.where(near, scores[:, s * rows :], neg_big)
             scores = jnp.concatenate([scores[:, : s * rows], last], axis=1) if s else last
             top = jnp.max(scores, axis=1, keepdims=True)
-            weights = jnp.exp((scores - top) * scale).astype(jnp.bfloat16)
+            weights = jnp.exp2(scores * scale - top * scale).astype(jnp.bfloat16)
             mixed = jnp.dot(weights, vals[g, : (s + 1) * rows, :], preferred_element_type=jnp.float32)
             out = jnp.where(valid, mixed[:, :HD] / mixed[:, HD:], 0.0).astype(jnp.bfloat16)
             for h in range(per_group):
@@ -248,28 +264,42 @@
     def swap(array, k):
         return lax.ppermute(array, "seq", [(i, i ^ k) for i in range(instances)])
 
-    all_k, all_v = {0: keys}, {0: values}
-    bit = instances // 2
-    while bit:
-        for k in list(all_k):
-            all_k[k ^ bit] = swap(all_k[k], bit)
-            all_v[k ^ bit] = swap(all_v[k], bit)
-        bit //= 2
-    height = heads * capacity + 16
+    tall = heads // heads_kv * capacity
+    kv_tall = 2 * heads_kv * rows
     vmem = pl.BlockSpec(memory_space=pltpu.VMEM)
     smem = pl.BlockSpec(memory_space=pltpu.SMEM)
+    hbm = pl.BlockSpec(memory_space=pltpu.HBM)
     me = lax.axis_index("seq").astype(jnp.int32).reshape(1)
+    own_kv = pl.pallas_call(
+        join_kernel,
+        out_shape=jax.ShapeDtypeStruct((kv_tall, HD), jnp.bfloat16),
+        in_specs=[vmem] * 2,
+        out_specs=vmem,
+        compiler_params=pltpu.CompilerParams(vmem_limit_bytes=16 << 20),
+        cost_estimate=pl.CostEstimate(flops=0, bytes_accessed=1 << 18, transcendentals=0),
+        name="join",
+    )(keys, values)
+    far_kv, near_kv = swap(own_kv, 2), swap(own_kv, 1)
+    both_kv = swap(far_kv, 1)
     sends = pl.pallas_call(
         functools.partial(pack_kernel, instances, capacity),
-        out_shape=(jax.ShapeDtypeStruct((height, HD), jnp.bfloat16),) * instances,
-        in_specs=[smem, pl.BlockSpec(memory_space=pl.ANY), vmem, vmem],
-        out_specs=(vmem,) * instances,
+        out_shape=tuple(
+            jax.ShapeDtypeStruct((tall + 16 * (g == 0), HD), jnp.bfloat16)
+            for k in range(instances)
+            for g in range(heads_kv)
+        ),
+        in_specs=[smem, hbm, vmem, vmem],
+        out_specs=(vmem,) * (instances * heads_kv),
         scratch_shapes=[pltpu.VMEM(queries.shape, jnp.bfloat16), pltpu.SemaphoreType.DMA],
         compiler_params=pltpu.CompilerParams(vmem_limit_bytes=16 << 20),
         cost_estimate=pl.CostEstimate(flops=1 << 27, bytes_accessed=2 << 20, transcendentals=0),
         name="pack",
     )(me, queries, query_owner.reshape(1, rows), cache_owner.reshape(1, rows))
-    got = [swap(sends[k], k) if k else sends[0] for k in range(instances)]
+    got = []
+    for g in range(heads_kv):
+        for k in DISTANCES:
+            piece = sends[k * heads_kv + g]
+            got.append(swap(piece, k) if k else piece)
     slots = instances * capacity
     return pl.pallas_call(
         functools.partial(attend_kernel, instances, capacity, heads, heads_kv),
@@ -278,21 +308,16 @@
             jax.ShapeDtypeStruct((slots, heads_kv * HD), jnp.bfloat16),
             jax.ShapeDtypeStruct((slots, heads_kv * HD), jnp.bfloat16),
         ),
-        in_specs=[smem] + [vmem] * (3 * instances),
+        in_specs=[smem] + [vmem] * (len(got) + instances),
         out_specs=(vmem, vmem, vmem),
         scratch_shapes=[
-            pltpu.VMEM((instances, height, HD), jnp.bfloat16),
+            pltpu.VMEM((instances, heads * capacity + 16, HD), jnp.bfloat16),
             pltpu.VMEM((heads_kv, instances * rows, HD), jnp.bfloat16),
             pltpu.VMEM((heads_kv, instances * rows, 2 * HD), jnp.bfloat16),
         ],
         compiler_params=pltpu.CompilerParams(vmem_limit_bytes=24 << 20),
         name="attend",
-    )(
-        me,
-        *got,
-        *[all_k[k] for k in range(instances)],
-        *[all_v[k] for k in range(instances)],
-    )
+    )(me, *got, own_kv, near_kv, far_kv, both_kv)
 
 
 def on_device(queries, keys, values, query_owner, cache_owner):
@@ -300,7 +325,7 @@
     rows = queries.shape[0]
     capacity = 3 * rows // (2 * instances)
     heads = queries.shape[1] // HD
-    whole_tiles = capacity % 16 == 0 and rows == HD and heads % 2 == 0 and instances & (instances - 1) == 0
+    whole_tiles = instances == 4 and capacity % 16 == 0 and rows == HD and heads % 2 == 0
     form = few_instances if whole_tiles else many_instances
     return form(queries, keys, values, query_owner, cache_owner)
 

time: 42.5 us -> 34.7 us (0.82)
  waiting for transfers between devices: 20.4 us -> 12.7 us
  starting transfers between devices: 15.6 us -> 13.7 us
  local copies, waits for them, and re-layouts: 1.7 us -> 3.38 us
    ppermute x9, waiting for transfers between devices: 20.4 us -> 12.7 us  [swap(): return lax.ppermute(array, 'seq', [(i, i ^ k) for i in range(instances)])]
    ppermute x9, starting transfers between devices: 15.6 us -> 13.7 us  [swap(): return lax.ppermute(array, 'seq', [(i, i ^ k) for i in range(instances)])]
    unnamed x10, local copies, waits for them, and re-layouts: 1.7 us -> 3.38 us
  transfers between devices with their start and end apart: 9 -> 9, of which waited for: 5 -> 3; matrix products, arithmetic and copies ran while one was open for 0% -> 0% of each run, Pallas kernels for 0% -> 2%
where the time goes in v7:
time: 34.7 us; the launch traced here: 34.4 us
  starting transfers between devices  13.7 us (39%)
  waiting for transfers between devices  12.7 us (37%)
  Pallas kernels  3.94 us (11%)
  local copies, waits for them, and re-layouts  3.38 us (10%)
  between operations  0.67 us (2%)
    ppermute x9, starting transfers between devices, swap(): return lax.ppermute(array, 'seq', [(i, i ^ k) for i in range(instances)])  13.7 us
    ppermute x9, waiting for transfers between devices, swap(): return lax.ppermute(array, 'seq', [(i, i ^ k) for i in range(instances)])  12.7 us
    unnamed x10, local copies, waits for them, and re-layouts  3.38 us
    pallas_call x1, Pallas kernels, few_instances(): pl.pallas_call(functools.partial(attend_kernel, instances, capacity, head...  3.36 us
  transfers between devices with their start and end apart: 9, of which 3 were waited for; matrix products, arithmetic and copies ran while one was open for 0% of the time, Pallas kernels for 2%

profile of v7, /device:TPU:0, one launch (start us, length us, event | category | flops | bytes accessed | tf_op | source)
XLA Modules:
  0.0 34.4 jit_solution(8042522606366078858)
XLA Ops:
  0.6 0.0 copy-start.1
  0.6 0.8 %copy-done.1 = bf16[128,256]{1,0:T(8,128)(2,1)S(1)} copy-done((bf16[128,256]{1,0:T(8,128)(2,1)S(1)}, bf16[128,256]{1,0:T(8,128)(2,1)}, u32[]{:S(2)}) %copy-start.1) | copy-done | bytes 65560
  1.5 0.0 copy-start.2
  1.5 0.8 %copy-done.2 = bf16[128,256]{1,0:T(8,128)(2,1)S(1)} copy-done((bf16[128,256]{1,0:T(8,128)(2,1)S(1)}, bf16[128,256]{1,0:T(8,128)(2,1)}, u32[]{:S(2)}) %copy-start.2) | copy-done | bytes 65560
  2.3 4.1 %collective-permute-start.7 = (bf16[512,128]{1,0:T(8,128)(2,1)S(1)}, bf16[512,128]{1,0:T(8,128)(2,1)S(1)}, u32[]{:S(2)}, u32[]{:S(2)}) collective-permute-start(bf16[512,128]{1,0:T(8,128)(2,1)S(1)} %join.1.rest_8_), channel_id=1, source_target_pairs={{0,8},{4,12},{8,0},{12,4},{1,9},{5,13},{9,1},{13,5},{2,10},{6,14},... | collective-permute-start | bytes 393224 | tf_op jit(solution)/shard_map/ppermute | solution.py:265
  6.4 0.0 copy-start.3
  6.4 0.0 copy-start.4
  6.4 0.7 %copy-done.3 = s32[128,1]{0,1:T(1,128)S(1)} copy-done((s32[128,1]{0,1:T(1,128)S(1)}, s32[128,1]{0,1:T(1,128)}, u32[]{:S(2)}) %copy-start.3) | copy-done | bytes 536
  7.1 0.0 copy-done.4
  7.1 0.0 copy-start
  7.1 1.0 %copy-done = bf16[128,2048]{1,0:T(8,128)(2,1)S(1)} copy-done((bf16[128,2048]{1,0:T(8,128)(2,1)S(1)}, bf16[128,2048]{1,0:T(8,128)(2,1)}, u32[]{:S(2)}) %copy-start) | copy-done | bytes 524312
  8.2 0.5 %pack.1 = (bf16[400,128]{1,0:T(8,128)(2,1)S(1)}, bf16[384,128]{1,0:T(8,128)(2,1)S(1)}, bf16[400,128]{1,0:T(8,128)(2,1)S(1)}, bf16[384,128]{1,0:T(8,128)(2,1)S(1)...) custom-call(s32[1]{0:T(128)} %bitcast.me_ref, ...), custom_call_target="tpu_custom_call" | custom-call | flops 134217728 | bytes 2097152 | tf_op jit(solution)/shard_map/pack/pallas_call | solution.py:284
  8.7 1.6 %collective-permute-start.3 = (bf16[384,128]{1,0:T(8,128)(2,1)S(1)}, bf16[384,128]{1,0:T(8,128)(2,1)S(1)}, u32[]{:S(2)}, u32[]{:S(2)}) collective-permute-start(bf16[384,128]{1,0:T(8,128)(2,1)S(1)} %get-tuple-element.16), channel_id=1, source_target_pairs={{0,4},{4,0},{8,12},{12,8},{1,5},{5,1},{9,13},{13,9},{2,6},{6,2},{1... | collective-permute-start | bytes 294920 | tf_op jit(solution)/shard_map/ppermute | solution.py:265
  10.3 0.3 collective-permute-start.4
  10.7 2.5 %collective-permute-start.5 = (bf16[384,128]{1,0:T(8,128)(2,1)S(1)}, bf16[384,128]{1,0:T(8,128)(2,1)S(1)}, u32[]{:S(2)}, u32[]{:S(2)}) collective-permute-start(bf16[384,128]{1,0:T(8,128)(2,1)S(1)} %get-tuple-element.18), channel_id=1, source_target_pairs={{0,12},{4,8},{8,4},{12,0},{1,13},{5,9},{9,5},{13,1},{2,14},{6,10},... | collective-permute-start | bytes 294920 | tf_op jit(solution)/shard_map/ppermute | solution.py:265
  13.2 0.7 %collective-permute-start.6 = (bf16[512,128]{1,0:T(8,128)(2,1)S(1)}, bf16[512,128]{1,0:T(8,128)(2,1)S(1)}, u32[]{:S(2)}, u32[]{:S(2)}) collective-permute-start(bf16[512,128]{1,0:T(8,128)(2,1)S(1)} %join.1.rest_8_), channel_id=1, source_target_pairs={{0,4},{4,0},{8,12},{12,8},{1,5},{5,1},{9,13},{13,9},{2,6},{6,2},{1... | collective-permute-start | bytes 393224 | tf_op jit(solution)/shard_map/ppermute | solution.py:265
  13.8 0.0 collective-permute-done.7.rest_10_
  13.8 1.4 %collective-permute-start.8 = (bf16[512,128]{1,0:T(8,128)(2,1)S(1)}, bf16[512,128]{1,0:T(8,128)(2,1)S(1)}, u32[]{:S(2)}, u32[]{:S(2)}) collective-permute-start(bf16[512,128]{1,0:T(8,128)(2,1)S(1)} %collective-permute-done.7.rest_10_), channel_id=1, source_target_pairs={{0,4},{4,0},{8,12},{12,8},{1,5},{5,1},{9,13},{13,9},{2,6},{6,2},{1... | collective-permute-start | bytes 393224 | tf_op jit(solution)/shard_map/ppermute | solution.py:265
  15.2 1.2 %collective-permute-done.3.rest_5_ = bf16[384,128]{1,0:T(8,128)(2,1)S(1)} collective-permute-done((bf16[384,128]{1,0:T(8,128)(2,1)S(1)}, bf16[384,128]{1,0:T(8,128)(2,1)S(1)}, u32[]{:S(2)}, u32[]{:S(2)}) %collective-permute-start.3) | collective-permute-done | bytes 98336 | tf_op jit(solution)/shard_map/ppermute | solution.py:265
  16.4 0.0 collective-permute-start
  16.4 3.2 %collective-permute-done.4.rest_6_ = bf16[384,128]{1,0:T(8,128)(2,1)S(1)} collective-permute-done((bf16[384,128]{1,0:T(8,128)(2,1)S(1)}, bf16[384,128]{1,0:T(8,128)(2,1)S(1)}, u32[]{:S(2)}, u32[]{:S(2)}) %collective-permute-start.4) | collective-permute-done | bytes 98336 | tf_op jit(solution)/shard_map/ppermute | solution.py:265
  19.6 0.0 collective-permute-start.1
  19.6 0.0 collective-permute-done.5.rest_7_
  19.6 3.1 %collective-permute-start.2 = (bf16[400,128]{1,0:T(8,128)(2,1)S(1)}, bf16[400,128]{1,0:T(8,128)(2,1)S(1)}, u32[]{:S(2)}, u32[]{:S(2)}) collective-permute-start(bf16[400,128]{1,0:T(8,128)(2,1)S(1)} %get-tuple-element.14), channel_id=1, source_target_pairs={{0,12},{4,8},{8,4},{12,0},{1,13},{5,9},{9,5},{13,1},{2,14},{6,10},... | collective-permute-start | bytes 307208 | tf_op jit(solution)/shard_map/ppermute | solution.py:265
  22.7 8.3 %collective-permute-done.rest_1_ = bf16[400,128]{1,0:T(8,128)(2,1)S(1)} collective-permute-done((bf16[400,128]{1,0:T(8,128)(2,1)S(1)}, bf16[400,128]{1,0:T(8,128)(2,1)S(1)}, u32[]{:S(2)}, u32[]{:S(2)}) %collective-permute-start) | collective-permute-done | bytes 102432 | tf_op jit(solution)/shard_map/ppermute | solution.py:265
  31.0 0.0 collective-permute-done.1.rest_2_
  31.0 0.0 collective-permute-done.2.rest_3_
  31.0 0.0 collective-permute-done.6.rest_9_
  31.0 0.0 collective-permute-done.8.rest_11_
  31.1 3.4 %attend.1 = (bf16[192,2048]{1,0:T(8,128)(2,1)}, bf16[192,256]{1,0:T(8,128)(2,1)}, bf16[192,256]{1,0:T(8,128)(2,1)}) custom-call(s32[1]{0:T(128)} %bitcast.me_ref, bf16[400,128]{1,0:T(8,128)(2,1)S(1)} %get-tuple-element.11.rest_0_, bf16[400,128]{1,0:T(8,128)(2,1)S(1)} %collective-permute-done.rest_1_, bf16[400,128]{1,0:T(8,128)(2,1)S(1)} %collective-permute-done.1.rest_2_, ...), custom_call_target="tpu_custom_call" | custom-call | tf_op jit(solution)/shard_map/attend/pallas_call | solution.py:304
  (1 shorter events, 0.0 us)
Async XLA Ops:
  0.6 0.8 %copy-start.1 = (bf16[128,256]{1,0:T(8,128)(2,1)S(1)}, bf16[128,256]{1,0:T(8,128)(2,1)}, u32[]{:S(2)}) copy-start(bf16[128,256]{1,0:T(8,128)(2,1)} %k_ref.1) | copy-start | bytes 196612
  1.5 0.8 %copy-start.2 = (bf16[128,256]{1,0:T(8,128)(2,1)S(1)}, bf16[128,256]{1,0:T(8,128)(2,1)}, u32[]{:S(2)}) copy-start(bf16[128,256]{1,0:T(8,128)(2,1)} %v_ref.1) | copy-start | bytes 196612
  2.3 11.5 %collective-permute-start.7 = (bf16[512,128]{1,0:T(8,128)(2,1)S(1)}, bf16[512,128]{1,0:T(8,128)(2,1)S(1)}, u32[]{:S(2)}, u32[]{:S(2)}) collective-permute-start(bf16[512,128]{1,0:T(8,128)(2,1)S(1)} %join.1.rest_8_), channel_id=1, source_target_pairs={{0,8},{4,12},{8,0},{12,4},{1,9},{5,13},{9,1},{13,5},{2,10},{6,14},... | collective-permute-start | bytes 393224 | tf_op jit(solution)/shard_map/ppermute | solution.py:265
  6.4 0.7 %copy-start.3 = (s32[128,1]{0,1:T(1,128)S(1)}, s32[128,1]{0,1:T(1,128)}, u32[]{:S(2)}) copy-start(s32[128,1]{0,1:T(1,128)} %param.8) | copy-start | bytes 1540
  6.4 0.7 %copy-start.4 = (s32[128,1]{0,1:T(1,128)S(1)}, s32[128,1]{0,1:T(1,128)}, u32[]{:S(2)}) copy-start(s32[128,1]{0,1:T(1,128)} %param.9) | copy-start | bytes 1540
  7.1 1.0 %copy-start = (bf16[128,2048]{1,0:T(8,128)(2,1)S(1)}, bf16[128,2048]{1,0:T(8,128)(2,1)}, u32[]{:S(2)}) copy-start(bf16[128,2048]{1,0:T(8,128)(2,1)} %q_hbm.1) | copy-start | bytes 1572868
  8.7 7.7 %collective-permute-start.3 = (bf16[384,128]{1,0:T(8,128)(2,1)S(1)}, bf16[384,128]{1,0:T(8,128)(2,1)S(1)}, u32[]{:S(2)}, u32[]{:S(2)}) collective-permute-start(bf16[384,128]{1,0:T(8,128)(2,1)S(1)} %get-tuple-element.16), channel_id=1, source_target_pairs={{0,4},{4,0},{8,12},{12,8},{1,5},{5,1},{9,13},{13,9},{2,6},{6,2},{1... | collective-permute-start | bytes 294920 | tf_op jit(solution)/shard_map/ppermute | solution.py:265
  10.3 9.2 %collective-permute-start.4 = (bf16[384,128]{1,0:T(8,128)(2,1)S(1)}, bf16[384,128]{1,0:T(8,128)(2,1)S(1)}, u32[]{:S(2)}, u32[]{:S(2)}) collective-permute-start(bf16[384,128]{1,0:T(8,128)(2,1)S(1)} %get-tuple-element.17), channel_id=1, source_target_pairs={{0,8},{4,12},{8,0},{12,4},{1,9},{5,13},{9,1},{13,5},{2,10},{6,14},... | collective-permute-start | bytes 294920 | tf_op jit(solution)/shard_map/ppermute | solution.py:265
  10.7 8.9 %collective-permute-start.5 = (bf16[384,128]{1,0:T(8,128)(2,1)S(1)}, bf16[384,128]{1,0:T(8,128)(2,1)S(1)}, u32[]{:S(2)}, u32[]{:S(2)}) collective-permute-start(bf16[384,128]{1,0:T(8,128)(2,1)S(1)} %get-tuple-element.18), channel_id=1, source_target_pairs={{0,12},{4,8},{8,4},{12,0},{1,13},{5,9},{9,5},{13,1},{2,14},{6,10},... | collective-permute-start | bytes 294920 | tf_op jit(solution)/shard_map/ppermute | solution.py:265
  13.2 17.9 %collective-permute-start.6 = (bf16[512,128]{1,0:T(8,128)(2,1)S(1)}, bf16[512,128]{1,0:T(8,128)(2,1)S(1)}, u32[]{:S(2)}, u32[]{:S(2)}) collective-permute-start(bf16[512,128]{1,0:T(8,128)(2,1)S(1)} %join.1.rest_8_), channel_id=1, source_target_pairs={{0,4},{4,0},{8,12},{12,8},{1,5},{5,1},{9,13},{13,9},{2,6},{6,2},{1... | collective-permute-start | bytes 393224 | tf_op jit(solution)/shard_map/ppermute | solution.py:265
  13.8 17.2 %collective-permute-start.8 = (bf16[512,128]{1,0:T(8,128)(2,1)S(1)}, bf16[512,128]{1,0:T(8,128)(2,1)S(1)}, u32[]{:S(2)}, u32[]{:S(2)}) collective-permute-start(bf16[512,128]{1,0:T(8,128)(2,1)S(1)} %collective-permute-done.7.rest_10_), channel_id=1, source_target_pairs={{0,4},{4,0},{8,12},{12,8},{1,5},{5,1},{9,13},{13,9},{2,6},{6,2},{1... | collective-permute-start | bytes 393224 | tf_op jit(solution)/shard_map/ppermute | solution.py:265
  16.4 14.6 %collective-permute-start = (bf16[400,128]{1,0:T(8,128)(2,1)S(1)}, bf16[400,128]{1,0:T(8,128)(2,1)S(1)}, u32[]{:S(2)}, u32[]{:S(2)}) collective-permute-start(bf16[400,128]{1,0:T(8,128)(2,1)S(1)} %get-tuple-element.12), channel_id=1, source_target_pairs={{0,4},{4,0},{8,12},{12,8},{1,5},{5,1},{9,13},{13,9},{2,6},{6,2},{1... | collective-permute-start | bytes 307208 | tf_op jit(solution)/shard_map/ppermute | solution.py:265
  19.6 11.5 %collective-permute-start.1 = (bf16[400,128]{1,0:T(8,128)(2,1)S(1)}, bf16[400,128]{1,0:T(8,128)(2,1)S(1)}, u32[]{:S(2)}, u32[]{:S(2)}) collective-permute-start(bf16[400,128]{1,0:T(8,128)(2,1)S(1)} %get-tuple-element.13), channel_id=1, source_target_pairs={{0,8},{4,12},{8,0},{12,4},{1,9},{5,13},{9,1},{13,5},{2,10},{6,14},... | collective-permute-start | bytes 307208 | tf_op jit(solution)/shard_map/ppermute | solution.py:265
  19.6 11.4 %collective-permute-start.2 = (bf16[400,128]{1,0:T(8,128)(2,1)S(1)}, bf16[400,128]{1,0:T(8,128)(2,1)S(1)}, u32[]{:S(2)}, u32[]{:S(2)}) collective-permute-start(bf16[400,128]{1,0:T(8,128)(2,1)S(1)} %get-tuple-element.14), channel_id=1, source_target_pairs={{0,12},{4,8},{8,4},{12,0},{1,13},{5,9},{9,5},{13,1},{2,14},{6,10},... | collective-permute-start | bytes 307208 | tf_op jit(solution)/shard_map/ppermute | solution.py:265

commit v8 on v2

--- a/solution.py
+++ b/solution.py
@@ -145,8 +145,9 @@
     return (chosen == slot).astype(jnp.bfloat16)
 
 
-def pack_kernel(instances, capacity, me_ref, q_hbm, qo_ref, co_ref, *rest):
-    sends, (q_ref, arrived) = rest[:instances], rest[instances:]
+def pack_kernel(instances, capacity, me_ref, q_hbm, kv_ref, qo_ref, co_ref, *rest):
+    lead, rest = rest[:instances], rest[instances:]
+    sends, (q_ref, arrived) = (lead, rest[:instances]), rest[instances:]
     rows = q_ref.shape[0]
     heads = q_ref.shape[1] // HD
     fetch = pltpu.make_async_copy(q_hbm, q_ref, arrived)
@@ -164,8 +165,13 @@
     lists = jnp.concatenate(
         [owners, co_ref[...], jnp.full((14, rows), -1, jnp.int32)], axis=0
     ).astype(jnp.float32).astype(jnp.bfloat16)
+    per_group = heads // 2
+    tall = per_group * capacity
     for k in range(instances):
-        sends[k][heads * capacity :, :] = lists
+        lead[k][tall : tall + 16, :] = lists
+    for block in range(kv_ref.shape[1] // HD):
+        at = tall + 16 + block * rows
+        lead[1][at : at + rows, :] = kv_ref[:, block * HD : (block + 1) * HD]
     fetch.wait()
     for pair in range(heads // 2):
         packed = jnp.dot(
@@ -175,124 +181,183 @@
         ).astype(jnp.bfloat16)
         for k in range(instances):
             for half in range(2):
-                at = (2 * pair + half) * capacity
-                sends[k][at : at + capacity, :] = packed[
+                g, h = divmod(2 * pair + half, per_group)
+                sends[g][k][h * capacity : (h + 1) * capacity, :] = packed[
                     k * capacity : (k + 1) * capacity, half * HD : (half + 1) * HD
                 ]
 
 
-def attend_kernel(instances, capacity, heads, heads_kv, me_ref, *rest):
+def attend_head(instances, capacity, per_group, wanted_ref, keys, vals, allowed_ref, store):
+    rows = HD
+    tall = per_group * capacity
+    scale = math.log2(math.e) / math.sqrt(HD)
+    for s in reversed(range(instances)):
+        slots = slice(s * capacity, (s + 1) * capacity)
+        allowed = allowed_ref[slots, :].astype(jnp.float32)
+        near = jnp.concatenate([allowed[:, :rows]] * per_group, axis=0) > 0.5
+        valid = jnp.concatenate([allowed[:, rows:]] * per_group, axis=0) > 0.5
+        scores = lax.dot_general(
+            wanted_ref[s, :tall, :],
+            keys[: (s + 1) * rows, :],
+            (((1,), (1,)), ((), ())),
+            preferred_element_type=jnp.float32,
+        )
+        last = jnp.where(near, scores[:, s * rows :], neg_big)
+        scores = jnp.concatenate([scores[:, : s * rows], last], axis=1) if s else last
+        top = jnp.max(scores, axis=1, keepdims=True)
+        weights = jnp.exp2(scores * scale - top * scale).astype(jnp.bfloat16)
+        mixed = jnp.dot(weights, vals[: (s + 1) * rows, :], preferred_element_type=jnp.float32)
+        out = jnp.where(valid, mixed[:, :HD] / mixed[:, HD:], 0.0).astype(jnp.bfloat16)
+        for h in range(per_group):
+            store(s, slots, h, out[h * capacity : (h + 1) * capacity, :])
+
+
+def lead_kernel(instances, capacity, per_group, me_ref, *rest):
     got, rest = rest[:instances], rest[instances:]
-    got_k, rest = rest[:instances], rest[instances:]
-    got_v, rest = rest[:instances], rest[instances:]
-    att_ref, kc_ref, vc_ref, wanted_ref, keys, vals = rest
-    rows = got_k[0].shape[0]
-    per_group = heads // heads_kv
-    tail = heads * capacity
+    own, far, both, half_ref, allowed_ref, keys_ref, vals_ref, kc_ref, vc_ref = rest[:9]
+    wanted_ref, keys, vals = rest[9:]
+    rows = HD
+    tall = per_group * capacity
     me = me_ref[0]
+    direct = {0: own, 2: far, 3: both}
+    ones = jnp.ones((rows, HD), jnp.bfloat16)
     for k in range(instances):
         source = jnp.bitwise_xor(me, k)
-        wanted_ref[source] = got[k][...]
+        wanted_ref[source] = got[k][: tall + 16, :]
         at = pl.ds(pl.multiple_of(source * rows, rows), rows)
-        for g in range(heads_kv):
-            keys[g, at, :] = got_k[k][:, g * HD : (g + 1) * HD]
-            vals[g, at, :HD] = got_v[k][:, g * HD : (g + 1) * HD]
-        vals[:, k * rows : (k + 1) * rows, HD:] = jnp.ones((heads_kv, rows, HD), jnp.bfloat16)
-    lists = jnp.concatenate([wanted_ref[s, tail : tail + 16, :] for s in range(instances)], axis=0)
+        blocks = []
+        for block in range(4):
+            if k in direct:
+                blocks.append(direct[k][:, block * HD : (block + 1) * HD])
+            else:
+                start = tall + 16 + block * rows
+                blocks.append(got[k][start : start + rows, :])
+        keys[at, :] = blocks[0]
+        keys_ref[at, :] = blocks[1]
+        vals[at, :HD] = blocks[2]
+        vals_ref[at, :HD] = blocks[3]
+        vals[k * rows : (k + 1) * rows, HD:] = ones
+        vals_ref[k * rows : (k + 1) * rows, HD:] = ones
+    lists = jnp.concatenate([wanted_ref[s, tall : tall + 16, :] for s in range(instances)], axis=0)
     wide = (lists.astype(jnp.float32) == me.astype(jnp.float32)).astype(jnp.float32)
     earlier = jnp.dot(wide.astype(jnp.bfloat16), before(rows), preferred_element_type=jnp.float32)
     r = lax.broadcasted_iota(jnp.int32, (rows, 2 * rows), 0)
     u = lax.broadcasted_iota(jnp.int32, (rows, 2 * rows), 1)
     reach = ((u <= r) | (u >= rows)).astype(jnp.bfloat16)
-    scale = 1.0 / math.sqrt(HD)
     for s in range(instances):
         q_at, c_at = 16 * s, 16 * s + 1
         cache_pick = picks(wide[c_at : c_at + 1], earlier[c_at : c_at + 1], capacity)
         query_pick = picks(wide[q_at : q_at + 1], earlier[q_at : q_at + 1], capacity)
         slots = slice(s * capacity, (s + 1) * capacity)
         block = slice(s * rows, (s + 1) * rows)
-        for g in range(heads_kv):
+        for g, (k_ref, v_ref) in enumerate(((keys, vals), (keys_ref, vals_ref))):
             columns = slice(g * HD, (g + 1) * HD)
-            both = jnp.concatenate([keys[g, block, :], vals[g, block, :HD]], axis=1)
-            cached = jnp.dot(cache_pick, both, preferred_element_type=jnp.float32).astype(jnp.bfloat16)
+            pair = jnp.concatenate([k_ref[block, :], v_ref[block, :HD]], axis=1)
+            cached = jnp.dot(cache_pick, pair, preferred_element_type=jnp.float32).astype(jnp.bfloat16)
             kc_ref[slots, columns] = cached[:, :HD]
             vc_ref[slots, columns] = cached[:, HD:]
-        allowed = jnp.dot(query_pick, reach, preferred_element_type=jnp.float32)
-        near = jnp.concatenate([allowed[:, :rows]] * per_group, axis=0) > 0.5
-        valid = jnp.concatenate([allowed[:, rows:]] * per_group, axis=0) > 0.5
-        for g in range(heads_kv):
-            wanted = wanted_ref[s, g * per_group * capacity : (g + 1) * per_group * capacity, :]
-            scores = lax.dot_general(
-                wanted,
-                keys[g, : (s + 1) * rows, :],
-                (((1,), (1,)), ((), ())),
-                preferred_element_type=jnp.float32,
+        allowed_ref[slots, :] = jnp.dot(query_pick, reach, preferred_element_type=jnp.float32).astype(
+            jnp.bfloat16
+        )
+
+    def store(s, slots, h, value):
+        half_ref[slots, h * HD : (h + 1) * HD] = value
+
+    attend_head(instances, capacity, per_group, wanted_ref, keys, vals, allowed_ref, store)
+
+
+def rest_kernel(instances, capacity, per_group, me_ref, *rest):
+    got, rest = rest[:instances], rest[instances:]
+    half_ref, allowed_ref, keys_ref, vals_ref, att_hbm, wanted_ref, mine_ref, sent = rest
+    width = per_group * HD
+    early = pltpu.make_async_copy(half_ref, att_hbm.at[:, :width], sent.at[instances])
+    early.start()
+    for k in range(instances):
+        wanted_ref[jnp.bitwise_xor(me_ref[0], k)] = got[k][...]
+    copies = []
+
+    def store(s, slots, h, value):
+        mine_ref[slots, h * HD : (h + 1) * HD] = value
+        if h == per_group - 1:
+            copy = pltpu.make_async_copy(
+                mine_ref.at[slots, :], att_hbm.at[slots, width:], sent.at[s]
             )
-            last = jnp.where(near, scores[:, s * rows :], neg_big)
-            scores = jnp.concatenate([scores[:, : s * rows], last], axis=1) if s else last
-            top = jnp.max(scores, axis=1, keepdims=True)
-            weights = jnp.exp((scores - top) * scale).astype(jnp.bfloat16)
-            mixed = jnp.dot(weights, vals[g, : (s + 1) * rows, :], preferred_element_type=jnp.float32)
-            out = jnp.where(valid, mixed[:, :HD] / mixed[:, HD:], 0.0).astype(jnp.bfloat16)
-            for h in range(per_group):
-                column = (g * per_group + h) * HD
-                att_ref[slots, column : column + HD] = out[h * capacity : (h + 1) * capacity, :]
+            copy.start()
+            copies.append(copy)
+
+    attend_head(instances, capacity, per_group, wanted_ref, keys_ref, vals_ref, allowed_ref, store)
+    for copy in [early, *copies]:
+        copy.wait()
 
 
 def few_instances(queries, keys, values, query_owner, cache_owner):
     instances = lax.axis_size("seq")
     rows = queries.shape[0]
     capacity = 3 * rows // (2 * instances)
-    heads, heads_kv = queries.shape[1] // HD, keys.shape[1] // HD
+    heads = queries.shape[1] // HD
+    per_group = heads // 2
+    tall = per_group * capacity
+    slots = instances * capacity
 
     def swap(array, k):
         return lax.ppermute(array, "seq", [(i, i ^ k) for i in range(instances)])
 
-    all_k, all_v = {0: keys}, {0: values}
-    bit = instances // 2
-    while bit:
-        for k in list(all_k):
-            all_k[k ^ bit] = swap(all_k[k], bit)
-            all_v[k ^ bit] = swap(all_v[k], bit)
-        bit //= 2
-    height = heads * capacity + 16
     vmem = pl.BlockSpec(memory_space=pltpu.VMEM)
     smem = pl.BlockSpec(memory_space=pltpu.SMEM)
+    hbm = pl.BlockSpec(memory_space=pltpu.HBM)
+    shape = lambda *dims: jax.ShapeDtypeStruct(dims, jnp.bfloat16)
     me = lax.axis_index("seq").astype(jnp.int32).reshape(1)
+    own_kv = jnp.concatenate([keys, values], axis=1)
+    far_kv = swap(own_kv, 2)
+    both_kv = swap(far_kv, 1)
     sends = pl.pallas_call(
         functools.partial(pack_kernel, instances, capacity),
-        out_shape=(jax.ShapeDtypeStruct((height, HD), jnp.bfloat16),) * instances,
-        in_specs=[smem, pl.BlockSpec(memory_space=pl.ANY), vmem, vmem],
-        out_specs=(vmem,) * instances,
+        out_shape=tuple(shape(tall + 16 + 4 * rows * (k == 1), HD) for k in range(instances))
+        + (shape(tall, HD),) * instances,
+        in_specs=[smem, hbm, vmem, vmem, vmem],
+        out_specs=(vmem,) * (2 * instances),
         scratch_shapes=[pltpu.VMEM(queries.shape, jnp.bfloat16), pltpu.SemaphoreType.DMA],
         compiler_params=pltpu.CompilerParams(vmem_limit_bytes=16 << 20),
         cost_estimate=pl.CostEstimate(flops=1 << 27, bytes_accessed=2 << 20, transcendentals=0),
         name="pack",
-    )(me, queries, query_owner.reshape(1, rows), cache_owner.reshape(1, rows))
-    got = [swap(sends[k], k) if k else sends[0] for k in range(instances)]
-    slots = instances * capacity
-    return pl.pallas_call(
-        functools.partial(attend_kernel, instances, capacity, heads, heads_kv),
+    )(me, queries, own_kv, query_owner.reshape(1, rows), cache_owner.reshape(1, rows))
+    got = [swap(piece, i % instances) if i % instances else piece for i, piece in enumerate(sends)]
+    half, allowed, keys_rest, vals_rest, key_cache, value_cache = pl.pallas_call(
+        functools.partial(lead_kernel, instances, capacity, per_group),
         out_shape=(
-            jax.ShapeDtypeStruct((slots, heads * HD), jnp.bfloat16),
-            jax.ShapeDtypeStruct((slots, heads_kv * HD), jnp.bfloat16),
-            jax.ShapeDtypeStruct((slots, heads_kv * HD), jnp.bfloat16),
+            shape(slots, per_group * HD),
+            shape(slots, 2 * rows),
+            shape(instances * rows, HD),
+            shape(instances * rows, 2 * HD),
+            shape(slots, 2 * HD),
+            shape(slots, 2 * HD),
         ),
-        in_specs=[smem] + [vmem] * (3 * instances),
-        out_specs=(vmem, vmem, vmem),
+        in_specs=[smem] + [vmem] * (instances + 3),
+        out_specs=(vmem,) * 6,
         scratch_shapes=[
-            pltpu.VMEM((instances, height, HD), jnp.bfloat16),
-            pltpu.VMEM((heads_kv, instances * rows, HD), jnp.bfloat16),
-            pltpu.VMEM((heads_kv, instances * rows, 2 * HD), jnp.bfloat16),
+            pltpu.VMEM((instances, tall + 16, HD), jnp.bfloat16),
+            pltpu.VMEM((instances * rows, HD), jnp.bfloat16),
+            pltpu.VMEM((instances * rows, 2 * HD), jnp.bfloat16),
         ],
         compiler_params=pltpu.CompilerParams(vmem_limit_bytes=24 << 20),
-        name="attend",
-    )(
-        me,
-        *got,
-        *[all_k[k] for k in range(instances)],
-        *[all_v[k] for k in range(instances)],
-    )
+        cost_estimate=pl.CostEstimate(flops=1 << 29, bytes_accessed=2 << 20, transcendentals=1 << 19),
+        name="attend_lead",
+    )(me, *got[:instances], own_kv, far_kv, both_kv)
+    attended = pl.pallas_call(
+        functools.partial(rest_kernel, instances, capacity, per_group),
+        out_shape=shape(slots, heads * HD),
+        in_specs=[smem] + [vmem] * (instances + 4),
+        out_specs=hbm,
+        scratch_shapes=[
+            pltpu.VMEM((instances, tall, HD), jnp.bfloat16),
+            pltpu.VMEM((slots, per_group * HD), jnp.bfloat16),
+            pltpu.SemaphoreType.DMA((instances + 1,)),
+        ],
+        compiler_params=pltpu.CompilerParams(vmem_limit_bytes=24 << 20),
+        cost_estimate=pl.CostEstimate(flops=1 << 29, bytes_accessed=2 << 20, transcendentals=1 << 19),
+        name="attend_rest",
+    )(me, *got[instances:], half, allowed, keys_rest, vals_rest)
+    return (attended, key_cache, value_cache)
 
 
 def on_device(queries, keys, values, query_owner, cache_owner):
@@ -300,7 +365,13 @@
     rows = queries.shape[0]
     capacity = 3 * rows // (2 * instances)
     heads = queries.shape[1] // HD
-    whole_tiles = capacity % 16 == 0 and rows == HD and heads % 2 == 0 and instances & (instances - 1) == 0
+    whole_tiles = (
+        instances == 4
+        and capacity % 16 == 0
+        and rows == HD
+        and keys.shape[1] == 2 * HD
+        and heads % 4 == 0
+    )
     form = few_instances if whole_tiles else many_instances
     return form(queries, keys, values, query_owner, cache_owner)
 

time: 42.5 us -> 32.4 us (0.76)
  waiting for transfers between devices: 20.4 us -> 10.1 us
  local copies, waits for them, and re-layouts: 1.7 us -> 2.6 us
  starting transfers between devices: 15.6 us -> 14.9 us
    ppermute x9 -> x8, waiting for transfers between devices: 20.4 us -> 10.1 us  [swap(): return lax.ppermute(array, 'seq', [(i, i ^ k) for i in range(instances)])]
    unnamed x10 -> x9, local copies, waits for them, and re-layouts: 1.7 us -> 2.59 us
    ppermute x9 -> x8, starting transfers between devices: 15.6 us -> 14.9 us  [swap(): return lax.ppermute(array, 'seq', [(i, i ^ k) for i in range(instances)])]
    pallas_call x1 -> x2, Pallas kernels: 3.37 us -> 3.28 us  [the longest x1 1.85 us: few_instances(): pl.pallas_call(functools.partial(rest_kernel, instances, capacity, per_gr...]
  transfers between devices with their start and end apart: 9 -> 8, of which waited for: 5 -> 4; matrix products, arithmetic and copies ran while one was open for 0% -> 0% of each run, Pallas kernels for 0% -> 6%
where the time goes in v8:
time: 32.4 us; the launch traced here: 32.2 us
  starting transfers between devices  14.9 us (46%)
  waiting for transfers between devices  10.1 us (31%)
  Pallas kernels  3.82 us (12%)
  local copies, waits for them, and re-layouts  2.6 us (8%)
  between operations  0.67 us (2%)
    ppermute x8, starting transfers between devices, swap(): return lax.ppermute(array, 'seq', [(i, i ^ k) for i in range(instances)])  14.9 us
    ppermute x8, waiting for transfers between devices, swap(): return lax.ppermute(array, 'seq', [(i, i ^ k) for i in range(instances)])  10.1 us
    unnamed x9, local copies, waits for them, and re-layouts  2.59 us
    pallas_call x1, Pallas kernels, few_instances(): pl.pallas_call(functools.partial(rest_kernel, instances, capacity, per_gr...  1.85 us
    pallas_call x1, Pallas kernels, few_instances(): pl.pallas_call(functools.partial(lead_kernel, instances, capacity, per_gr...  1.43 us
  transfers between devices with their start and end apart: 8, of which 4 were waited for; matrix products, arithmetic and copies ran while one was open for 0% of the time, Pallas kernels for 6%

profile of v8, /device:TPU:0, one launch (start us, length us, event | category | flops | bytes accessed | tf_op | source)
XLA Modules:
  0.0 32.2 jit_solution(3921532900115726608)
XLA Ops:
  0.6 0.0 copy-start.3
  0.6 0.9 %constant_dynamic-update-slice_fusion.1 = bf16[128,512]{1,0:T(8,128)(2,1)S(1)} fusion(bf16[128,256]{1,0:T(8,128)(2,1)} %param.6), kind=kLoop, calls=%fused_computation.1 | loop fusion | bytes 131072
  1.5 0.0 copy-done.3
  1.5 4.1 %collective-permute-start.6 = (bf16[128,512]{1,0:T(8,128)(2,1)S(1)}, bf16[128,512]{1,0:T(8,128)(2,1)S(1)}, u32[]{:S(2)}, u32[]{:S(2)}) collective-permute-start(bf16[128,512]{1,0:T(8,128)(2,1)S(1)} %constant_dynamic-update-slice_fusion.kv_ref.rest_4_), channel_id=1, source_target_pairs={{0,8},{4,12},{8,0},{12,4},{1,9},{5,13},{9,1},{13,5},{2,10},{6,14},... | collective-permute-start | bytes 393224 | tf_op jit(solution)/shard_map/ppermute | solution.py:303
  5.6 0.0 copy-start.1
  5.6 0.0 copy-start.2
  5.6 0.7 %copy-done.1 = s32[128,1]{0,1:T(1,128)S(1)} copy-done((s32[128,1]{0,1:T(1,128)S(1)}, s32[128,1]{0,1:T(1,128)}, u32[]{:S(2)}) %copy-start.1) | copy-done | bytes 536
  6.3 0.0 copy-done.2
  6.3 0.0 copy-start
  6.3 1.0 %copy-done = bf16[128,2048]{1,0:T(8,128)(2,1)S(1)} copy-done((bf16[128,2048]{1,0:T(8,128)(2,1)S(1)}, bf16[128,2048]{1,0:T(8,128)(2,1)}, u32[]{:S(2)}) %copy-start) | copy-done | bytes 524312
  7.3 0.5 %pack.1 = (bf16[400,128]{1,0:T(8,128)(2,1)S(1)}, bf16[912,128]{1,0:T(8,128)(2,1)S(1)}, bf16[400,128]{1,0:T(8,128)(2,1)S(1)}, bf16[400,128]{1,0:T(8,128)(2,1)S(1)...) custom-call(s32[1]{0:T(128)} %bitcast.me_ref, ...), custom_call_target="tpu_custom_call" | custom-call | flops 134217728 | bytes 2097152 | tf_op jit(solution)/shard_map/pack/pallas_call | solution.py:313
  7.9 1.6 %collective-permute-start.3 = (bf16[912,128]{1,0:T(8,128)(2,1)S(1)}, bf16[912,128]{1,0:T(8,128)(2,1)S(1)}, u32[]{:S(2)}, u32[]{:S(2)}) collective-permute-start(bf16[912,128]{1,0:T(8,128)(2,1)S(1)} %get-tuple-element.22), channel_id=1, source_target_pairs={{0,4},{4,0},{8,12},{12,8},{1,5},{5,1},{9,13},{13,9},{2,6},{6,2},{1... | collective-permute-start | bytes 700424 | tf_op jit(solution)/shard_map/ppermute | solution.py:303
  9.5 0.3 %collective-permute-start.4 = (bf16[400,128]{1,0:T(8,128)(2,1)S(1)}, bf16[400,128]{1,0:T(8,128)(2,1)S(1)}, u32[]{:S(2)}, u32[]{:S(2)}) collective-permute-start(bf16[400,128]{1,0:T(8,128)(2,1)S(1)} %get-tuple-element.23), channel_id=1, source_target_pairs={{0,8},{4,12},{8,0},{12,4},{1,9},{5,13},{9,1},{13,5},{2,10},{6,14},... | collective-permute-start | bytes 307208 | tf_op jit(solution)/shard_map/ppermute | solution.py:303
  9.9 2.5 %collective-permute-start.5 = (bf16[400,128]{1,0:T(8,128)(2,1)S(1)}, bf16[400,128]{1,0:T(8,128)(2,1)S(1)}, u32[]{:S(2)}, u32[]{:S(2)}) collective-permute-start(bf16[400,128]{1,0:T(8,128)(2,1)S(1)} %get-tuple-element.24), channel_id=1, source_target_pairs={{0,12},{4,8},{8,4},{12,0},{1,13},{5,9},{9,5},{13,1},{2,14},{6,10},... | collective-permute-start | bytes 307208 | tf_op jit(solution)/shard_map/ppermute | solution.py:303
  12.3 0.0 collective-permute-done.6.rest_5_
  12.4 0.7 %collective-permute-start.7 = (bf16[128,512]{1,0:T(8,128)(2,1)S(1)}, bf16[128,512]{1,0:T(8,128)(2,1)S(1)}, u32[]{:S(2)}, u32[]{:S(2)}) collective-permute-start(bf16[128,512]{1,0:T(8,128)(2,1)S(1)} %collective-permute-done.6.rest_5_), channel_id=1, source_target_pairs={{0,4},{4,0},{8,12},{12,8},{1,5},{5,1},{9,13},{13,9},{2,6},{6,2},{1... | collective-permute-start | bytes 393224 | tf_op jit(solution)/shard_map/ppermute | solution.py:303
  13.0 1.3 %collective-permute-start = (bf16[384,128]{1,0:T(8,128)(2,1)S(1)}, bf16[384,128]{1,0:T(8,128)(2,1)S(1)}, u32[]{:S(2)}, u32[]{:S(2)}) collective-permute-start(bf16[384,128]{1,0:T(8,128)(2,1)S(1)} %get-tuple-element.18), channel_id=1, source_target_pairs={{0,4},{4,0},{8,12},{12,8},{1,5},{5,1},{9,13},{13,9},{2,6},{6,2},{1... | collective-permute-start | bytes 294920 | tf_op jit(solution)/shard_map/ppermute | solution.py:303
  14.4 5.7 %collective-permute-done.4.rest_2_ = bf16[400,128]{1,0:T(8,128)(2,1)S(1)} collective-permute-done((bf16[400,128]{1,0:T(8,128)(2,1)S(1)}, bf16[400,128]{1,0:T(8,128)(2,1)S(1)}, u32[]{:S(2)}, u32[]{:S(2)}) %collective-permute-start.4) | collective-permute-done | bytes 102432 | tf_op jit(solution)/shard_map/ppermute | solution.py:303
  20.1 1.2 %collective-permute-start.1 = (bf16[384,128]{1,0:T(8,128)(2,1)S(1)}, bf16[384,128]{1,0:T(8,128)(2,1)S(1)}, u32[]{:S(2)}, u32[]{:S(2)}) collective-permute-start(bf16[384,128]{1,0:T(8,128)(2,1)S(1)} %get-tuple-element.19), channel_id=1, source_target_pairs={{0,8},{4,12},{8,0},{12,4},{1,9},{5,13},{9,1},{13,5},{2,10},{6,14},... | collective-permute-start | bytes 294920 | tf_op jit(solution)/shard_map/ppermute | solution.py:303
  21.3 0.0 collective-permute-done.5.rest_3_
  21.3 3.1 %collective-permute-start.2 = (bf16[384,128]{1,0:T(8,128)(2,1)S(1)}, bf16[384,128]{1,0:T(8,128)(2,1)S(1)}, u32[]{:S(2)}, u32[]{:S(2)}) collective-permute-start(bf16[384,128]{1,0:T(8,128)(2,1)S(1)} %get-tuple-element.20), channel_id=1, source_target_pairs={{0,12},{4,8},{8,4},{12,0},{1,13},{5,9},{9,5},{13,1},{2,14},{6,10},... | collective-permute-start | bytes 294920 | tf_op jit(solution)/shard_map/ppermute | solution.py:303
  24.4 0.0 collective-permute-done.3.rest_1_
  24.4 1.1 %collective-permute-done.7.rest_6_ = bf16[128,512]{1,0:T(8,128)(2,1)S(1)} collective-permute-done((bf16[128,512]{1,0:T(8,128)(2,1)S(1)}, bf16[128,512]{1,0:T(8,128)(2,1)S(1)}, u32[]{:S(2)}, u32[]{:S(2)}) %collective-permute-start.7) | collective-permute-done | bytes 131104 | tf_op jit(solution)/shard_map/ppermute | solution.py:303
  25.5 1.4 %attend_lead.1 = (bf16[192,1024]{1,0:T(8,128)(2,1)S(1)}, bf16[192,256]{1,0:T(8,128)(2,1)S(1)}, bf16[512,128]{1,0:T(8,128)(2,1)S(1)}, bf16[512,256]{1,0:T(8,128)(...) custom-call(s32[1]{0:T(128)} %bitcast.me_ref, bf16[400,128]{1,0:T(8,128)(2,1)S(1)} %get-tuple-element.21.rest_0_, ...), custom_call_target="tpu_custom_call" | custom-call | flops 536870912 | bytes 2097152 | tf_op jit(solution)/shard_map/attend_lead/pallas_call | solution.py:325
  27.0 2.9 %collective-permute-done.rest_1_ = bf16[384,128]{1,0:T(8,128)(2,1)S(1)} collective-permute-done((bf16[384,128]{1,0:T(8,128)(2,1)S(1)}, bf16[384,128]{1,0:T(8,128)(2,1)S(1)}, u32[]{:S(2)}, u32[]{:S(2)}) %collective-permute-start) | collective-permute-done | bytes 98336 | tf_op jit(solution)/shard_map/ppermute | solution.py:303
  29.9 0.4 %collective-permute-done.1.rest_2_ = bf16[384,128]{1,0:T(8,128)(2,1)S(1)} collective-permute-done((bf16[384,128]{1,0:T(8,128)(2,1)S(1)}, bf16[384,128]{1,0:T(8,128)(2,1)S(1)}, u32[]{:S(2)}, u32[]{:S(2)}) %collective-permute-start.1) | collective-permute-done | bytes 98336 | tf_op jit(solution)/shard_map/ppermute | solution.py:303
  30.3 0.0 collective-permute-done.2.rest_3_
  30.3 1.8 %attend_rest.1 = bf16[192,2048]{1,0:T(8,128)(2,1)} custom-call(s32[1]{0:T(128)} %bitcast.me_ref, bf16[384,128]{1,0:T(8,128)(2,1)S(1)} %get-tuple-element.17.rest_0_, bf16[384,128]{1,0:T(8,128)(2,1)S(1)} %collective-permute-done.rest_1_, bf16[384,128]{1,0:T(8,128)(2,1)S(1)} %collective-permute-done.1.rest_2_, ...), custom_call_target="tpu_custom_call" | custom-call | flops 536870912 | bytes 2097152 | tf_op jit(solution)/shard_map/attend_rest/pallas_call | solution.py:346
  (1 shorter events, 0.0 us)
Async XLA Ops:
  0.6 0.9 %copy-start.3 = (bf16[128,256]{1,0:T(8,128)(2,1)S(1)}, bf16[128,256]{1,0:T(8,128)(2,1)}, u32[]{:S(2)}) copy-start(bf16[128,256]{1,0:T(8,128)(2,1)} %param.7) | copy-start | bytes 196612
  1.5 10.8 %collective-permute-start.6 = (bf16[128,512]{1,0:T(8,128)(2,1)S(1)}, bf16[128,512]{1,0:T(8,128)(2,1)S(1)}, u32[]{:S(2)}, u32[]{:S(2)}) collective-permute-start(bf16[128,512]{1,0:T(8,128)(2,1)S(1)} %constant_dynamic-update-slice_fusion.kv_ref.rest_4_), channel_id=1, source_target_pairs={{0,8},{4,12},{8,0},{12,4},{1,9},{5,13},{9,1},{13,5},{2,10},{6,14},... | collective-permute-start | bytes 393224 | tf_op jit(solution)/shard_map/ppermute | solution.py:303
  5.6 0.7 %copy-start.1 = (s32[128,1]{0,1:T(1,128)S(1)}, s32[128,1]{0,1:T(1,128)}, u32[]{:S(2)}) copy-start(s32[128,1]{0,1:T(1,128)} %param.8) | copy-start | bytes 1540
  5.6 0.7 %copy-start.2 = (s32[128,1]{0,1:T(1,128)S(1)}, s32[128,1]{0,1:T(1,128)}, u32[]{:S(2)}) copy-start(s32[128,1]{0,1:T(1,128)} %param.9) | copy-start | bytes 1540
  6.3 1.0 %copy-start = (bf16[128,2048]{1,0:T(8,128)(2,1)S(1)}, bf16[128,2048]{1,0:T(8,128)(2,1)}, u32[]{:S(2)}) copy-start(bf16[128,2048]{1,0:T(8,128)(2,1)} %q_hbm.1) | copy-start | bytes 1572868
  7.9 16.5 %collective-permute-start.3 = (bf16[912,128]{1,0:T(8,128)(2,1)S(1)}, bf16[912,128]{1,0:T(8,128)(2,1)S(1)}, u32[]{:S(2)}, u32[]{:S(2)}) collective-permute-start(bf16[912,128]{1,0:T(8,128)(2,1)S(1)} %get-tuple-element.22), channel_id=1, source_target_pairs={{0,4},{4,0},{8,12},{12,8},{1,5},{5,1},{9,13},{13,9},{2,6},{6,2},{1... | collective-permute-start | bytes 700424 | tf_op jit(solution)/shard_map/ppermute | solution.py:303
  9.5 10.5 %collective-permute-start.4 = (bf16[400,128]{1,0:T(8,128)(2,1)S(1)}, bf16[400,128]{1,0:T(8,128)(2,1)S(1)}, u32[]{:S(2)}, u32[]{:S(2)}) collective-permute-start(bf16[400,128]{1,0:T(8,128)(2,1)S(1)} %get-tuple-element.23), channel_id=1, source_target_pairs={{0,8},{4,12},{8,0},{12,4},{1,9},{5,13},{9,1},{13,5},{2,10},{6,14},... | collective-permute-start | bytes 307208 | tf_op jit(solution)/shard_map/ppermute | solution.py:303
  9.9 11.4 %collective-permute-start.5 = (bf16[400,128]{1,0:T(8,128)(2,1)S(1)}, bf16[400,128]{1,0:T(8,128)(2,1)S(1)}, u32[]{:S(2)}, u32[]{:S(2)}) collective-permute-start(bf16[400,128]{1,0:T(8,128)(2,1)S(1)} %get-tuple-element.24), channel_id=1, source_target_pairs={{0,12},{4,8},{8,4},{12,0},{1,13},{5,9},{9,5},{13,1},{2,14},{6,10},... | collective-permute-start | bytes 307208 | tf_op jit(solution)/shard_map/ppermute | solution.py:303
  12.4 13.2 %collective-permute-start.7 = (bf16[128,512]{1,0:T(8,128)(2,1)S(1)}, bf16[128,512]{1,0:T(8,128)(2,1)S(1)}, u32[]{:S(2)}, u32[]{:S(2)}) collective-permute-start(bf16[128,512]{1,0:T(8,128)(2,1)S(1)} %collective-permute-done.6.rest_5_), channel_id=1, source_target_pairs={{0,4},{4,0},{8,12},{12,8},{1,5},{5,1},{9,13},{13,9},{2,6},{6,2},{1... | collective-permute-start | bytes 393224 | tf_op jit(solution)/shard_map/ppermute | solution.py:303
  13.0 16.9 %collective-permute-start = (bf16[384,128]{1,0:T(8,128)(2,1)S(1)}, bf16[384,128]{1,0:T(8,128)(2,1)S(1)}, u32[]{:S(2)}, u32[]{:S(2)}) collective-permute-start(bf16[384,128]{1,0:T(8,128)(2,1)S(1)} %get-tuple-element.18), channel_id=1, source_target_pairs={{0,4},{4,0},{8,12},{12,8},{1,5},{5,1},{9,13},{13,9},{2,6},{6,2},{1... | collective-permute-start | bytes 294920 | tf_op jit(solution)/shard_map/ppermute | solution.py:303
  20.1 10.2 %collective-permute-start.1 = (bf16[384,128]{1,0:T(8,128)(2,1)S(1)}, bf16[384,128]{1,0:T(8,128)(2,1)S(1)}, u32[]{:S(2)}, u32[]{:S(2)}) collective-permute-start(bf16[384,128]{1,0:T(8,128)(2,1)S(1)} %get-tuple-element.19), channel_id=1, source_target_pairs={{0,8},{4,12},{8,0},{12,4},{1,9},{5,13},{9,1},{13,5},{2,10},{6,14},... | collective-permute-start | bytes 294920 | tf_op jit(solution)/shard_map/ppermute | solution.py:303
  21.3 9.0 %collective-permute-start.2 = (bf16[384,128]{1,0:T(8,128)(2,1)S(1)}, bf16[384,128]{1,0:T(8,128)(2,1)S(1)}, u32[]{:S(2)}, u32[]{:S(2)}) collective-permute-start(bf16[384,128]{1,0:T(8,128)(2,1)S(1)} %get-tuple-element.20), channel_id=1, source_target_pairs={{0,12},{4,8},{8,4},{12,0},{1,13},{5,9},{9,5},{13,1},{2,14},{6,10},... | collective-permute-start | bytes 294920 | tf_op jit(solution)/shard_map/ppermute | solution.py:303

commit v9 on v8

--- a/solution.py
+++ b/solution.py
@@ -12,6 +12,7 @@
 
 
 neg_big = -1e30
+SECOND = (0, 2, 3, 1)
 
 
 def slot_select(owner_list, instances, capacity):
@@ -147,7 +148,8 @@
 
 def pack_kernel(instances, capacity, me_ref, q_hbm, kv_ref, qo_ref, co_ref, *rest):
     lead, rest = rest[:instances], rest[instances:]
-    sends, (q_ref, arrived) = (lead, rest[:instances]), rest[instances:]
+    second, (q_ref, arrived) = dict(zip(SECOND, rest)), rest[instances:]
+    sends = (lead, second)
     rows = q_ref.shape[0]
     heads = q_ref.shape[1] // HD
     fetch = pltpu.make_async_copy(q_hbm, q_ref, arrived)
@@ -272,8 +274,8 @@
     width = per_group * HD
     early = pltpu.make_async_copy(half_ref, att_hbm.at[:, :width], sent.at[instances])
     early.start()
-    for k in range(instances):
-        wanted_ref[jnp.bitwise_xor(me_ref[0], k)] = got[k][...]
+    for k, piece in zip(SECOND, got):
+        wanted_ref[jnp.bitwise_xor(me_ref[0], k)] = piece[...]
     copies = []
 
     def store(s, slots, h, value):
@@ -321,7 +323,8 @@
         cost_estimate=pl.CostEstimate(flops=1 << 27, bytes_accessed=2 << 20, transcendentals=0),
         name="pack",
     )(me, queries, own_kv, query_owner.reshape(1, rows), cache_owner.reshape(1, rows))
-    got = [swap(piece, i % instances) if i % instances else piece for i, piece in enumerate(sends)]
+    distances = (*range(instances), *SECOND)
+    got = [swap(piece, k) if k else piece for k, piece in zip(distances, sends)]
     half, allowed, keys_rest, vals_rest, key_cache, value_cache = pl.pallas_call(
         functools.partial(lead_kernel, instances, capacity, per_group),
         out_shape=(

time: 32.4 us -> 32.3 us (level)
  waiting for transfers between devices: 10.1 us -> 9.29 us
  starting transfers between devices: 14.9 us -> 15.7 us
    ppermute x8, waiting for transfers between devices: 10.1 us -> 9.29 us  [swap(): return lax.ppermute(array, 'seq', [(i, i ^ k) for i in range(instances)])]
    ppermute x8, starting transfers between devices: 14.9 us -> 15.7 us  [swap(): return lax.ppermute(array, 'seq', [(i, i ^ k) for i in range(instances)])]
where the time goes in v9:
time: 32.3 us; the launch traced here: 32.1 us
  starting transfers between devices  15.7 us (49%)
  waiting for transfers between devices  9.29 us (29%)
  Pallas kernels  3.82 us (12%)
  local copies, waits for them, and re-layouts  2.6 us (8%)
  between operations  0.68 us (2%)
    ppermute x8, starting transfers between devices, swap(): return lax.ppermute(array, 'seq', [(i, i ^ k) for i in range(instances)])  15.7 us
    ppermute x8, waiting for transfers between devices, swap(): return lax.ppermute(array, 'seq', [(i, i ^ k) for i in range(instances)])  9.29 us
    unnamed x9, local copies, waits for them, and re-layouts  2.59 us
    pallas_call x1, Pallas kernels, few_instances(): pl.pallas_call(functools.partial(rest_kernel, instances, capacity, per_gr...  1.85 us
    pallas_call x1, Pallas kernels, few_instances(): pl.pallas_call(functools.partial(lead_kernel, instances, capacity, per_gr...  1.43 us
  transfers between devices with their start and end apart: 8, of which 4 were waited for; matrix products, arithmetic and copies ran while one was open for 0% of the time, Pallas kernels for 6%

profile of v9, /device:TPU:0, one launch (start us, length us, event | category | flops | bytes accessed | tf_op | source)
XLA Modules:
  0.0 32.1 jit_solution(15562867495617700072)
XLA Ops:
  0.6 0.0 copy-start.3
  0.6 0.9 %constant_dynamic-update-slice_fusion.1 = bf16[128,512]{1,0:T(8,128)(2,1)S(1)} fusion(bf16[128,256]{1,0:T(8,128)(2,1)} %param.6), kind=kLoop, calls=%fused_computation.1 | loop fusion | bytes 131072
  1.5 0.0 copy-done.3
  1.5 4.1 %collective-permute-start.6 = (bf16[128,512]{1,0:T(8,128)(2,1)S(1)}, bf16[128,512]{1,0:T(8,128)(2,1)S(1)}, u32[]{:S(2)}, u32[]{:S(2)}) collective-permute-start(bf16[128,512]{1,0:T(8,128)(2,1)S(1)} %constant_dynamic-update-slice_fusion.kv_ref.rest_4_), channel_id=1, source_target_pairs={{0,8},{4,12},{8,0},{12,4},{1,9},{5,13},{9,1},{13,5},{2,10},{6,14},... | collective-permute-start | bytes 393224 | tf_op jit(solution)/shard_map/ppermute | solution.py:305
  5.6 0.0 copy-start.1
  5.6 0.0 copy-start.2
  5.6 0.7 %copy-done.1 = s32[128,1]{0,1:T(1,128)S(1)} copy-done((s32[128,1]{0,1:T(1,128)S(1)}, s32[128,1]{0,1:T(1,128)}, u32[]{:S(2)}) %copy-start.1) | copy-done | bytes 536
  6.3 0.0 copy-done.2
  6.3 0.0 copy-start
  6.3 1.0 %copy-done = bf16[128,2048]{1,0:T(8,128)(2,1)S(1)} copy-done((bf16[128,2048]{1,0:T(8,128)(2,1)S(1)}, bf16[128,2048]{1,0:T(8,128)(2,1)}, u32[]{:S(2)}) %copy-start) | copy-done | bytes 524312
  7.3 0.5 %pack.1 = (bf16[400,128]{1,0:T(8,128)(2,1)S(1)}, bf16[912,128]{1,0:T(8,128)(2,1)S(1)}, bf16[400,128]{1,0:T(8,128)(2,1)S(1)}, bf16[400,128]{1,0:T(8,128)(2,1)S(1)...) custom-call(s32[1]{0:T(128)} %bitcast.me_ref, ...), custom_call_target="tpu_custom_call" | custom-call | flops 134217728 | bytes 2097152 | tf_op jit(solution)/shard_map/pack/pallas_call | solution.py:315
  7.9 1.6 %collective-permute-start.3 = (bf16[912,128]{1,0:T(8,128)(2,1)S(1)}, bf16[912,128]{1,0:T(8,128)(2,1)S(1)}, u32[]{:S(2)}, u32[]{:S(2)}) collective-permute-start(bf16[912,128]{1,0:T(8,128)(2,1)S(1)} %get-tuple-element.22), channel_id=1, source_target_pairs={{0,4},{4,0},{8,12},{12,8},{1,5},{5,1},{9,13},{13,9},{2,6},{6,2},{1... | collective-permute-start | bytes 700424 | tf_op jit(solution)/shard_map/ppermute | solution.py:305
  9.5 0.3 %collective-permute-start.4 = (bf16[400,128]{1,0:T(8,128)(2,1)S(1)}, bf16[400,128]{1,0:T(8,128)(2,1)S(1)}, u32[]{:S(2)}, u32[]{:S(2)}) collective-permute-start(bf16[400,128]{1,0:T(8,128)(2,1)S(1)} %get-tuple-element.23), channel_id=1, source_target_pairs={{0,8},{4,12},{8,0},{12,4},{1,9},{5,13},{9,1},{13,5},{2,10},{6,14},... | collective-permute-start | bytes 307208 | tf_op jit(solution)/shard_map/ppermute | solution.py:305
  9.9 2.5 %collective-permute-start.5 = (bf16[400,128]{1,0:T(8,128)(2,1)S(1)}, bf16[400,128]{1,0:T(8,128)(2,1)S(1)}, u32[]{:S(2)}, u32[]{:S(2)}) collective-permute-start(bf16[400,128]{1,0:T(8,128)(2,1)S(1)} %get-tuple-element.24), channel_id=1, source_target_pairs={{0,12},{4,8},{8,4},{12,0},{1,13},{5,9},{9,5},{13,1},{2,14},{6,10},... | collective-permute-start | bytes 307208 | tf_op jit(solution)/shard_map/ppermute | solution.py:305
  12.3 0.0 collective-permute-done.6.rest_5_
  12.4 0.7 %collective-permute-start.7 = (bf16[128,512]{1,0:T(8,128)(2,1)S(1)}, bf16[128,512]{1,0:T(8,128)(2,1)S(1)}, u32[]{:S(2)}, u32[]{:S(2)}) collective-permute-start(bf16[128,512]{1,0:T(8,128)(2,1)S(1)} %collective-permute-done.6.rest_5_), channel_id=1, source_target_pairs={{0,4},{4,0},{8,12},{12,8},{1,5},{5,1},{9,13},{13,9},{2,6},{6,2},{1... | collective-permute-start | bytes 393224 | tf_op jit(solution)/shard_map/ppermute | solution.py:305
  13.0 3.2 %collective-permute-start = (bf16[384,128]{1,0:T(8,128)(2,1)S(1)}, bf16[384,128]{1,0:T(8,128)(2,1)S(1)}, u32[]{:S(2)}, u32[]{:S(2)}) collective-permute-start(bf16[384,128]{1,0:T(8,128)(2,1)S(1)} %get-tuple-element.18), channel_id=1, source_target_pairs={{0,8},{4,12},{8,0},{12,4},{1,9},{5,13},{9,1},{13,5},{2,10},{6,14},... | collective-permute-start | bytes 294920 | tf_op jit(solution)/shard_map/ppermute | solution.py:305
  16.2 3.8 %collective-permute-done.4.rest_2_ = bf16[400,128]{1,0:T(8,128)(2,1)S(1)} collective-permute-done((bf16[400,128]{1,0:T(8,128)(2,1)S(1)}, bf16[400,128]{1,0:T(8,128)(2,1)S(1)}, u32[]{:S(2)}, u32[]{:S(2)}) %collective-permute-start.4) | collective-permute-done | bytes 102432 | tf_op jit(solution)/shard_map/ppermute | solution.py:305
  20.1 0.0 collective-permute-start.1
  20.1 0.4 %collective-permute-done.5.rest_3_ = bf16[400,128]{1,0:T(8,128)(2,1)S(1)} collective-permute-done((bf16[400,128]{1,0:T(8,128)(2,1)S(1)}, bf16[400,128]{1,0:T(8,128)(2,1)S(1)}, u32[]{:S(2)}, u32[]{:S(2)}) %collective-permute-start.5) | collective-permute-done | bytes 102432 | tf_op jit(solution)/shard_map/ppermute | solution.py:305
  20.4 3.2 %collective-permute-start.2 = (bf16[384,128]{1,0:T(8,128)(2,1)S(1)}, bf16[384,128]{1,0:T(8,128)(2,1)S(1)}, u32[]{:S(2)}, u32[]{:S(2)}) collective-permute-start(bf16[384,128]{1,0:T(8,128)(2,1)S(1)} %get-tuple-element.20), channel_id=1, source_target_pairs={{0,4},{4,0},{8,12},{12,8},{1,5},{5,1},{9,13},{13,9},{2,6},{6,2},{1... | collective-permute-start | bytes 294920 | tf_op jit(solution)/shard_map/ppermute | solution.py:305
  23.7 0.0 collective-permute-done.3.rest_1_
  23.7 4.5 %collective-permute-done.7.rest_6_ = bf16[128,512]{1,0:T(8,128)(2,1)S(1)} collective-permute-done((bf16[128,512]{1,0:T(8,128)(2,1)S(1)}, bf16[128,512]{1,0:T(8,128)(2,1)S(1)}, u32[]{:S(2)}, u32[]{:S(2)}) %collective-permute-start.7) | collective-permute-done | bytes 131104 | tf_op jit(solution)/shard_map/ppermute | solution.py:305
  28.1 1.4 %attend_lead.1 = (bf16[192,1024]{1,0:T(8,128)(2,1)S(1)}, bf16[192,256]{1,0:T(8,128)(2,1)S(1)}, bf16[512,128]{1,0:T(8,128)(2,1)S(1)}, bf16[512,256]{1,0:T(8,128)(...) custom-call(s32[1]{0:T(128)} %bitcast.me_ref, bf16[400,128]{1,0:T(8,128)(2,1)S(1)} %get-tuple-element.21.rest_0_, ...), custom_call_target="tpu_custom_call" | custom-call | flops 536870912 | bytes 2097152 | tf_op jit(solution)/shard_map/attend_lead/pallas_call | solution.py:328
  29.6 0.0 collective-permute-done.rest_1_
  29.6 0.0 collective-permute-done.1.rest_2_
  29.6 0.6 %collective-permute-done.2.rest_3_ = bf16[384,128]{1,0:T(8,128)(2,1)S(1)} collective-permute-done((bf16[384,128]{1,0:T(8,128)(2,1)S(1)}, bf16[384,128]{1,0:T(8,128)(2,1)S(1)}, u32[]{:S(2)}, u32[]{:S(2)}) %collective-permute-start.2) | collective-permute-done | bytes 98336 | tf_op jit(solution)/shard_map/ppermute | solution.py:305
  30.2 1.8 %attend_rest.1 = bf16[192,2048]{1,0:T(8,128)(2,1)} custom-call(s32[1]{0:T(128)} %bitcast.me_ref, bf16[384,128]{1,0:T(8,128)(2,1)S(1)} %get-tuple-element.17.rest_0_, bf16[384,128]{1,0:T(8,128)(2,1)S(1)} %collective-permute-done.rest_1_, bf16[384,128]{1,0:T(8,128)(2,1)S(1)} %collective-permute-done.1.rest_2_, ...), custom_call_target="tpu_custom_call" | custom-call | flops 536870912 | bytes 2097152 | tf_op jit(solution)/shard_map/attend_rest/pallas_call | solution.py:349
  (1 shorter events, 0.0 us)
Async XLA Ops:
  0.6 0.9 %copy-start.3 = (bf16[128,256]{1,0:T(8,128)(2,1)S(1)}, bf16[128,256]{1,0:T(8,128)(2,1)}, u32[]{:S(2)}) copy-start(bf16[128,256]{1,0:T(8,128)(2,1)} %param.7) | copy-start | bytes 196612
  1.5 10.8 %collective-permute-start.6 = (bf16[128,512]{1,0:T(8,128)(2,1)S(1)}, bf16[128,512]{1,0:T(8,128)(2,1)S(1)}, u32[]{:S(2)}, u32[]{:S(2)}) collective-permute-start(bf16[128,512]{1,0:T(8,128)(2,1)S(1)} %constant_dynamic-update-slice_fusion.kv_ref.rest_4_), channel_id=1, source_target_pairs={{0,8},{4,12},{8,0},{12,4},{1,9},{5,13},{9,1},{13,5},{2,10},{6,14},... | collective-permute-start | bytes 393224 | tf_op jit(solution)/shard_map/ppermute | solution.py:305
  5.6 0.7 %copy-start.1 = (s32[128,1]{0,1:T(1,128)S(1)}, s32[128,1]{0,1:T(1,128)}, u32[]{:S(2)}) copy-start(s32[128,1]{0,1:T(1,128)} %param.8) | copy-start | bytes 1540
  5.6 0.7 %copy-start.2 = (s32[128,1]{0,1:T(1,128)S(1)}, s32[128,1]{0,1:T(1,128)}, u32[]{:S(2)}) copy-start(s32[128,1]{0,1:T(1,128)} %param.9) | copy-start | bytes 1540
  6.3 1.0 %copy-start = (bf16[128,2048]{1,0:T(8,128)(2,1)S(1)}, bf16[128,2048]{1,0:T(8,128)(2,1)}, u32[]{:S(2)}) copy-start(bf16[128,2048]{1,0:T(8,128)(2,1)} %q_hbm.1) | copy-start | bytes 1572868
  7.9 15.8 %collective-permute-start.3 = (bf16[912,128]{1,0:T(8,128)(2,1)S(1)}, bf16[912,128]{1,0:T(8,128)(2,1)S(1)}, u32[]{:S(2)}, u32[]{:S(2)}) collective-permute-start(bf16[912,128]{1,0:T(8,128)(2,1)S(1)} %get-tuple-element.22), channel_id=1, source_target_pairs={{0,4},{4,0},{8,12},{12,8},{1,5},{5,1},{9,13},{13,9},{2,6},{6,2},{1... | collective-permute-start | bytes 700424 | tf_op jit(solution)/shard_map/ppermute | solution.py:305
  9.5 10.5 %collective-permute-start.4 = (bf16[400,128]{1,0:T(8,128)(2,1)S(1)}, bf16[400,128]{1,0:T(8,128)(2,1)S(1)}, u32[]{:S(2)}, u32[]{:S(2)}) collective-permute-start(bf16[400,128]{1,0:T(8,128)(2,1)S(1)} %get-tuple-element.23), channel_id=1, source_target_pairs={{0,8},{4,12},{8,0},{12,4},{1,9},{5,13},{9,1},{13,5},{2,10},{6,14},... | collective-permute-start | bytes 307208 | tf_op jit(solution)/shard_map/ppermute | solution.py:305
  9.9 10.6 %collective-permute-start.5 = (bf16[400,128]{1,0:T(8,128)(2,1)S(1)}, bf16[400,128]{1,0:T(8,128)(2,1)S(1)}, u32[]{:S(2)}, u32[]{:S(2)}) collective-permute-start(bf16[400,128]{1,0:T(8,128)(2,1)S(1)} %get-tuple-element.24), channel_id=1, source_target_pairs={{0,12},{4,8},{8,4},{12,0},{1,13},{5,9},{9,5},{13,1},{2,14},{6,10},... | collective-permute-start | bytes 307208 | tf_op jit(solution)/shard_map/ppermute | solution.py:305
  12.4 15.8 %collective-permute-start.7 = (bf16[128,512]{1,0:T(8,128)(2,1)S(1)}, bf16[128,512]{1,0:T(8,128)(2,1)S(1)}, u32[]{:S(2)}, u32[]{:S(2)}) collective-permute-start(bf16[128,512]{1,0:T(8,128)(2,1)S(1)} %collective-permute-done.6.rest_5_), channel_id=1, source_target_pairs={{0,4},{4,0},{8,12},{12,8},{1,5},{5,1},{9,13},{13,9},{2,6},{6,2},{1... | collective-permute-start | bytes 393224 | tf_op jit(solution)/shard_map/ppermute | solution.py:305
  13.0 16.6 %collective-permute-start = (bf16[384,128]{1,0:T(8,128)(2,1)S(1)}, bf16[384,128]{1,0:T(8,128)(2,1)S(1)}, u32[]{:S(2)}, u32[]{:S(2)}) collective-permute-start(bf16[384,128]{1,0:T(8,128)(2,1)S(1)} %get-tuple-element.18), channel_id=1, source_target_pairs={{0,8},{4,12},{8,0},{12,4},{1,9},{5,13},{9,1},{13,5},{2,10},{6,14},... | collective-permute-start | bytes 294920 | tf_op jit(solution)/shard_map/ppermute | solution.py:305
  20.1 9.5 %collective-permute-start.1 = (bf16[384,128]{1,0:T(8,128)(2,1)S(1)}, bf16[384,128]{1,0:T(8,128)(2,1)S(1)}, u32[]{:S(2)}, u32[]{:S(2)}) collective-permute-start(bf16[384,128]{1,0:T(8,128)(2,1)S(1)} %get-tuple-element.19), channel_id=1, source_target_pairs={{0,12},{4,8},{8,4},{12,0},{1,13},{5,9},{9,5},{13,1},{2,14},{6,10},... | collective-permute-start | bytes 294920 | tf_op jit(solution)/shard_map/ppermute | solution.py:305
  20.4 9.8 %collective-permute-start.2 = (bf16[384,128]{1,0:T(8,128)(2,1)S(1)}, bf16[384,128]{1,0:T(8,128)(2,1)S(1)}, u32[]{:S(2)}, u32[]{:S(2)}) collective-permute-start(bf16[384,128]{1,0:T(8,128)(2,1)S(1)} %get-tuple-element.20), channel_id=1, source_target_pairs={{0,4},{4,0},{8,12},{12,8},{1,5},{5,1},{9,13},{13,9},{2,6},{6,2},{1... | collective-permute-start | bytes 294920 | tf_op jit(solution)/shard_map/ppermute | solution.py:305

commit v10 on v8

--- a/solution.py
+++ b/solution.py
@@ -12,6 +12,7 @@
 
 
 neg_big = -1e30
+SECOND = (2, 3)
 
 
 def slot_select(owner_list, instances, capacity):
@@ -145,9 +146,13 @@
     return (chosen == slot).astype(jnp.bfloat16)
 
 
-def pack_kernel(instances, capacity, me_ref, q_hbm, kv_ref, qo_ref, co_ref, *rest):
+def gate_kernel(near_ref, slots_ref, through_ref):
+    pass
+
+
+def pack_kernel(instances, capacity, me_ref, q_hbm, qo_ref, co_ref, *rest):
     lead, rest = rest[:instances], rest[instances:]
-    sends, (q_ref, arrived) = (lead, rest[:instances]), rest[instances:]
+    second, (q_ref, arrived) = dict(zip(SECOND, rest)), rest[len(SECOND) :]
     rows = q_ref.shape[0]
     heads = q_ref.shape[1] // HD
     fetch = pltpu.make_async_copy(q_hbm, q_ref, arrived)
@@ -169,9 +174,6 @@
     tall = per_group * capacity
     for k in range(instances):
         lead[k][tall : tall + 16, :] = lists
-    for block in range(kv_ref.shape[1] // HD):
-        at = tall + 16 + block * rows
-        lead[1][at : at + rows, :] = kv_ref[:, block * HD : (block + 1) * HD]
     fetch.wait()
     for pair in range(heads // 2):
         packed = jnp.dot(
@@ -182,7 +184,9 @@
         for k in range(instances):
             for half in range(2):
                 g, h = divmod(2 * pair + half, per_group)
-                sends[g][k][h * capacity : (h + 1) * capacity, :] = packed[
+                at = h * capacity + (tall + 16) * (g == 1 and k not in second)
+                ref = second[k] if g == 1 and k in second else lead[k]
+                ref[at : at + capacity, :] = packed[
                     k * capacity : (k + 1) * capacity, half * HD : (half + 1) * HD
                 ]
 
@@ -214,24 +218,17 @@
 
 def lead_kernel(instances, capacity, per_group, me_ref, *rest):
     got, rest = rest[:instances], rest[instances:]
-    own, far, both, half_ref, allowed_ref, keys_ref, vals_ref, kc_ref, vc_ref = rest[:9]
-    wanted_ref, keys, vals = rest[9:]
+    blocks_of, rest = rest[:instances], rest[instances:]
+    half_ref, allowed_ref, keys_ref, vals_ref, kc_ref, vc_ref, wanted_ref, keys, vals = rest
     rows = HD
     tall = per_group * capacity
     me = me_ref[0]
-    direct = {0: own, 2: far, 3: both}
     ones = jnp.ones((rows, HD), jnp.bfloat16)
     for k in range(instances):
         source = jnp.bitwise_xor(me, k)
         wanted_ref[source] = got[k][: tall + 16, :]
         at = pl.ds(pl.multiple_of(source * rows, rows), rows)
-        blocks = []
-        for block in range(4):
-            if k in direct:
-                blocks.append(direct[k][:, block * HD : (block + 1) * HD])
-            else:
-                start = tall + 16 + block * rows
-                blocks.append(got[k][start : start + rows, :])
+        blocks = [blocks_of[k][:, block * HD : (block + 1) * HD] for block in range(4)]
         keys[at, :] = blocks[0]
         keys_ref[at, :] = blocks[1]
         vals[at, :HD] = blocks[2]
@@ -272,8 +269,10 @@
     width = per_group * HD
     early = pltpu.make_async_copy(half_ref, att_hbm.at[:, :width], sent.at[instances])
     early.start()
-    for k in range(instances):
-        wanted_ref[jnp.bitwise_xor(me_ref[0], k)] = got[k][...]
+    tall = per_group * capacity
+    for k, piece in zip((0, 1, *SECOND), got):
+        start = 0 if k in SECOND else tall + 16
+        wanted_ref[jnp.bitwise_xor(me_ref[0], k)] = piece[start : start + tall, :]
     copies = []
 
     def store(s, slots, h, value):
@@ -308,20 +307,35 @@
     shape = lambda *dims: jax.ShapeDtypeStruct(dims, jnp.bfloat16)
     me = lax.axis_index("seq").astype(jnp.int32).reshape(1)
     own_kv = jnp.concatenate([keys, values], axis=1)
-    far_kv = swap(own_kv, 2)
+    far_kv, near_kv = swap(own_kv, 2), swap(own_kv, 1)
     both_kv = swap(far_kv, 1)
+    distances = (*range(instances), *SECOND)
     sends = pl.pallas_call(
         functools.partial(pack_kernel, instances, capacity),
-        out_shape=tuple(shape(tall + 16 + 4 * rows * (k == 1), HD) for k in range(instances))
-        + (shape(tall, HD),) * instances,
-        in_specs=[smem, hbm, vmem, vmem, vmem],
-        out_specs=(vmem,) * (2 * instances),
+        out_shape=tuple(
+            shape(tall + 16 + tall * (k not in SECOND), HD) for k in range(instances)
+        )
+        + (shape(tall, HD),) * len(SECOND),
+        in_specs=[smem, hbm, vmem, vmem],
+        out_specs=(vmem,) * len(distances),
         scratch_shapes=[pltpu.VMEM(queries.shape, jnp.bfloat16), pltpu.SemaphoreType.DMA],
         compiler_params=pltpu.CompilerParams(vmem_limit_bytes=16 << 20),
         cost_estimate=pl.CostEstimate(flops=1 << 27, bytes_accessed=2 << 20, transcendentals=0),
         name="pack",
-    )(me, queries, own_kv, query_owner.reshape(1, rows), cache_owner.reshape(1, rows))
-    got = [swap(piece, i % instances) if i % instances else piece for i, piece in enumerate(sends)]
+    )(me, queries, query_owner.reshape(1, rows), cache_owner.reshape(1, rows))
+    anyspace = pl.BlockSpec(memory_space=pl.ANY)
+    beside = pl.pallas_call(
+        gate_kernel,
+        out_shape=shape(*sends[1].shape),
+        in_specs=[anyspace] * 2,
+        out_specs=anyspace,
+        input_output_aliases={1: 0},
+        compiler_params=pltpu.CompilerParams(vmem_limit_bytes=16 << 20),
+        cost_estimate=pl.CostEstimate(flops=0, bytes_accessed=0, transcendentals=0),
+        name="gate",
+    )(near_kv, sends[1])
+    sends = [sends[0], beside, *sends[2:]]
+    got = [swap(piece, k) if k else piece for k, piece in zip(distances, sends)]
     half, allowed, keys_rest, vals_rest, key_cache, value_cache = pl.pallas_call(
         functools.partial(lead_kernel, instances, capacity, per_group),
         out_shape=(
@@ -332,7 +346,7 @@
             shape(slots, 2 * HD),
             shape(slots, 2 * HD),
         ),
-        in_specs=[smem] + [vmem] * (instances + 3),
+        in_specs=[smem] + [vmem] * (2 * instances),
         out_specs=(vmem,) * 6,
         scratch_shapes=[
             pltpu.VMEM((instances, tall + 16, HD), jnp.bfloat16),
@@ -342,7 +356,7 @@
         compiler_params=pltpu.CompilerParams(vmem_limit_bytes=24 << 20),
         cost_estimate=pl.CostEstimate(flops=1 << 29, bytes_accessed=2 << 20, transcendentals=1 << 19),
         name="attend_lead",
-    )(me, *got[:instances], own_kv, far_kv, both_kv)
+    )(me, *got[:instances], own_kv, near_kv, far_kv, both_kv)
     attended = pl.pallas_call(
         functools.partial(rest_kernel, instances, capacity, per_group),
         out_shape=shape(slots, heads * HD),
@@ -356,7 +370,7 @@
         compiler_params=pltpu.CompilerParams(vmem_limit_bytes=24 << 20),
         cost_estimate=pl.CostEstimate(flops=1 << 29, bytes_accessed=2 << 20, transcendentals=1 << 19),
         name="attend_rest",
-    )(me, *got[instances:], half, allowed, keys_rest, vals_rest)
+    )(me, *got[:2], *got[instances:], half, allowed, keys_rest, vals_rest)
     return (attended, key_cache, value_cache)
 
 

time: 32.4 us -> 32.7 us (level)
  starting transfers between devices: 14.9 us -> 16.8 us
  waiting for transfers between devices: 10.1 us -> 8.59 us
    ppermute x8, starting transfers between devices: 14.9 us -> 16.8 us  [swap(): return lax.ppermute(array, 'seq', [(i, i ^ k) for i in range(instances)])]
    ppermute x8, waiting for transfers between devices: 10.1 us -> 8.59 us  [swap(): return lax.ppermute(array, 'seq', [(i, i ^ k) for i in range(instances)])]
where the time goes in v10:
time: 32.7 us; the launch traced here: 32.5 us
  starting transfers between devices  16.8 us (51%)
  waiting for transfers between devices  8.59 us (26%)
  Pallas kernels  3.84 us (12%)
  local copies, waits for them, and re-layouts  2.6 us (8%)
  between operations  0.67 us (2%)
    ppermute x8, starting transfers between devices, swap(): return lax.ppermute(array, 'seq', [(i, i ^ k) for i in range(instances)])  16.8 us
    ppermute x8, waiting for transfers between devices, swap(): return lax.ppermute(array, 'seq', [(i, i ^ k) for i in range(instances)])  8.59 us
    unnamed x9, local copies, waits for them, and re-layouts  2.59 us
    pallas_call x1, Pallas kernels, few_instances(): pl.pallas_call(functools.partial(rest_kernel, instances, capacity, per_gr...  1.86 us
    pallas_call x1, Pallas kernels, few_instances(): pl.pallas_call(functools.partial(lead_kernel, instances, capacity, per_gr...  1.44 us
  transfers between devices with their start and end apart: 8, of which 4 were waited for; matrix products, arithmetic and copies ran while one was open for 0% of the time, Pallas kernels for 6%

profile of v10, /device:TPU:0, one launch (start us, length us, event | category | flops | bytes accessed | tf_op | source)
XLA Modules:
  0.0 32.5 jit_solution(4198191023365153569)
XLA Ops:
  0.6 0.0 copy-start.3
  0.6 0.9 %constant_dynamic-update-slice_fusion.1 = bf16[128,512]{1,0:T(8,128)(2,1)S(1)} fusion(bf16[128,256]{1,0:T(8,128)(2,1)} %param.6), kind=kLoop, calls=%fused_computation.1 | loop fusion | bytes 131072
  1.5 0.0 copy-done.3
  1.5 3.1 %collective-permute-start = (bf16[128,512]{1,0:T(8,128)(2,1)S(1)}, bf16[128,512]{1,0:T(8,128)(2,1)S(1)}, u32[]{:S(2)}, u32[]{:S(2)}) collective-permute-start(bf16[128,512]{1,0:T(8,128)(2,1)S(1)} %constant_dynamic-update-slice_fusion.rest_4_), channel_id=1, source_target_pairs={{0,4},{4,0},{8,12},{12,8},{1,5},{5,1},{9,13},{13,9},{2,6},{6,2},{1... | collective-permute-start | bytes 393224 | tf_op jit(solution)/shard_map/ppermute | solution.py:302
  4.6 2.6 %collective-permute-start.6 = (bf16[128,512]{1,0:T(8,128)(2,1)S(1)}, bf16[128,512]{1,0:T(8,128)(2,1)S(1)}, u32[]{:S(2)}, u32[]{:S(2)}) collective-permute-start(bf16[128,512]{1,0:T(8,128)(2,1)S(1)} %constant_dynamic-update-slice_fusion.rest_4_), channel_id=1, source_target_pairs={{0,8},{4,12},{8,0},{12,4},{1,9},{5,13},{9,1},{13,5},{2,10},{6,14},... | collective-permute-start | bytes 393224 | tf_op jit(solution)/shard_map/ppermute | solution.py:302
  7.2 0.0 copy-start.1
  7.2 0.0 copy-start.2
  7.2 0.7 %copy-done.1 = s32[128,1]{0,1:T(1,128)S(1)} copy-done((s32[128,1]{0,1:T(1,128)S(1)}, s32[128,1]{0,1:T(1,128)}, u32[]{:S(2)}) %copy-start.1) | copy-done | bytes 536
  7.9 0.0 copy-done.2
  7.9 0.0 copy-start
  7.9 1.0 %copy-done = bf16[128,2048]{1,0:T(8,128)(2,1)S(1)} copy-done((bf16[128,2048]{1,0:T(8,128)(2,1)S(1)}, bf16[128,2048]{1,0:T(8,128)(2,1)}, u32[]{:S(2)}) %copy-start) | copy-done | bytes 524312
  8.9 0.5 %pack.1 = (bf16[784,128]{1,0:T(8,128)(2,1)S(1)}, bf16[784,128]{1,0:T(8,128)(2,1)S(1)}, bf16[400,128]{1,0:T(8,128)(2,1)S(1)}, bf16[400,128]{1,0:T(8,128)(2,1)S(1)...) custom-call(s32[1]{0:T(128)} %bitcast.me_ref, bf16[128,2048]{1,0:T(8,128)(2,1)S(1)} %copy-done, ...), custom_call_target="tpu_custom_call" | custom-call | flops 134217728 | bytes 2097152 | tf_op jit(solution)/shard_map/pack/pallas_call | solution.py:313
  9.5 0.5 %collective-permute-done.near_ref.rest_5_ = bf16[128,512]{1,0:T(8,128)(2,1)S(1)} collective-permute-done((bf16[128,512]{1,0:T(8,128)(2,1)S(1)}, bf16[128,512]{1,0:T(8,128)(2,1)S(1)}, u32[]{:S(2)}, u32[]{:S(2)}) %collective-permute-start) | collective-permute-done | bytes 131104 | tf_op jit(solution)/shard_map/ppermute | solution.py:302
  10.0 0.4 %collective-permute-start.1 = (bf16[784,128]{1,0:T(8,128)(2,1)S(1)}, bf16[784,128]{1,0:T(8,128)(2,1)S(1)}, u32[]{:S(2)}, u32[]{:S(2)}) collective-permute-start(bf16[784,128]{1,0:T(8,128)(2,1)S(1)} %gate.1), channel_id=1, source_target_pairs={{0,4},{4,0},{8,12},{12,8},{1,5},{5,1},{9,13},{13,9},{2,6},{6,2},{1... | collective-permute-start | bytes 602120 | tf_op jit(solution)/shard_map/ppermute | solution.py:302
  10.3 3.7 %collective-permute-start.4 = (bf16[400,128]{1,0:T(8,128)(2,1)S(1)}, bf16[400,128]{1,0:T(8,128)(2,1)S(1)}, u32[]{:S(2)}, u32[]{:S(2)}) collective-permute-start(bf16[400,128]{1,0:T(8,128)(2,1)S(1)} %get-tuple-element.19), channel_id=1, source_target_pairs={{0,8},{4,12},{8,0},{12,4},{1,9},{5,13},{9,1},{13,5},{2,10},{6,14},... | collective-permute-start | bytes 307208 | tf_op jit(solution)/shard_map/ppermute | solution.py:302
  14.0 0.0 collective-permute-done.6.rest_6_
  14.0 0.0 collective-permute-start.7
  14.0 1.9 %collective-permute-start.5 = (bf16[400,128]{1,0:T(8,128)(2,1)S(1)}, bf16[400,128]{1,0:T(8,128)(2,1)S(1)}, u32[]{:S(2)}, u32[]{:S(2)}) collective-permute-start(bf16[400,128]{1,0:T(8,128)(2,1)S(1)} %get-tuple-element.20), channel_id=1, source_target_pairs={{0,12},{4,8},{8,4},{12,0},{1,13},{5,9},{9,5},{13,1},{2,14},{6,10},... | collective-permute-start | bytes 307208 | tf_op jit(solution)/shard_map/ppermute | solution.py:302
  15.9 1.6 %collective-permute-start.2 = (bf16[384,128]{1,0:T(8,128)(2,1)S(1)}, bf16[384,128]{1,0:T(8,128)(2,1)S(1)}, u32[]{:S(2)}, u32[]{:S(2)}) collective-permute-start(bf16[384,128]{1,0:T(8,128)(2,1)S(1)} %get-tuple-element.17), channel_id=1, source_target_pairs={{0,8},{4,12},{8,0},{12,4},{1,9},{5,13},{9,1},{13,5},{2,10},{6,14},... | collective-permute-start | bytes 294920 | tf_op jit(solution)/shard_map/ppermute | solution.py:302
  17.5 1.0 %collective-permute-done.4.rest_2_ = bf16[400,128]{1,0:T(8,128)(2,1)S(1)} collective-permute-done((bf16[400,128]{1,0:T(8,128)(2,1)S(1)}, bf16[400,128]{1,0:T(8,128)(2,1)S(1)}, u32[]{:S(2)}, u32[]{:S(2)}) %collective-permute-start.4) | collective-permute-done | bytes 102432 | tf_op jit(solution)/shard_map/ppermute | solution.py:302
  18.5 3.6 %collective-permute-start.3 = (bf16[384,128]{1,0:T(8,128)(2,1)S(1)}, bf16[384,128]{1,0:T(8,128)(2,1)S(1)}, u32[]{:S(2)}, u32[]{:S(2)}) collective-permute-start(bf16[384,128]{1,0:T(8,128)(2,1)S(1)} %get-tuple-element.18), channel_id=1, source_target_pairs={{0,12},{4,8},{8,4},{12,0},{1,13},{5,9},{9,5},{13,1},{2,14},{6,10},... | collective-permute-start | bytes 294920 | tf_op jit(solution)/shard_map/ppermute | solution.py:302
  22.0 4.6 %collective-permute-done.5.rest_3_ = bf16[400,128]{1,0:T(8,128)(2,1)S(1)} collective-permute-done((bf16[400,128]{1,0:T(8,128)(2,1)S(1)}, bf16[400,128]{1,0:T(8,128)(2,1)S(1)}, u32[]{:S(2)}, u32[]{:S(2)}) %collective-permute-start.5) | collective-permute-done | bytes 102432 | tf_op jit(solution)/shard_map/ppermute | solution.py:302
  26.6 0.0 collective-permute-done.7.rest_7_
  26.6 0.0 collective-permute-done.1.rest_1_
  26.6 1.4 %attend_lead.1 = (bf16[192,1024]{1,0:T(8,128)(2,1)S(1)}, bf16[192,256]{1,0:T(8,128)(2,1)S(1)}, bf16[512,128]{1,0:T(8,128)(2,1)S(1)}, bf16[512,256]{1,0:T(8,128)(...) custom-call(s32[1]{0:T(128)} %bitcast.me_ref, bf16[784,128]{1,0:T(8,128)(2,1)S(1)} %get-tuple-element.15.rest_0_, ...), custom_call_target="tpu_custom_call" | custom-call | flops 536870912 | bytes 2097152 | tf_op jit(solution)/shard_map/attend_lead/pallas_call | solution.py:339
  28.0 2.6 %collective-permute-done.2.rest_2_ = bf16[384,128]{1,0:T(8,128)(2,1)S(1)} collective-permute-done((bf16[384,128]{1,0:T(8,128)(2,1)S(1)}, bf16[384,128]{1,0:T(8,128)(2,1)S(1)}, u32[]{:S(2)}, u32[]{:S(2)}) %collective-permute-start.2) | collective-permute-done | bytes 98336 | tf_op jit(solution)/shard_map/ppermute | solution.py:302
  30.6 0.0 collective-permute-done.3.rest_3_
  30.6 1.9 %attend_rest.1 = bf16[192,2048]{1,0:T(8,128)(2,1)} custom-call(s32[1]{0:T(128)} %bitcast.me_ref, bf16[784,128]{1,0:T(8,128)(2,1)S(1)} %get-tuple-element.15.rest_0_, bf16[784,128]{1,0:T(8,128)(2,1)S(1)} %collective-permute-done.1.rest_1_, bf16[384,128]{1,0:T(8,128)(2,1)S(1)} %collective-permute-done.2.rest_2_, ...), custom_call_target="tpu_custom_call" | custom-call | flops 536870912 | bytes 2097152 | tf_op jit(solution)/shard_map/attend_rest/pallas_call | solution.py:360
  (2 shorter events, 0.0 us)
Async XLA Ops:
  0.6 0.9 %copy-start.3 = (bf16[128,256]{1,0:T(8,128)(2,1)S(1)}, bf16[128,256]{1,0:T(8,128)(2,1)}, u32[]{:S(2)}) copy-start(bf16[128,256]{1,0:T(8,128)(2,1)} %param.7) | copy-start | bytes 196612
  1.5 8.4 %collective-permute-start = (bf16[128,512]{1,0:T(8,128)(2,1)S(1)}, bf16[128,512]{1,0:T(8,128)(2,1)S(1)}, u32[]{:S(2)}, u32[]{:S(2)}) collective-permute-start(bf16[128,512]{1,0:T(8,128)(2,1)S(1)} %constant_dynamic-update-slice_fusion.rest_4_), channel_id=1, source_target_pairs={{0,4},{4,0},{8,12},{12,8},{1,5},{5,1},{9,13},{13,9},{2,6},{6,2},{1... | collective-permute-start | bytes 393224 | tf_op jit(solution)/shard_map/ppermute | solution.py:302
  4.6 9.4 %collective-permute-start.6 = (bf16[128,512]{1,0:T(8,128)(2,1)S(1)}, bf16[128,512]{1,0:T(8,128)(2,1)S(1)}, u32[]{:S(2)}, u32[]{:S(2)}) collective-permute-start(bf16[128,512]{1,0:T(8,128)(2,1)S(1)} %constant_dynamic-update-slice_fusion.rest_4_), channel_id=1, source_target_pairs={{0,8},{4,12},{8,0},{12,4},{1,9},{5,13},{9,1},{13,5},{2,10},{6,14},... | collective-permute-start | bytes 393224 | tf_op jit(solution)/shard_map/ppermute | solution.py:302
  7.2 0.7 %copy-start.1 = (s32[128,1]{0,1:T(1,128)S(1)}, s32[128,1]{0,1:T(1,128)}, u32[]{:S(2)}) copy-start(s32[128,1]{0,1:T(1,128)} %param.8) | copy-start | bytes 1540
  7.2 0.7 %copy-start.2 = (s32[128,1]{0,1:T(1,128)S(1)}, s32[128,1]{0,1:T(1,128)}, u32[]{:S(2)}) copy-start(s32[128,1]{0,1:T(1,128)} %param.9) | copy-start | bytes 1540
  7.9 1.0 %copy-start = (bf16[128,2048]{1,0:T(8,128)(2,1)S(1)}, bf16[128,2048]{1,0:T(8,128)(2,1)}, u32[]{:S(2)}) copy-start(bf16[128,2048]{1,0:T(8,128)(2,1)} %q_hbm.1) | copy-start | bytes 1572868
  10.0 16.6 %collective-permute-start.1 = (bf16[784,128]{1,0:T(8,128)(2,1)S(1)}, bf16[784,128]{1,0:T(8,128)(2,1)S(1)}, u32[]{:S(2)}, u32[]{:S(2)}) collective-permute-start(bf16[784,128]{1,0:T(8,128)(2,1)S(1)} %gate.1), channel_id=1, source_target_pairs={{0,4},{4,0},{8,12},{12,8},{1,5},{5,1},{9,13},{13,9},{2,6},{6,2},{1... | collective-permute-start | bytes 602120 | tf_op jit(solution)/shard_map/ppermute | solution.py:302
  10.3 8.1 %collective-permute-start.4 = (bf16[400,128]{1,0:T(8,128)(2,1)S(1)}, bf16[400,128]{1,0:T(8,128)(2,1)S(1)}, u32[]{:S(2)}, u32[]{:S(2)}) collective-permute-start(bf16[400,128]{1,0:T(8,128)(2,1)S(1)} %get-tuple-element.19), channel_id=1, source_target_pairs={{0,8},{4,12},{8,0},{12,4},{1,9},{5,13},{9,1},{13,5},{2,10},{6,14},... | collective-permute-start | bytes 307208 | tf_op jit(solution)/shard_map/ppermute | solution.py:302
  14.0 12.6 %collective-permute-start.7 = (bf16[128,512]{1,0:T(8,128)(2,1)S(1)}, bf16[128,512]{1,0:T(8,128)(2,1)S(1)}, u32[]{:S(2)}, u32[]{:S(2)}) collective-permute-start(bf16[128,512]{1,0:T(8,128)(2,1)S(1)} %collective-permute-done.6.rest_6_), channel_id=1, source_target_pairs={{0,4},{4,0},{8,12},{12,8},{1,5},{5,1},{9,13},{13,9},{2,6},{6,2},{1... | collective-permute-start | bytes 393224 | tf_op jit(solution)/shard_map/ppermute | solution.py:302
  14.0 12.5 %collective-permute-start.5 = (bf16[400,128]{1,0:T(8,128)(2,1)S(1)}, bf16[400,128]{1,0:T(8,128)(2,1)S(1)}, u32[]{:S(2)}, u32[]{:S(2)}) collective-permute-start(bf16[400,128]{1,0:T(8,128)(2,1)S(1)} %get-tuple-element.20), channel_id=1, source_target_pairs={{0,12},{4,8},{8,4},{12,0},{1,13},{5,9},{9,5},{13,1},{2,14},{6,10},... | collective-permute-start | bytes 307208 | tf_op jit(solution)/shard_map/ppermute | solution.py:302
  15.9 14.7 %collective-permute-start.2 = (bf16[384,128]{1,0:T(8,128)(2,1)S(1)}, bf16[384,128]{1,0:T(8,128)(2,1)S(1)}, u32[]{:S(2)}, u32[]{:S(2)}) collective-permute-start(bf16[384,128]{1,0:T(8,128)(2,1)S(1)} %get-tuple-element.17), channel_id=1, source_target_pairs={{0,8},{4,12},{8,0},{12,4},{1,9},{5,13},{9,1},{13,5},{2,10},{6,14},... | collective-permute-start | bytes 294920 | tf_op jit(solution)/shard_map/ppermute | solution.py:302
  18.5 12.2 %collective-permute-start.3 = (bf16[384,128]{1,0:T(8,128)(2,1)S(1)}, bf16[384,128]{1,0:T(8,128)(2,1)S(1)}, u32[]{:S(2)}, u32[]{:S(2)}) collective-permute-start(bf16[384,128]{1,0:T(8,128)(2,1)S(1)} %get-tuple-element.18), channel_id=1, source_target_pairs={{0,12},{4,8},{8,4},{12,0},{1,13},{5,9},{9,5},{13,1},{2,14},{6,10},... | collective-permute-start | bytes 294920 | tf_op jit(solution)/shard_map/ppermute | solution.py:302

commit v11 on v10

--- a/solution.py
+++ b/solution.py
@@ -324,17 +324,17 @@
         name="pack",
     )(me, queries, query_owner.reshape(1, rows), cache_owner.reshape(1, rows))
     anyspace = pl.BlockSpec(memory_space=pl.ANY)
-    beside = pl.pallas_call(
+    opposite = pl.pallas_call(
         gate_kernel,
-        out_shape=shape(*sends[1].shape),
+        out_shape=shape(*sends[2].shape),
         in_specs=[anyspace] * 2,
         out_specs=anyspace,
         input_output_aliases={1: 0},
         compiler_params=pltpu.CompilerParams(vmem_limit_bytes=16 << 20),
         cost_estimate=pl.CostEstimate(flops=0, bytes_accessed=0, transcendentals=0),
         name="gate",
-    )(near_kv, sends[1])
-    sends = [sends[0], beside, *sends[2:]]
+    )(near_kv, sends[2])
+    sends = [*sends[:2], opposite, *sends[3:]]
     got = [swap(piece, k) if k else piece for k, piece in zip(distances, sends)]
     half, allowed, keys_rest, vals_rest, key_cache, value_cache = pl.pallas_call(
         functools.partial(lead_kernel, instances, capacity, per_group),

time: 32.7 us -> 32 us (0.979)
  starting transfers between devices: 16.8 us -> 14.2 us
  waiting for transfers between devices: 8.59 us -> 10.5 us
    ppermute x8, starting transfers between devices: 16.8 us -> 14.2 us  [swap(): return lax.ppermute(array, 'seq', [(i, i ^ k) for i in range(instances)])]
    ppermute x8, waiting for transfers between devices: 8.59 us -> 10.5 us  [swap(): return lax.ppermute(array, 'seq', [(i, i ^ k) for i in range(instances)])]
  transfers between devices with their start and end apart: 8 -> 8, of which waited for: 4 -> 5; matrix products, arithmetic and copies ran while one was open for 0% -> 0% of each run, Pallas kernels for 6% -> 6%
where the time goes in v11:
time: 32 us; the launch traced here: 31.8 us
  starting transfers between devices  14.2 us (44%)
  waiting for transfers between devices  10.5 us (33%)
  Pallas kernels  3.83 us (12%)
  local copies, waits for them, and re-layouts  2.6 us (8%)
  between operations  0.67 us (2%)
    ppermute x8, starting transfers between devices, swap(): return lax.ppermute(array, 'seq', [(i, i ^ k) for i in range(instances)])  14.2 us
    ppermute x8, waiting for transfers between devices, swap(): return lax.ppermute(array, 'seq', [(i, i ^ k) for i in range(instances)])  10.5 us
    unnamed x9, local copies, waits for them, and re-layouts  2.59 us
    pallas_call x1, Pallas kernels, few_instances(): pl.pallas_call(functools.partial(rest_kernel, instances, capacity, per_gr...  1.85 us
    pallas_call x1, Pallas kernels, few_instances(): pl.pallas_call(functools.partial(lead_kernel, instances, capacity, per_gr...  1.43 us
  transfers between devices with their start and end apart: 8, of which 5 were waited for; matrix products, arithmetic and copies ran while one was open for 0% of the time, Pallas kernels for 6%

profile of v11, /device:TPU:0, one launch (start us, length us, event | category | flops | bytes accessed | tf_op | source)
XLA Modules:
  0.0 31.8 jit_solution(12115803342549979239)
XLA Ops:
  0.6 0.0 copy-start.3
  0.6 0.9 %constant_dynamic-update-slice_fusion.1 = bf16[128,512]{1,0:T(8,128)(2,1)S(1)} fusion(bf16[128,256]{1,0:T(8,128)(2,1)} %param.6), kind=kLoop, calls=%fused_computation.1 | loop fusion | bytes 131072
  1.5 0.0 copy-done.3
  1.5 4.1 %collective-permute-start.6 = (bf16[128,512]{1,0:T(8,128)(2,1)S(1)}, bf16[128,512]{1,0:T(8,128)(2,1)S(1)}, u32[]{:S(2)}, u32[]{:S(2)}) collective-permute-start(bf16[128,512]{1,0:T(8,128)(2,1)S(1)} %constant_dynamic-update-slice_fusion.rest_4_), channel_id=1, source_target_pairs={{0,8},{4,12},{8,0},{12,4},{1,9},{5,13},{9,1},{13,5},{2,10},{6,14},... | collective-permute-start | bytes 393224 | tf_op jit(solution)/shard_map/ppermute | solution.py:302
  5.6 1.6 %collective-permute-start.3 = (bf16[128,512]{1,0:T(8,128)(2,1)S(1)}, bf16[128,512]{1,0:T(8,128)(2,1)S(1)}, u32[]{:S(2)}, u32[]{:S(2)}) collective-permute-start(bf16[128,512]{1,0:T(8,128)(2,1)S(1)} %constant_dynamic-update-slice_fusion.rest_4_), channel_id=1, source_target_pairs={{0,4},{4,0},{8,12},{12,8},{1,5},{5,1},{9,13},{13,9},{2,6},{6,2},{1... | collective-permute-start | bytes 393224 | tf_op jit(solution)/shard_map/ppermute | solution.py:302
  7.2 0.0 copy-start.1
  7.2 0.0 copy-start.2
  7.2 0.7 %copy-done.1 = s32[128,1]{0,1:T(1,128)S(1)} copy-done((s32[128,1]{0,1:T(1,128)S(1)}, s32[128,1]{0,1:T(1,128)}, u32[]{:S(2)}) %copy-start.1) | copy-done | bytes 536
  7.9 0.0 copy-done.2
  7.9 0.0 copy-start
  7.9 1.0 %copy-done = bf16[128,2048]{1,0:T(8,128)(2,1)S(1)} copy-done((bf16[128,2048]{1,0:T(8,128)(2,1)S(1)}, bf16[128,2048]{1,0:T(8,128)(2,1)}, u32[]{:S(2)}) %copy-start) | copy-done | bytes 524312
  8.9 0.5 %pack.1 = (bf16[784,128]{1,0:T(8,128)(2,1)S(1)}, bf16[784,128]{1,0:T(8,128)(2,1)S(1)}, bf16[400,128]{1,0:T(8,128)(2,1)S(1)}, bf16[400,128]{1,0:T(8,128)(2,1)S(1)...) custom-call(s32[1]{0:T(128)} %bitcast.me_ref, bf16[128,2048]{1,0:T(8,128)(2,1)S(1)} %copy-done, ...), custom_call_target="tpu_custom_call" | custom-call | flops 134217728 | bytes 2097152 | tf_op jit(solution)/shard_map/pack/pallas_call | solution.py:313
  9.5 0.5 %collective-permute-start = (bf16[784,128]{1,0:T(8,128)(2,1)S(1)}, bf16[784,128]{1,0:T(8,128)(2,1)S(1)}, u32[]{:S(2)}, u32[]{:S(2)}) collective-permute-start(bf16[784,128]{1,0:T(8,128)(2,1)S(1)} %get-tuple-element.16), channel_id=1, source_target_pairs={{0,4},{4,0},{8,12},{12,8},{1,5},{5,1},{9,13},{13,9},{2,6},{6,2},{1... | collective-permute-start | bytes 602120 | tf_op jit(solution)/shard_map/ppermute | solution.py:302
  10.0 1.3 %collective-permute-start.5 = (bf16[400,128]{1,0:T(8,128)(2,1)S(1)}, bf16[400,128]{1,0:T(8,128)(2,1)S(1)}, u32[]{:S(2)}, u32[]{:S(2)}) collective-permute-start(bf16[400,128]{1,0:T(8,128)(2,1)S(1)} %get-tuple-element.20), channel_id=1, source_target_pairs={{0,12},{4,8},{8,4},{12,0},{1,13},{5,9},{9,5},{13,1},{2,14},{6,10},... | collective-permute-start | bytes 307208 | tf_op jit(solution)/shard_map/ppermute | solution.py:302
  11.3 0.7 %collective-permute-done.6.rest_6_ = bf16[128,512]{1,0:T(8,128)(2,1)S(1)} collective-permute-done((bf16[128,512]{1,0:T(8,128)(2,1)S(1)}, bf16[128,512]{1,0:T(8,128)(2,1)S(1)}, u32[]{:S(2)}, u32[]{:S(2)}) %collective-permute-start.6) | collective-permute-done | bytes 131104 | tf_op jit(solution)/shard_map/ppermute | solution.py:302
  12.0 0.8 %collective-permute-start.7 = (bf16[128,512]{1,0:T(8,128)(2,1)S(1)}, bf16[128,512]{1,0:T(8,128)(2,1)S(1)}, u32[]{:S(2)}, u32[]{:S(2)}) collective-permute-start(bf16[128,512]{1,0:T(8,128)(2,1)S(1)} %collective-permute-done.6.rest_6_), channel_id=1, source_target_pairs={{0,4},{4,0},{8,12},{12,8},{1,5},{5,1},{9,13},{13,9},{2,6},{6,2},{1... | collective-permute-start | bytes 393224 | tf_op jit(solution)/shard_map/ppermute | solution.py:302
  12.8 0.0 collective-permute-done.3.near_ref.rest_5_
  12.8 3.4 %collective-permute-start.4 = (bf16[400,128]{1,0:T(8,128)(2,1)S(1)}, bf16[400,128]{1,0:T(8,128)(2,1)S(1)}, u32[]{:S(2)}, u32[]{:S(2)}) collective-permute-start(bf16[400,128]{1,0:T(8,128)(2,1)S(1)} %gate.1), channel_id=1, source_target_pairs={{0,8},{4,12},{8,0},{12,4},{1,9},{5,13},{9,1},{13,5},{2,10},{6,14},... | collective-permute-start | bytes 307208 | tf_op jit(solution)/shard_map/ppermute | solution.py:302
  16.2 0.0 collective-permute-start.1
  16.2 4.5 %collective-permute-done.5.rest_3_ = bf16[400,128]{1,0:T(8,128)(2,1)S(1)} collective-permute-done((bf16[400,128]{1,0:T(8,128)(2,1)S(1)}, bf16[400,128]{1,0:T(8,128)(2,1)S(1)}, u32[]{:S(2)}, u32[]{:S(2)}) %collective-permute-start.5) | collective-permute-done | bytes 102432 | tf_op jit(solution)/shard_map/ppermute | solution.py:302
  20.7 2.5 %collective-permute-start.2 = (bf16[384,128]{1,0:T(8,128)(2,1)S(1)}, bf16[384,128]{1,0:T(8,128)(2,1)S(1)}, u32[]{:S(2)}, u32[]{:S(2)}) collective-permute-start(bf16[384,128]{1,0:T(8,128)(2,1)S(1)} %get-tuple-element.18), channel_id=1, source_target_pairs={{0,12},{4,8},{8,4},{12,0},{1,13},{5,9},{9,5},{13,1},{2,14},{6,10},... | collective-permute-start | bytes 294920 | tf_op jit(solution)/shard_map/ppermute | solution.py:302
  23.2 0.0 collective-permute-done.rest_1_
  23.2 0.7 %collective-permute-done.4.rest_2_ = bf16[400,128]{1,0:T(8,128)(2,1)S(1)} collective-permute-done((bf16[400,128]{1,0:T(8,128)(2,1)S(1)}, bf16[400,128]{1,0:T(8,128)(2,1)S(1)}, u32[]{:S(2)}, u32[]{:S(2)}) %collective-permute-start.4) | collective-permute-done | bytes 102432 | tf_op jit(solution)/shard_map/ppermute | solution.py:302
  23.9 1.4 %collective-permute-done.7.rest_7_ = bf16[128,512]{1,0:T(8,128)(2,1)S(1)} collective-permute-done((bf16[128,512]{1,0:T(8,128)(2,1)S(1)}, bf16[128,512]{1,0:T(8,128)(2,1)S(1)}, u32[]{:S(2)}, u32[]{:S(2)}) %collective-permute-start.7) | collective-permute-done | bytes 131104 | tf_op jit(solution)/shard_map/ppermute | solution.py:302
  25.3 1.4 %attend_lead.1 = (bf16[192,1024]{1,0:T(8,128)(2,1)S(1)}, bf16[192,256]{1,0:T(8,128)(2,1)S(1)}, bf16[512,128]{1,0:T(8,128)(2,1)S(1)}, bf16[512,256]{1,0:T(8,128)(...) custom-call(s32[1]{0:T(128)} %bitcast.me_ref, bf16[784,128]{1,0:T(8,128)(2,1)S(1)} %get-tuple-element.15.rest_0_, ...), custom_call_target="tpu_custom_call" | custom-call | flops 536870912 | bytes 2097152 | tf_op jit(solution)/shard_map/attend_lead/pallas_call | solution.py:339
  26.7 3.2 %collective-permute-done.1.rest_2_ = bf16[384,128]{1,0:T(8,128)(2,1)S(1)} collective-permute-done((bf16[384,128]{1,0:T(8,128)(2,1)S(1)}, bf16[384,128]{1,0:T(8,128)(2,1)S(1)}, u32[]{:S(2)}, u32[]{:S(2)}) %collective-permute-start.1) | collective-permute-done | bytes 98336 | tf_op jit(solution)/shard_map/ppermute | solution.py:302
  29.9 0.0 collective-permute-done.2.rest_3_
  29.9 1.8 %attend_rest.1 = bf16[192,2048]{1,0:T(8,128)(2,1)} custom-call(s32[1]{0:T(128)} %bitcast.me_ref, bf16[784,128]{1,0:T(8,128)(2,1)S(1)} %get-tuple-element.15.rest_0_, bf16[784,128]{1,0:T(8,128)(2,1)S(1)} %collective-permute-done.rest_1_, bf16[384,128]{1,0:T(8,128)(2,1)S(1)} %collective-permute-done.1.rest_2_, ...), custom_call_target="tpu_custom_call" | custom-call | flops 536870912 | bytes 2097152 | tf_op jit(solution)/shard_map/attend_rest/pallas_call | solution.py:360
  (2 shorter events, 0.0 us)
Async XLA Ops:
  0.6 0.9 %copy-start.3 = (bf16[128,256]{1,0:T(8,128)(2,1)S(1)}, bf16[128,256]{1,0:T(8,128)(2,1)}, u32[]{:S(2)}) copy-start(bf16[128,256]{1,0:T(8,128)(2,1)} %param.7) | copy-start | bytes 196612
  1.5 10.5 %collective-permute-start.6 = (bf16[128,512]{1,0:T(8,128)(2,1)S(1)}, bf16[128,512]{1,0:T(8,128)(2,1)S(1)}, u32[]{:S(2)}, u32[]{:S(2)}) collective-permute-start(bf16[128,512]{1,0:T(8,128)(2,1)S(1)} %constant_dynamic-update-slice_fusion.rest_4_), channel_id=1, source_target_pairs={{0,8},{4,12},{8,0},{12,4},{1,9},{5,13},{9,1},{13,5},{2,10},{6,14},... | collective-permute-start | bytes 393224 | tf_op jit(solution)/shard_map/ppermute | solution.py:302
  5.6 7.2 %collective-permute-start.3 = (bf16[128,512]{1,0:T(8,128)(2,1)S(1)}, bf16[128,512]{1,0:T(8,128)(2,1)S(1)}, u32[]{:S(2)}, u32[]{:S(2)}) collective-permute-start(bf16[128,512]{1,0:T(8,128)(2,1)S(1)} %constant_dynamic-update-slice_fusion.rest_4_), channel_id=1, source_target_pairs={{0,4},{4,0},{8,12},{12,8},{1,5},{5,1},{9,13},{13,9},{2,6},{6,2},{1... | collective-permute-start | bytes 393224 | tf_op jit(solution)/shard_map/ppermute | solution.py:302
  7.2 0.7 %copy-start.1 = (s32[128,1]{0,1:T(1,128)S(1)}, s32[128,1]{0,1:T(1,128)}, u32[]{:S(2)}) copy-start(s32[128,1]{0,1:T(1,128)} %param.8) | copy-start | bytes 1540
  7.2 0.7 %copy-start.2 = (s32[128,1]{0,1:T(1,128)S(1)}, s32[128,1]{0,1:T(1,128)}, u32[]{:S(2)}) copy-start(s32[128,1]{0,1:T(1,128)} %param.9) | copy-start | bytes 1540
  7.9 1.0 %copy-start = (bf16[128,2048]{1,0:T(8,128)(2,1)S(1)}, bf16[128,2048]{1,0:T(8,128)(2,1)}, u32[]{:S(2)}) copy-start(bf16[128,2048]{1,0:T(8,128)(2,1)} %q_hbm.1) | copy-start | bytes 1572868
  9.5 13.7 %collective-permute-start = (bf16[784,128]{1,0:T(8,128)(2,1)S(1)}, bf16[784,128]{1,0:T(8,128)(2,1)S(1)}, u32[]{:S(2)}, u32[]{:S(2)}) collective-permute-start(bf16[784,128]{1,0:T(8,128)(2,1)S(1)} %get-tuple-element.16), channel_id=1, source_target_pairs={{0,4},{4,0},{8,12},{12,8},{1,5},{5,1},{9,13},{13,9},{2,6},{6,2},{1... | collective-permute-start | bytes 602120 | tf_op jit(solution)/shard_map/ppermute | solution.py:302
  10.0 10.7 %collective-permute-start.5 = (bf16[400,128]{1,0:T(8,128)(2,1)S(1)}, bf16[400,128]{1,0:T(8,128)(2,1)S(1)}, u32[]{:S(2)}, u32[]{:S(2)}) collective-permute-start(bf16[400,128]{1,0:T(8,128)(2,1)S(1)} %get-tuple-element.20), channel_id=1, source_target_pairs={{0,12},{4,8},{8,4},{12,0},{1,13},{5,9},{9,5},{13,1},{2,14},{6,10},... | collective-permute-start | bytes 307208 | tf_op jit(solution)/shard_map/ppermute | solution.py:302
  12.0 13.3 %collective-permute-start.7 = (bf16[128,512]{1,0:T(8,128)(2,1)S(1)}, bf16[128,512]{1,0:T(8,128)(2,1)S(1)}, u32[]{:S(2)}, u32[]{:S(2)}) collective-permute-start(bf16[128,512]{1,0:T(8,128)(2,1)S(1)} %collective-permute-done.6.rest_6_), channel_id=1, source_target_pairs={{0,4},{4,0},{8,12},{12,8},{1,5},{5,1},{9,13},{13,9},{2,6},{6,2},{1... | collective-permute-start | bytes 393224 | tf_op jit(solution)/shard_map/ppermute | solution.py:302
  12.8 11.1 %collective-permute-start.4 = (bf16[400,128]{1,0:T(8,128)(2,1)S(1)}, bf16[400,128]{1,0:T(8,128)(2,1)S(1)}, u32[]{:S(2)}, u32[]{:S(2)}) collective-permute-start(bf16[400,128]{1,0:T(8,128)(2,1)S(1)} %gate.1), channel_id=1, source_target_pairs={{0,8},{4,12},{8,0},{12,4},{1,9},{5,13},{9,1},{13,5},{2,10},{6,14},... | collective-permute-start | bytes 307208 | tf_op jit(solution)/shard_map/ppermute | solution.py:302
  16.2 13.7 %collective-permute-start.1 = (bf16[384,128]{1,0:T(8,128)(2,1)S(1)}, bf16[384,128]{1,0:T(8,128)(2,1)S(1)}, u32[]{:S(2)}, u32[]{:S(2)}) collective-permute-start(bf16[384,128]{1,0:T(8,128)(2,1)S(1)} %get-tuple-element.17), channel_id=1, source_target_pairs={{0,8},{4,12},{8,0},{12,4},{1,9},{5,13},{9,1},{13,5},{2,10},{6,14},... | collective-permute-start | bytes 294920 | tf_op jit(solution)/shard_map/ppermute | solution.py:302
  20.7 9.2 %collective-permute-start.2 = (bf16[384,128]{1,0:T(8,128)(2,1)S(1)}, bf16[384,128]{1,0:T(8,128)(2,1)S(1)}, u32[]{:S(2)}, u32[]{:S(2)}) collective-permute-start(bf16[384,128]{1,0:T(8,128)(2,1)S(1)} %get-tuple-element.18), channel_id=1, source_target_pairs={{0,12},{4,8},{8,4},{12,0},{1,13},{5,9},{9,5},{13,1},{2,14},{6,10},... | collective-permute-start | bytes 294920 | tf_op jit(solution)/shard_map/ppermute | solution.py:302

commit v12 on v11

--- a/solution.py
+++ b/solution.py
@@ -146,7 +146,11 @@
     return (chosen == slot).astype(jnp.bfloat16)
 
 
-def gate_kernel(near_ref, slots_ref, through_ref):
+def lead_heads(heads):
+    return heads // 2 + 3 * heads // 16
+
+
+def gate_kernel(near_ref, far_ref, through_ref):
     pass
 
 
@@ -170,8 +174,8 @@
     lists = jnp.concatenate(
         [owners, co_ref[...], jnp.full((14, rows), -1, jnp.int32)], axis=0
     ).astype(jnp.float32).astype(jnp.bfloat16)
-    per_group = heads // 2
-    tall = per_group * capacity
+    first = lead_heads(heads)
+    tall = first * capacity
     for k in range(instances):
         lead[k][tall : tall + 16, :] = lists
     fetch.wait()
@@ -183,25 +187,26 @@
         ).astype(jnp.bfloat16)
         for k in range(instances):
             for half in range(2):
-                g, h = divmod(2 * pair + half, per_group)
-                at = h * capacity + (tall + 16) * (g == 1 and k not in second)
-                ref = second[k] if g == 1 and k in second else lead[k]
+                h = 2 * pair + half
+                ref, at = lead[k], h * capacity
+                if h >= first:
+                    ref, at = (second[k], at - tall) if k in second else (ref, at + 16)
                 ref[at : at + capacity, :] = packed[
                     k * capacity : (k + 1) * capacity, half * HD : (half + 1) * HD
                 ]
 
 
-def attend_head(instances, capacity, per_group, wanted_ref, keys, vals, allowed_ref, store):
+def attend_head(instances, capacity, span, wanted_ref, keys, vals, allowed_ref, store):
     rows = HD
-    tall = per_group * capacity
+    count = span.stop - span.start
     scale = math.log2(math.e) / math.sqrt(HD)
     for s in reversed(range(instances)):
         slots = slice(s * capacity, (s + 1) * capacity)
         allowed = allowed_ref[slots, :].astype(jnp.float32)
-        near = jnp.concatenate([allowed[:, :rows]] * per_group, axis=0) > 0.5
-        valid = jnp.concatenate([allowed[:, rows:]] * per_group, axis=0) > 0.5
+        near = jnp.concatenate([allowed[:, :rows]] * count, axis=0) > 0.5
+        valid = jnp.concatenate([allowed[:, rows:]] * count, axis=0) > 0.5
         scores = lax.dot_general(
-            wanted_ref[s, :tall, :],
+            wanted_ref[s, span.start * capacity : span.stop * capacity, :],
             keys[: (s + 1) * rows, :],
             (((1,), (1,)), ((), ())),
             preferred_element_type=jnp.float32,
@@ -212,16 +217,16 @@
         weights = jnp.exp2(scores * scale - top * scale).astype(jnp.bfloat16)
         mixed = jnp.dot(weights, vals[: (s + 1) * rows, :], preferred_element_type=jnp.float32)
         out = jnp.where(valid, mixed[:, :HD] / mixed[:, HD:], 0.0).astype(jnp.bfloat16)
-        for h in range(per_group):
-            store(s, slots, h, out[h * capacity : (h + 1) * capacity, :])
-
-
-def lead_kernel(instances, capacity, per_group, me_ref, *rest):
+        for h in range(count):
+            store(s, slots, span.start + h, out[h * capacity : (h + 1) * capacity, :])
+
+
+def lead_kernel(instances, capacity, heads, me_ref, *rest):
     got, rest = rest[:instances], rest[instances:]
     blocks_of, rest = rest[:instances], rest[instances:]
     half_ref, allowed_ref, keys_ref, vals_ref, kc_ref, vc_ref, wanted_ref, keys, vals = rest
     rows = HD
-    tall = per_group * capacity
+    tall = lead_heads(heads) * capacity
     me = me_ref[0]
     ones = jnp.ones((rows, HD), jnp.bfloat16)
     for k in range(instances):
@@ -260,31 +265,35 @@
     def store(s, slots, h, value):
         half_ref[slots, h * HD : (h + 1) * HD] = value
 
-    attend_head(instances, capacity, per_group, wanted_ref, keys, vals, allowed_ref, store)
-
-
-def rest_kernel(instances, capacity, per_group, me_ref, *rest):
+    halves = (slice(0, heads // 2), keys, vals), (slice(heads // 2, lead_heads(heads)), keys_ref, vals_ref)
+    for span, k_ref, v_ref in halves:
+        attend_head(instances, capacity, span, wanted_ref, k_ref, v_ref, allowed_ref, store)
+
+
+def rest_kernel(instances, capacity, heads, me_ref, *rest):
     got, rest = rest[:instances], rest[instances:]
     half_ref, allowed_ref, keys_ref, vals_ref, att_hbm, wanted_ref, mine_ref, sent = rest
-    width = per_group * HD
-    early = pltpu.make_async_copy(half_ref, att_hbm.at[:, :width], sent.at[instances])
+    first = lead_heads(heads)
+    count = heads - first
+    early = pltpu.make_async_copy(half_ref, att_hbm.at[:, : first * HD], sent.at[instances])
     early.start()
-    tall = per_group * capacity
     for k, piece in zip((0, 1, *SECOND), got):
-        start = 0 if k in SECOND else tall + 16
-        wanted_ref[jnp.bitwise_xor(me_ref[0], k)] = piece[start : start + tall, :]
+        start = 0 if k in SECOND else first * capacity + 16
+        wanted_ref[jnp.bitwise_xor(me_ref[0], k)] = piece[start : start + count * capacity, :]
     copies = []
 
     def store(s, slots, h, value):
         mine_ref[slots, h * HD : (h + 1) * HD] = value
-        if h == per_group - 1:
+        if h == count - 1:
             copy = pltpu.make_async_copy(
-                mine_ref.at[slots, :], att_hbm.at[slots, width:], sent.at[s]
+                mine_ref.at[slots, :], att_hbm.at[slots, first * HD :], sent.at[s]
             )
             copy.start()
             copies.append(copy)
 
-    attend_head(instances, capacity, per_group, wanted_ref, keys_ref, vals_ref, allowed_ref, store)
+    attend_head(
+        instances, capacity, slice(0, count), wanted_ref, keys_ref, vals_ref, allowed_ref, store
+    )
     for copy in [early, *copies]:
         copy.wait()
 
@@ -294,8 +303,8 @@
     rows = queries.shape[0]
     capacity = 3 * rows // (2 * instances)
     heads = queries.shape[1] // HD
-    per_group = heads // 2
-    tall = per_group * capacity
+    first = lead_heads(heads)
+    tall, short = first * capacity, (heads - first) * capacity
     slots = instances * capacity
 
     def swap(array, k):
@@ -308,14 +317,13 @@
     me = lax.axis_index("seq").astype(jnp.int32).reshape(1)
     own_kv = jnp.concatenate([keys, values], axis=1)
     far_kv, near_kv = swap(own_kv, 2), swap(own_kv, 1)
-    both_kv = swap(far_kv, 1)
     distances = (*range(instances), *SECOND)
     sends = pl.pallas_call(
         functools.partial(pack_kernel, instances, capacity),
         out_shape=tuple(
-            shape(tall + 16 + tall * (k not in SECOND), HD) for k in range(instances)
+            shape(tall + 16 + short * (k not in SECOND), HD) for k in range(instances)
         )
-        + (shape(tall, HD),) * len(SECOND),
+        + (shape(short, HD),) * len(SECOND),
         in_specs=[smem, hbm, vmem, vmem],
         out_specs=(vmem,) * len(distances),
         scratch_shapes=[pltpu.VMEM(queries.shape, jnp.bfloat16), pltpu.SemaphoreType.DMA],
@@ -324,22 +332,22 @@
         name="pack",
     )(me, queries, query_owner.reshape(1, rows), cache_owner.reshape(1, rows))
     anyspace = pl.BlockSpec(memory_space=pl.ANY)
-    opposite = pl.pallas_call(
+    passed_kv = pl.pallas_call(
         gate_kernel,
-        out_shape=shape(*sends[2].shape),
+        out_shape=shape(*far_kv.shape),
         in_specs=[anyspace] * 2,
         out_specs=anyspace,
         input_output_aliases={1: 0},
         compiler_params=pltpu.CompilerParams(vmem_limit_bytes=16 << 20),
         cost_estimate=pl.CostEstimate(flops=0, bytes_accessed=0, transcendentals=0),
         name="gate",
-    )(near_kv, sends[2])
-    sends = [*sends[:2], opposite, *sends[3:]]
+    )(near_kv, far_kv)
+    both_kv = swap(passed_kv, 1)
     got = [swap(piece, k) if k else piece for k, piece in zip(distances, sends)]
     half, allowed, keys_rest, vals_rest, key_cache, value_cache = pl.pallas_call(
-        functools.partial(lead_kernel, instances, capacity, per_group),
+        functools.partial(lead_kernel, instances, capacity, heads),
         out_shape=(
-            shape(slots, per_group * HD),
+            shape(slots, first * HD),
             shape(slots, 2 * rows),
             shape(instances * rows, HD),
             shape(instances * rows, 2 * HD),
@@ -356,15 +364,15 @@
         compiler_params=pltpu.CompilerParams(vmem_limit_bytes=24 << 20),
         cost_estimate=pl.CostEstimate(flops=1 << 29, bytes_accessed=2 << 20, transcendentals=1 << 19),
         name="attend_lead",
-    )(me, *got[:instances], own_kv, near_kv, far_kv, both_kv)
+    )(me, *got[:instances], own_kv, near_kv, passed_kv, both_kv)
     attended = pl.pallas_call(
-        functools.partial(rest_kernel, instances, capacity, per_group),
+        functools.partial(rest_kernel, instances, capacity, heads),
         out_shape=shape(slots, heads * HD),
         in_specs=[smem] + [vmem] * (instances + 4),
         out_specs=hbm,
         scratch_shapes=[
-            pltpu.VMEM((instances, tall, HD), jnp.bfloat16),
-            pltpu.VMEM((slots, per_group * HD), jnp.bfloat16),
+            pltpu.VMEM((instances, short, HD), jnp.bfloat16),
+            pltpu.VMEM((slots, (heads - first) * HD), jnp.bfloat16),
             pltpu.SemaphoreType.DMA((instances + 1,)),
         ],
         compiler_params=pltpu.CompilerParams(vmem_limit_bytes=24 << 20),
@@ -384,7 +392,7 @@
         and capacity % 16 == 0
         and rows == HD
         and keys.shape[1] == 2 * HD
-        and heads % 4 == 0
+        and heads % 16 == 0
     )
     form = few_instances if whole_tiles else many_instances
     return form(queries, keys, values, query_owner, cache_owner)

time: 32 us -> 30.8 us (0.963)
  waiting for transfers between devices: 10.5 us -> 9.05 us
  Pallas kernels: 3.83 us -> 4.52 us
  starting transfers between devices: 14.2 us -> 13.8 us
    ppermute x8, waiting for transfers between devices: 10.5 us -> 9.05 us  [swap(): return lax.ppermute(array, 'seq', [(i, i ^ k) for i in range(instances)])]
    pallas_call x3, Pallas kernels: 3.28 us -> 3.98 us  [the longest x1 2.39 us: few_instances(): pl.pallas_call(functools.partial(lead_kernel, instances, capacity, heads)...]
    ppermute x8, starting transfers between devices: 14.2 us -> 13.8 us  [swap(): return lax.ppermute(array, 'seq', [(i, i ^ k) for i in range(instances)])]
  transfers between devices with their start and end apart: 8 -> 8, of which waited for: 5 -> 4; matrix products, arithmetic and copies ran while one was open for 0% -> 0% of each run, Pallas kernels for 6% -> 10%
where the time goes in v12:
time: 30.8 us; the launch traced here: 30.6 us
  starting transfers between devices  13.8 us (45%)
  waiting for transfers between devices  9.05 us (29%)
  Pallas kernels  4.52 us (15%)
  local copies, waits for them, and re-layouts  2.6 us (8%)
  between operations  0.66 us (2%)
    ppermute x8, starting transfers between devices, swap(): return lax.ppermute(array, 'seq', [(i, i ^ k) for i in range(instances)])  13.8 us
    ppermute x8, waiting for transfers between devices, swap(): return lax.ppermute(array, 'seq', [(i, i ^ k) for i in range(instances)])  9.05 us
    unnamed x9, local copies, waits for them, and re-layouts  2.59 us
    pallas_call x1, Pallas kernels, few_instances(): pl.pallas_call(functools.partial(lead_kernel, instances, capacity, heads)...  2.39 us
    pallas_call x1, Pallas kernels, few_instances(): pl.pallas_call(functools.partial(rest_kernel, instances, capacity, heads)...  1.58 us
  transfers between devices with their start and end apart: 8, of which 4 were waited for; matrix products, arithmetic and copies ran while one was open for 0% of the time, Pallas kernels for 10%

profile of v12, /device:TPU:0, one launch (start us, length us, event | category | flops | bytes accessed | tf_op | source)
XLA Modules:
  0.0 30.6 jit_solution(7082140222946050274)
XLA Ops:
  0.6 0.0 copy-start.3
  0.6 0.9 %constant_dynamic-update-slice_fusion.1 = bf16[128,512]{1,0:T(8,128)(2,1)S(1)} fusion(bf16[128,256]{1,0:T(8,128)(2,1)} %param.6), kind=kLoop, calls=%fused_computation.1 | loop fusion | bytes 131072
  1.5 0.0 copy-done.3
  1.5 4.1 %collective-permute-start.6 = (bf16[128,512]{1,0:T(8,128)(2,1)S(1)}, bf16[128,512]{1,0:T(8,128)(2,1)S(1)}, u32[]{:S(2)}, u32[]{:S(2)}) collective-permute-start(bf16[128,512]{1,0:T(8,128)(2,1)S(1)} %constant_dynamic-update-slice_fusion.rest_4_), channel_id=1, source_target_pairs={{0,8},{4,12},{8,0},{12,4},{1,9},{5,13},{9,1},{13,5},{2,10},{6,14},... | collective-permute-start | bytes 393224 | tf_op jit(solution)/shard_map/ppermute | solution.py:311
  5.6 1.6 %collective-permute-start.5 = (bf16[128,512]{1,0:T(8,128)(2,1)S(1)}, bf16[128,512]{1,0:T(8,128)(2,1)S(1)}, u32[]{:S(2)}, u32[]{:S(2)}) collective-permute-start(bf16[128,512]{1,0:T(8,128)(2,1)S(1)} %constant_dynamic-update-slice_fusion.rest_4_), channel_id=1, source_target_pairs={{0,4},{4,0},{8,12},{12,8},{1,5},{5,1},{9,13},{13,9},{2,6},{6,2},{1... | collective-permute-start | bytes 393224 | tf_op jit(solution)/shard_map/ppermute | solution.py:311
  7.2 0.0 copy-start.1
  7.2 0.0 copy-start.2
  7.2 0.7 %copy-done.1 = s32[128,1]{0,1:T(1,128)S(1)} copy-done((s32[128,1]{0,1:T(1,128)S(1)}, s32[128,1]{0,1:T(1,128)}, u32[]{:S(2)}) %copy-start.1) | copy-done | bytes 536
  7.9 0.0 copy-done.2
  7.9 0.0 copy-start
  7.9 1.0 %copy-done = bf16[128,2048]{1,0:T(8,128)(2,1)S(1)} copy-done((bf16[128,2048]{1,0:T(8,128)(2,1)S(1)}, bf16[128,2048]{1,0:T(8,128)(2,1)}, u32[]{:S(2)}) %copy-start) | copy-done | bytes 524312
  8.9 0.5 %pack.1 = (bf16[784,128]{1,0:T(8,128)(2,1)S(1)}, bf16[784,128]{1,0:T(8,128)(2,1)S(1)}, bf16[544,128]{1,0:T(8,128)(2,1)S(1)}, bf16[544,128]{1,0:T(8,128)(2,1)S(1)...) custom-call(s32[1]{0:T(128)} %bitcast.me_ref, bf16[128,2048]{1,0:T(8,128)(2,1)S(1)} %copy-done, ...), custom_call_target="tpu_custom_call" | custom-call | flops 134217728 | bytes 2097152 | tf_op jit(solution)/shard_map/pack/pallas_call | solution.py:321
  9.5 0.5 %collective-permute-start = (bf16[784,128]{1,0:T(8,128)(2,1)S(1)}, bf16[784,128]{1,0:T(8,128)(2,1)S(1)}, u32[]{:S(2)}, u32[]{:S(2)}) collective-permute-start(bf16[784,128]{1,0:T(8,128)(2,1)S(1)} %get-tuple-element.16), channel_id=1, source_target_pairs={{0,4},{4,0},{8,12},{12,8},{1,5},{5,1},{9,13},{13,9},{2,6},{6,2},{1... | collective-permute-start | bytes 602120 | tf_op jit(solution)/shard_map/ppermute | solution.py:311
  10.0 0.1 collective-permute-start.3
  10.1 3.9 %collective-permute-start.4 = (bf16[544,128]{1,0:T(8,128)(2,1)S(1)}, bf16[544,128]{1,0:T(8,128)(2,1)S(1)}, u32[]{:S(2)}, u32[]{:S(2)}) collective-permute-start(bf16[544,128]{1,0:T(8,128)(2,1)S(1)} %get-tuple-element.20), channel_id=1, source_target_pairs={{0,12},{4,8},{8,4},{12,0},{1,13},{5,9},{9,5},{13,1},{2,14},{6,10},... | collective-permute-start | bytes 417800 | tf_op jit(solution)/shard_map/ppermute | solution.py:311
  13.9 0.0 collective-permute-done.6.far_ref
  13.9 0.0 collective-permute-done.5.near_ref.rest_5_
  13.9 0.9 %collective-permute-start.7 = (bf16[128,512]{1,0:T(8,128)(2,1)S(1)}, bf16[128,512]{1,0:T(8,128)(2,1)S(1)}, u32[]{:S(2)}, u32[]{:S(2)}) collective-permute-start(bf16[128,512]{1,0:T(8,128)(2,1)S(1)} %gate.1.rest_6_), channel_id=1, source_target_pairs={{0,4},{4,0},{8,12},{12,8},{1,5},{5,1},{9,13},{13,9},{2,6},{6,2},{1... | collective-permute-start | bytes 393224 | tf_op jit(solution)/shard_map/ppermute | solution.py:311
  14.8 1.4 %collective-permute-start.1 = (bf16[240,128]{1,0:T(8,128)(2,1)S(1)}, bf16[240,128]{1,0:T(8,128)(2,1)S(1)}, u32[]{:S(2)}, u32[]{:S(2)}) collective-permute-start(bf16[240,128]{1,0:T(8,128)(2,1)S(1)} %get-tuple-element.17), channel_id=1, source_target_pairs={{0,8},{4,12},{8,0},{12,4},{1,9},{5,13},{9,1},{13,5},{2,10},{6,14},... | collective-permute-start | bytes 184328 | tf_op jit(solution)/shard_map/ppermute | solution.py:311
  16.2 3.4 %collective-permute-done.3.rest_2_ = bf16[544,128]{1,0:T(8,128)(2,1)S(1)} collective-permute-done((bf16[544,128]{1,0:T(8,128)(2,1)S(1)}, bf16[544,128]{1,0:T(8,128)(2,1)S(1)}, u32[]{:S(2)}, u32[]{:S(2)}) %collective-permute-start.3) | collective-permute-done | bytes 139296 | tf_op jit(solution)/shard_map/ppermute | solution.py:311
  19.7 1.3 %collective-permute-start.2 = (bf16[240,128]{1,0:T(8,128)(2,1)S(1)}, bf16[240,128]{1,0:T(8,128)(2,1)S(1)}, u32[]{:S(2)}, u32[]{:S(2)}) collective-permute-start(bf16[240,128]{1,0:T(8,128)(2,1)S(1)} %get-tuple-element.18), channel_id=1, source_target_pairs={{0,12},{4,8},{8,4},{12,0},{1,13},{5,9},{9,5},{13,1},{2,14},{6,10},... | collective-permute-start | bytes 184328 | tf_op jit(solution)/shard_map/ppermute | solution.py:311
  21.0 3.4 %collective-permute-done.4.rest_3_ = bf16[544,128]{1,0:T(8,128)(2,1)S(1)} collective-permute-done((bf16[544,128]{1,0:T(8,128)(2,1)S(1)}, bf16[544,128]{1,0:T(8,128)(2,1)S(1)}, u32[]{:S(2)}, u32[]{:S(2)}) %collective-permute-start.4) | collective-permute-done | bytes 139296 | tf_op jit(solution)/shard_map/ppermute | solution.py:311
  24.5 0.0 collective-permute-done.rest_1_
  24.5 1.5 %collective-permute-done.7.rest_7_ = bf16[128,512]{1,0:T(8,128)(2,1)S(1)} collective-permute-done((bf16[128,512]{1,0:T(8,128)(2,1)S(1)}, bf16[128,512]{1,0:T(8,128)(2,1)S(1)}, u32[]{:S(2)}, u32[]{:S(2)}) %collective-permute-start.7) | collective-permute-done | bytes 131104 | tf_op jit(solution)/shard_map/ppermute | solution.py:311
  26.0 2.4 %attend_lead.1 = (bf16[192,1408]{1,0:T(8,128)(2,1)S(1)}, bf16[192,256]{1,0:T(8,128)(2,1)S(1)}, bf16[512,128]{1,0:T(8,128)(2,1)S(1)}, bf16[512,256]{1,0:T(8,128)(...) custom-call(s32[1]{0:T(128)} %bitcast.me_ref, bf16[784,128]{1,0:T(8,128)(2,1)S(1)} %get-tuple-element.15.rest_0_, ...), custom_call_target="tpu_custom_call" | custom-call | flops 536870912 | bytes 2097152 | tf_op jit(solution)/shard_map/attend_lead/pallas_call | solution.py:347
  28.4 0.6 %collective-permute-done.1.rest_2_ = bf16[240,128]{1,0:T(8,128)(2,1)S(1)} collective-permute-done((bf16[240,128]{1,0:T(8,128)(2,1)S(1)}, bf16[240,128]{1,0:T(8,128)(2,1)S(1)}, u32[]{:S(2)}, u32[]{:S(2)}) %collective-permute-start.1) | collective-permute-done | bytes 61472 | tf_op jit(solution)/shard_map/ppermute | solution.py:311
  29.0 0.0 collective-permute-done.2.rest_3_
  29.0 1.6 %attend_rest.1 = bf16[192,2048]{1,0:T(8,128)(2,1)} custom-call(s32[1]{0:T(128)} %bitcast.me_ref, bf16[784,128]{1,0:T(8,128)(2,1)S(1)} %get-tuple-element.15.rest_0_, bf16[784,128]{1,0:T(8,128)(2,1)S(1)} %collective-permute-done.rest_1_, bf16[240,128]{1,0:T(8,128)(2,1)S(1)} %collective-permute-done.1.rest_2_, ...), custom_call_target="tpu_custom_call" | custom-call | flops 536870912 | bytes 2097152 | tf_op jit(solution)/shard_map/attend_rest/pallas_call | solution.py:368
  (2 shorter events, 0.0 us)
Async XLA Ops:
  0.6 0.9 %copy-start.3 = (bf16[128,256]{1,0:T(8,128)(2,1)S(1)}, bf16[128,256]{1,0:T(8,128)(2,1)}, u32[]{:S(2)}) copy-start(bf16[128,256]{1,0:T(8,128)(2,1)} %param.7) | copy-start | bytes 196612
  1.5 12.4 %collective-permute-start.6 = (bf16[128,512]{1,0:T(8,128)(2,1)S(1)}, bf16[128,512]{1,0:T(8,128)(2,1)S(1)}, u32[]{:S(2)}, u32[]{:S(2)}) collective-permute-start(bf16[128,512]{1,0:T(8,128)(2,1)S(1)} %constant_dynamic-update-slice_fusion.rest_4_), channel_id=1, source_target_pairs={{0,8},{4,12},{8,0},{12,4},{1,9},{5,13},{9,1},{13,5},{2,10},{6,14},... | collective-permute-start | bytes 393224 | tf_op jit(solution)/shard_map/ppermute | solution.py:311
  5.6 8.3 %collective-permute-start.5 = (bf16[128,512]{1,0:T(8,128)(2,1)S(1)}, bf16[128,512]{1,0:T(8,128)(2,1)S(1)}, u32[]{:S(2)}, u32[]{:S(2)}) collective-permute-start(bf16[128,512]{1,0:T(8,128)(2,1)S(1)} %constant_dynamic-update-slice_fusion.rest_4_), channel_id=1, source_target_pairs={{0,4},{4,0},{8,12},{12,8},{1,5},{5,1},{9,13},{13,9},{2,6},{6,2},{1... | collective-permute-start | bytes 393224 | tf_op jit(solution)/shard_map/ppermute | solution.py:311
  7.2 0.7 %copy-start.1 = (s32[128,1]{0,1:T(1,128)S(1)}, s32[128,1]{0,1:T(1,128)}, u32[]{:S(2)}) copy-start(s32[128,1]{0,1:T(1,128)} %param.8) | copy-start | bytes 1540
  7.2 0.7 %copy-start.2 = (s32[128,1]{0,1:T(1,128)S(1)}, s32[128,1]{0,1:T(1,128)}, u32[]{:S(2)}) copy-start(s32[128,1]{0,1:T(1,128)} %param.9) | copy-start | bytes 1540
  7.9 1.0 %copy-start = (bf16[128,2048]{1,0:T(8,128)(2,1)S(1)}, bf16[128,2048]{1,0:T(8,128)(2,1)}, u32[]{:S(2)}) copy-start(bf16[128,2048]{1,0:T(8,128)(2,1)} %q_hbm.1) | copy-start | bytes 1572868
  9.5 15.0 %collective-permute-start = (bf16[784,128]{1,0:T(8,128)(2,1)S(1)}, bf16[784,128]{1,0:T(8,128)(2,1)S(1)}, u32[]{:S(2)}, u32[]{:S(2)}) collective-permute-start(bf16[784,128]{1,0:T(8,128)(2,1)S(1)} %get-tuple-element.16), channel_id=1, source_target_pairs={{0,4},{4,0},{8,12},{12,8},{1,5},{5,1},{9,13},{13,9},{2,6},{6,2},{1... | collective-permute-start | bytes 602120 | tf_op jit(solution)/shard_map/ppermute | solution.py:311
  10.0 9.7 %collective-permute-start.3 = (bf16[544,128]{1,0:T(8,128)(2,1)S(1)}, bf16[544,128]{1,0:T(8,128)(2,1)S(1)}, u32[]{:S(2)}, u32[]{:S(2)}) collective-permute-start(bf16[544,128]{1,0:T(8,128)(2,1)S(1)} %get-tuple-element.19), channel_id=1, source_target_pairs={{0,8},{4,12},{8,0},{12,4},{1,9},{5,13},{9,1},{13,5},{2,10},{6,14},... | collective-permute-start | bytes 417800 | tf_op jit(solution)/shard_map/ppermute | solution.py:311
  10.1 14.4 %collective-permute-start.4 = (bf16[544,128]{1,0:T(8,128)(2,1)S(1)}, bf16[544,128]{1,0:T(8,128)(2,1)S(1)}, u32[]{:S(2)}, u32[]{:S(2)}) collective-permute-start(bf16[544,128]{1,0:T(8,128)(2,1)S(1)} %get-tuple-element.20), channel_id=1, source_target_pairs={{0,12},{4,8},{8,4},{12,0},{1,13},{5,9},{9,5},{13,1},{2,14},{6,10},... | collective-permute-start | bytes 417800 | tf_op jit(solution)/shard_map/ppermute | solution.py:311
  13.9 12.0 %collective-permute-start.7 = (bf16[128,512]{1,0:T(8,128)(2,1)S(1)}, bf16[128,512]{1,0:T(8,128)(2,1)S(1)}, u32[]{:S(2)}, u32[]{:S(2)}) collective-permute-start(bf16[128,512]{1,0:T(8,128)(2,1)S(1)} %gate.1.rest_6_), channel_id=1, source_target_pairs={{0,4},{4,0},{8,12},{12,8},{1,5},{5,1},{9,13},{13,9},{2,6},{6,2},{1... | collective-permute-start | bytes 393224 | tf_op jit(solution)/shard_map/ppermute | solution.py:311
  14.8 14.2 %collective-permute-start.1 = (bf16[240,128]{1,0:T(8,128)(2,1)S(1)}, bf16[240,128]{1,0:T(8,128)(2,1)S(1)}, u32[]{:S(2)}, u32[]{:S(2)}) collective-permute-start(bf16[240,128]{1,0:T(8,128)(2,1)S(1)} %get-tuple-element.17), channel_id=1, source_target_pairs={{0,8},{4,12},{8,0},{12,4},{1,9},{5,13},{9,1},{13,5},{2,10},{6,14},... | collective-permute-start | bytes 184328 | tf_op jit(solution)/shard_map/ppermute | solution.py:311
  19.7 9.4 %collective-permute-start.2 = (bf16[240,128]{1,0:T(8,128)(2,1)S(1)}, bf16[240,128]{1,0:T(8,128)(2,1)S(1)}, u32[]{:S(2)}, u32[]{:S(2)}) collective-permute-start(bf16[240,128]{1,0:T(8,128)(2,1)S(1)} %get-tuple-element.18), channel_id=1, source_target_pairs={{0,12},{4,8},{8,4},{12,0},{1,13},{5,9},{9,5},{13,1},{2,14},{6,10},... | collective-permute-start | bytes 184328 | tf_op jit(solution)/shard_map/ppermute | solution.py:311

commit v13 on v12

--- a/solution.py
+++ b/solution.py
@@ -147,7 +147,7 @@
 
 
 def lead_heads(heads):
-    return heads // 2 + 3 * heads // 16
+    return heads // 2 + 5 * heads // 16
 
 
 def gate_kernel(near_ref, far_ref, through_ref):

time: 30.8 us -> 32.1 us (1.042)
  waiting for transfers between devices: 9.05 us -> 11.8 us
  starting transfers between devices: 13.8 us -> 12.4 us
    ppermute x8, waiting for transfers between devices: 9.05 us -> 11.8 us  [swap(): return lax.ppermute(array, 'seq', [(i, i ^ k) for i in range(instances)])]
    ppermute x8, starting transfers between devices: 13.8 us -> 12.4 us  [swap(): return lax.ppermute(array, 'seq', [(i, i ^ k) for i in range(instances)])]
  transfers between devices with their start and end apart: 8 -> 8, of which waited for: 4 -> 4; matrix products, arithmetic and copies ran while one was open for 0% -> 0% of each run, Pallas kernels for 10% -> 9%
where the time goes in v13:
time: 32.1 us; the launch traced here: 31.9 us
  starting transfers between devices  12.4 us (39%)
  waiting for transfers between devices  11.8 us (37%)
  Pallas kernels  4.37 us (14%)
  local copies, waits for them, and re-layouts  2.6 us (8%)
  between operations  0.66 us (2%)
    ppermute x8, starting transfers between devices, swap(): return lax.ppermute(array, 'seq', [(i, i ^ k) for i in range(instances)])  12.4 us
    ppermute x8, waiting for transfers between devices, swap(): return lax.ppermute(array, 'seq', [(i, i ^ k) for i in range(instances)])  11.8 us
    unnamed x9, local copies, waits for them, and re-layouts  2.59 us
    pallas_call x1, Pallas kernels, few_instances(): pl.pallas_call(functools.partial(lead_kernel, instances, capacity, heads)...  2.39 us
    pallas_call x1, Pallas kernels, few_instances(): pl.pallas_call(functools.partial(rest_kernel, instances, capacity, heads)...  1.43 us
  transfers between devices with their start and end apart: 8, of which 4 were waited for; matrix products, arithmetic and copies ran while one was open for 0% of the time, Pallas kernels for 9%

profile of v13, /device:TPU:0, one launch (start us, length us, event | category | flops | bytes accessed | tf_op | source)
XLA Modules:
  0.0 31.9 jit_solution(14640781551029008112)
XLA Ops:
  0.6 0.0 copy-start.3
  0.6 0.9 %constant_dynamic-update-slice_fusion.1 = bf16[128,512]{1,0:T(8,128)(2,1)S(1)} fusion(bf16[128,256]{1,0:T(8,128)(2,1)} %param.6), kind=kLoop, calls=%fused_computation.1 | loop fusion | bytes 131072
  1.5 0.0 copy-done.3
  1.5 4.1 %collective-permute-start.6 = (bf16[128,512]{1,0:T(8,128)(2,1)S(1)}, bf16[128,512]{1,0:T(8,128)(2,1)S(1)}, u32[]{:S(2)}, u32[]{:S(2)}) collective-permute-start(bf16[128,512]{1,0:T(8,128)(2,1)S(1)} %constant_dynamic-update-slice_fusion.rest_4_), channel_id=1, source_target_pairs={{0,8},{4,12},{8,0},{12,4},{1,9},{5,13},{9,1},{13,5},{2,10},{6,14},... | collective-permute-start | bytes 393224 | tf_op jit(solution)/shard_map/ppermute | solution.py:311
  5.6 1.6 %collective-permute-start.5 = (bf16[128,512]{1,0:T(8,128)(2,1)S(1)}, bf16[128,512]{1,0:T(8,128)(2,1)S(1)}, u32[]{:S(2)}, u32[]{:S(2)}) collective-permute-start(bf16[128,512]{1,0:T(8,128)(2,1)S(1)} %constant_dynamic-update-slice_fusion.rest_4_), channel_id=1, source_target_pairs={{0,4},{4,0},{8,12},{12,8},{1,5},{5,1},{9,13},{13,9},{2,6},{6,2},{1... | collective-permute-start | bytes 393224 | tf_op jit(solution)/shard_map/ppermute | solution.py:311
  7.2 0.0 copy-start.1
  7.2 0.0 copy-start.2
  7.2 0.7 %copy-done.1 = s32[128,1]{0,1:T(1,128)S(1)} copy-done((s32[128,1]{0,1:T(1,128)S(1)}, s32[128,1]{0,1:T(1,128)}, u32[]{:S(2)}) %copy-start.1) | copy-done | bytes 536
  7.9 0.0 copy-done.2
  7.9 0.0 copy-start
  7.9 1.0 %copy-done = bf16[128,2048]{1,0:T(8,128)(2,1)S(1)} copy-done((bf16[128,2048]{1,0:T(8,128)(2,1)S(1)}, bf16[128,2048]{1,0:T(8,128)(2,1)}, u32[]{:S(2)}) %copy-start) | copy-done | bytes 524312
  8.9 0.5 %pack.1 = (bf16[784,128]{1,0:T(8,128)(2,1)S(1)}, bf16[784,128]{1,0:T(8,128)(2,1)S(1)}, bf16[640,128]{1,0:T(8,128)(2,1)S(1)}, bf16[640,128]{1,0:T(8,128)(2,1)S(1)...) custom-call(s32[1]{0:T(128)} %bitcast.me_ref, bf16[128,2048]{1,0:T(8,128)(2,1)S(1)} %copy-done, ...), custom_call_target="tpu_custom_call" | custom-call | flops 134217728 | bytes 2097152 | tf_op jit(solution)/shard_map/pack/pallas_call | solution.py:321
  9.5 0.5 %collective-permute-start = (bf16[784,128]{1,0:T(8,128)(2,1)S(1)}, bf16[784,128]{1,0:T(8,128)(2,1)S(1)}, u32[]{:S(2)}, u32[]{:S(2)}) collective-permute-start(bf16[784,128]{1,0:T(8,128)(2,1)S(1)} %get-tuple-element.16), channel_id=1, source_target_pairs={{0,4},{4,0},{8,12},{12,8},{1,5},{5,1},{9,13},{13,9},{2,6},{6,2},{1... | collective-permute-start | bytes 602120 | tf_op jit(solution)/shard_map/ppermute | solution.py:311
  10.0 0.1 collective-permute-start.3
  10.1 3.9 %collective-permute-start.4 = (bf16[640,128]{1,0:T(8,128)(2,1)S(1)}, bf16[640,128]{1,0:T(8,128)(2,1)S(1)}, u32[]{:S(2)}, u32[]{:S(2)}) collective-permute-start(bf16[640,128]{1,0:T(8,128)(2,1)S(1)} %get-tuple-element.20), channel_id=1, source_target_pairs={{0,12},{4,8},{8,4},{12,0},{1,13},{5,9},{9,5},{13,1},{2,14},{6,10},... | collective-permute-start | bytes 491528 | tf_op jit(solution)/shard_map/ppermute | solution.py:311
  13.9 0.0 collective-permute-done.6.far_ref
  13.9 0.0 collective-permute-done.5.near_ref.rest_5_
  13.9 0.9 %collective-permute-start.7 = (bf16[128,512]{1,0:T(8,128)(2,1)S(1)}, bf16[128,512]{1,0:T(8,128)(2,1)S(1)}, u32[]{:S(2)}, u32[]{:S(2)}) collective-permute-start(bf16[128,512]{1,0:T(8,128)(2,1)S(1)} %gate.1.rest_6_), channel_id=1, source_target_pairs={{0,4},{4,0},{8,12},{12,8},{1,5},{5,1},{9,13},{13,9},{2,6},{6,2},{1... | collective-permute-start | bytes 393224 | tf_op jit(solution)/shard_map/ppermute | solution.py:311
  14.8 1.4 %collective-permute-start.1 = (bf16[144,128]{1,0:T(8,128)(2,1)S(1)}, bf16[144,128]{1,0:T(8,128)(2,1)S(1)}, u32[]{:S(2)}, u32[]{:S(2)}) collective-permute-start(bf16[144,128]{1,0:T(8,128)(2,1)S(1)} %get-tuple-element.17), channel_id=1, source_target_pairs={{0,8},{4,12},{8,0},{12,4},{1,9},{5,13},{9,1},{13,5},{2,10},{6,14},... | collective-permute-start | bytes 110600 | tf_op jit(solution)/shard_map/ppermute | solution.py:311
  16.2 8.5 %collective-permute-done.3.rest_2_ = bf16[640,128]{1,0:T(8,128)(2,1)S(1)} collective-permute-done((bf16[640,128]{1,0:T(8,128)(2,1)S(1)}, bf16[640,128]{1,0:T(8,128)(2,1)S(1)}, u32[]{:S(2)}, u32[]{:S(2)}) %collective-permute-start.3) | collective-permute-done | bytes 163872 | tf_op jit(solution)/shard_map/ppermute | solution.py:311
  24.7 0.0 collective-permute-start.2
  24.7 0.8 %collective-permute-done.4.rest_3_ = bf16[640,128]{1,0:T(8,128)(2,1)S(1)} collective-permute-done((bf16[640,128]{1,0:T(8,128)(2,1)S(1)}, bf16[640,128]{1,0:T(8,128)(2,1)S(1)}, u32[]{:S(2)}, u32[]{:S(2)}) %collective-permute-start.4) | collective-permute-done | bytes 163872 | tf_op jit(solution)/shard_map/ppermute | solution.py:311
  25.5 0.0 collective-permute-done.rest_1_
  25.5 1.2 %collective-permute-done.7.rest_7_ = bf16[128,512]{1,0:T(8,128)(2,1)S(1)} collective-permute-done((bf16[128,512]{1,0:T(8,128)(2,1)S(1)}, bf16[128,512]{1,0:T(8,128)(2,1)S(1)}, u32[]{:S(2)}, u32[]{:S(2)}) %collective-permute-start.7) | collective-permute-done | bytes 131104 | tf_op jit(solution)/shard_map/ppermute | solution.py:311
  26.8 2.4 %attend_lead.1 = (bf16[192,1664]{1,0:T(8,128)(2,1)S(1)}, bf16[192,256]{1,0:T(8,128)(2,1)S(1)}, bf16[512,128]{1,0:T(8,128)(2,1)S(1)}, bf16[512,256]{1,0:T(8,128)(...) custom-call(s32[1]{0:T(128)} %bitcast.me_ref, bf16[784,128]{1,0:T(8,128)(2,1)S(1)} %get-tuple-element.15.rest_0_, ...), custom_call_target="tpu_custom_call" | custom-call | flops 536870912 | bytes 2097152 | tf_op jit(solution)/shard_map/attend_lead/pallas_call | solution.py:347
  29.2 0.0 collective-permute-done.1.rest_2_
  29.2 1.3 %collective-permute-done.2.rest_3_ = bf16[144,128]{1,0:T(8,128)(2,1)S(1)} collective-permute-done((bf16[144,128]{1,0:T(8,128)(2,1)S(1)}, bf16[144,128]{1,0:T(8,128)(2,1)S(1)}, u32[]{:S(2)}, u32[]{:S(2)}) %collective-permute-start.2) | collective-permute-done | bytes 36896 | tf_op jit(solution)/shard_map/ppermute | solution.py:311
  30.5 1.4 %attend_rest.1 = bf16[192,2048]{1,0:T(8,128)(2,1)} custom-call(s32[1]{0:T(128)} %bitcast.me_ref, bf16[784,128]{1,0:T(8,128)(2,1)S(1)} %get-tuple-element.15.rest_0_, bf16[784,128]{1,0:T(8,128)(2,1)S(1)} %collective-permute-done.rest_1_, bf16[144,128]{1,0:T(8,128)(2,1)S(1)} %collective-permute-done.1.rest_2_, ...), custom_call_target="tpu_custom_call" | custom-call | flops 536870912 | bytes 2097152 | tf_op jit(solution)/shard_map/attend_rest/pallas_call | solution.py:368
  (2 shorter events, 0.0 us)
Async XLA Ops:
  0.6 0.9 %copy-start.3 = (bf16[128,256]{1,0:T(8,128)(2,1)S(1)}, bf16[128,256]{1,0:T(8,128)(2,1)}, u32[]{:S(2)}) copy-start(bf16[128,256]{1,0:T(8,128)(2,1)} %param.7) | copy-start | bytes 196612
  1.5 12.4 %collective-permute-start.6 = (bf16[128,512]{1,0:T(8,128)(2,1)S(1)}, bf16[128,512]{1,0:T(8,128)(2,1)S(1)}, u32[]{:S(2)}, u32[]{:S(2)}) collective-permute-start(bf16[128,512]{1,0:T(8,128)(2,1)S(1)} %constant_dynamic-update-slice_fusion.rest_4_), channel_id=1, source_target_pairs={{0,8},{4,12},{8,0},{12,4},{1,9},{5,13},{9,1},{13,5},{2,10},{6,14},... | collective-permute-start | bytes 393224 | tf_op jit(solution)/shard_map/ppermute | solution.py:311
  5.6 8.3 %collective-permute-start.5 = (bf16[128,512]{1,0:T(8,128)(2,1)S(1)}, bf16[128,512]{1,0:T(8,128)(2,1)S(1)}, u32[]{:S(2)}, u32[]{:S(2)}) collective-permute-start(bf16[128,512]{1,0:T(8,128)(2,1)S(1)} %constant_dynamic-update-slice_fusion.rest_4_), channel_id=1, source_target_pairs={{0,4},{4,0},{8,12},{12,8},{1,5},{5,1},{9,13},{13,9},{2,6},{6,2},{1... | collective-permute-start | bytes 393224 | tf_op jit(solution)/shard_map/ppermute | solution.py:311
  7.2 0.7 %copy-start.1 = (s32[128,1]{0,1:T(1,128)S(1)}, s32[128,1]{0,1:T(1,128)}, u32[]{:S(2)}) copy-start(s32[128,1]{0,1:T(1,128)} %param.8) | copy-start | bytes 1540
  7.2 0.7 %copy-start.2 = (s32[128,1]{0,1:T(1,128)S(1)}, s32[128,1]{0,1:T(1,128)}, u32[]{:S(2)}) copy-start(s32[128,1]{0,1:T(1,128)} %param.9) | copy-start | bytes 1540
  7.9 1.0 %copy-start = (bf16[128,2048]{1,0:T(8,128)(2,1)S(1)}, bf16[128,2048]{1,0:T(8,128)(2,1)}, u32[]{:S(2)}) copy-start(bf16[128,2048]{1,0:T(8,128)(2,1)} %q_hbm.1) | copy-start | bytes 1572868
  9.5 16.0 %collective-permute-start = (bf16[784,128]{1,0:T(8,128)(2,1)S(1)}, bf16[784,128]{1,0:T(8,128)(2,1)S(1)}, u32[]{:S(2)}, u32[]{:S(2)}) collective-permute-start(bf16[784,128]{1,0:T(8,128)(2,1)S(1)} %get-tuple-element.16), channel_id=1, source_target_pairs={{0,4},{4,0},{8,12},{12,8},{1,5},{5,1},{9,13},{13,9},{2,6},{6,2},{1... | collective-permute-start | bytes 602120 | tf_op jit(solution)/shard_map/ppermute | solution.py:311
  10.0 14.7 %collective-permute-start.3 = (bf16[640,128]{1,0:T(8,128)(2,1)S(1)}, bf16[640,128]{1,0:T(8,128)(2,1)S(1)}, u32[]{:S(2)}, u32[]{:S(2)}) collective-permute-start(bf16[640,128]{1,0:T(8,128)(2,1)S(1)} %get-tuple-element.19), channel_id=1, source_target_pairs={{0,8},{4,12},{8,0},{12,4},{1,9},{5,13},{9,1},{13,5},{2,10},{6,14},... | collective-permute-start | bytes 491528 | tf_op jit(solution)/shard_map/ppermute | solution.py:311
  10.1 15.5 %collective-permute-start.4 = (bf16[640,128]{1,0:T(8,128)(2,1)S(1)}, bf16[640,128]{1,0:T(8,128)(2,1)S(1)}, u32[]{:S(2)}, u32[]{:S(2)}) collective-permute-start(bf16[640,128]{1,0:T(8,128)(2,1)S(1)} %get-tuple-element.20), channel_id=1, source_target_pairs={{0,12},{4,8},{8,4},{12,0},{1,13},{5,9},{9,5},{13,1},{2,14},{6,10},... | collective-permute-start | bytes 491528 | tf_op jit(solution)/shard_map/ppermute | solution.py:311
  13.9 12.8 %collective-permute-start.7 = (bf16[128,512]{1,0:T(8,128)(2,1)S(1)}, bf16[128,512]{1,0:T(8,128)(2,1)S(1)}, u32[]{:S(2)}, u32[]{:S(2)}) collective-permute-start(bf16[128,512]{1,0:T(8,128)(2,1)S(1)} %gate.1.rest_6_), channel_id=1, source_target_pairs={{0,4},{4,0},{8,12},{12,8},{1,5},{5,1},{9,13},{13,9},{2,6},{6,2},{1... | collective-permute-start | bytes 393224 | tf_op jit(solution)/shard_map/ppermute | solution.py:311
  14.8 14.3 %collective-permute-start.1 = (bf16[144,128]{1,0:T(8,128)(2,1)S(1)}, bf16[144,128]{1,0:T(8,128)(2,1)S(1)}, u32[]{:S(2)}, u32[]{:S(2)}) collective-permute-start(bf16[144,128]{1,0:T(8,128)(2,1)S(1)} %get-tuple-element.17), channel_id=1, source_target_pairs={{0,8},{4,12},{8,0},{12,4},{1,9},{5,13},{9,1},{13,5},{2,10},{6,14},... | collective-permute-start | bytes 110600 | tf_op jit(solution)/shard_map/ppermute | solution.py:311
  24.7 5.8 %collective-permute-start.2 = (bf16[144,128]{1,0:T(8,128)(2,1)S(1)}, bf16[144,128]{1,0:T(8,128)(2,1)S(1)}, u32[]{:S(2)}, u32[]{:S(2)}) collective-permute-start(bf16[144,128]{1,0:T(8,128)(2,1)S(1)} %get-tuple-element.18), channel_id=1, source_target_pairs={{0,12},{4,8},{8,4},{12,0},{1,13},{5,9},{9,5},{13,1},{2,14},{6,10},... | collective-permute-start | bytes 110600 | tf_op jit(solution)/shard_map/ppermute | solution.py:311

commit v14 on v12

--- a/solution.py
+++ b/solution.py
@@ -224,7 +224,7 @@
 def lead_kernel(instances, capacity, heads, me_ref, *rest):
     got, rest = rest[:instances], rest[instances:]
     blocks_of, rest = rest[:instances], rest[instances:]
-    half_ref, allowed_ref, keys_ref, vals_ref, kc_ref, vc_ref, wanted_ref, keys, vals = rest
+    att_hbm, allowed_ref, keys_ref, vals_ref, kc_ref, vc_ref, wanted_ref, keys, vals, half_ref, sent = rest
     rows = HD
     tall = lead_heads(heads) * capacity
     me = me_ref[0]
@@ -262,21 +262,30 @@
             jnp.bfloat16
         )
 
+    first = lead_heads(heads)
+    copies = []
+
     def store(s, slots, h, value):
         half_ref[slots, h * HD : (h + 1) * HD] = value
-
-    halves = (slice(0, heads // 2), keys, vals), (slice(heads // 2, lead_heads(heads)), keys_ref, vals_ref)
+        if h == first - 1:
+            copy = pltpu.make_async_copy(
+                half_ref.at[slots, :], att_hbm.at[slots, : first * HD], sent.at[s]
+            )
+            copy.start()
+            copies.append(copy)
+
+    halves = (slice(0, heads // 2), keys, vals), (slice(heads // 2, first), keys_ref, vals_ref)
     for span, k_ref, v_ref in halves:
         attend_head(instances, capacity, span, wanted_ref, k_ref, v_ref, allowed_ref, store)
+    for copy in copies:
+        copy.wait()
 
 
 def rest_kernel(instances, capacity, heads, me_ref, *rest):
     got, rest = rest[:instances], rest[instances:]
-    half_ref, allowed_ref, keys_ref, vals_ref, att_hbm, wanted_ref, mine_ref, sent = rest
+    _, allowed_ref, keys_ref, vals_ref, att_hbm, wanted_ref, mine_ref, sent = rest
     first = lead_heads(heads)
     count = heads - first
-    early = pltpu.make_async_copy(half_ref, att_hbm.at[:, : first * HD], sent.at[instances])
-    early.start()
     for k, piece in zip((0, 1, *SECOND), got):
         start = 0 if k in SECOND else first * capacity + 16
         wanted_ref[jnp.bitwise_xor(me_ref[0], k)] = piece[start : start + count * capacity, :]
@@ -294,7 +303,7 @@
     attend_head(
         instances, capacity, slice(0, count), wanted_ref, keys_ref, vals_ref, allowed_ref, store
     )
-    for copy in [early, *copies]:
+    for copy in copies:
         copy.wait()
 
 
@@ -344,10 +353,10 @@
     )(near_kv, far_kv)
     both_kv = swap(passed_kv, 1)
     got = [swap(piece, k) if k else piece for k, piece in zip(distances, sends)]
-    half, allowed, keys_rest, vals_rest, key_cache, value_cache = pl.pallas_call(
+    attended, allowed, keys_rest, vals_rest, key_cache, value_cache = pl.pallas_call(
         functools.partial(lead_kernel, instances, capacity, heads),
         out_shape=(
-            shape(slots, first * HD),
+            shape(slots, heads * HD),
             shape(slots, 2 * rows),
             shape(instances * rows, HD),
             shape(instances * rows, 2 * HD),
@@ -355,11 +364,13 @@
             shape(slots, 2 * HD),
         ),
         in_specs=[smem] + [vmem] * (2 * instances),
-        out_specs=(vmem,) * 6,
+        out_specs=(hbm,) + (vmem,) * 5,
         scratch_shapes=[
             pltpu.VMEM((instances, tall + 16, HD), jnp.bfloat16),
             pltpu.VMEM((instances * rows, HD), jnp.bfloat16),
             pltpu.VMEM((instances * rows, 2 * HD), jnp.bfloat16),
+            pltpu.VMEM((slots, first * HD), jnp.bfloat16),
+            pltpu.SemaphoreType.DMA((instances,)),
         ],
         compiler_params=pltpu.CompilerParams(vmem_limit_bytes=24 << 20),
         cost_estimate=pl.CostEstimate(flops=1 << 29, bytes_accessed=2 << 20, transcendentals=1 << 19),
@@ -368,17 +379,18 @@
     attended = pl.pallas_call(
         functools.partial(rest_kernel, instances, capacity, heads),
         out_shape=shape(slots, heads * HD),
-        in_specs=[smem] + [vmem] * (instances + 4),
+        in_specs=[smem] + [vmem] * instances + [hbm] + [vmem] * 3,
         out_specs=hbm,
+        input_output_aliases={instances + 1: 0},
         scratch_shapes=[
             pltpu.VMEM((instances, short, HD), jnp.bfloat16),
             pltpu.VMEM((slots, (heads - first) * HD), jnp.bfloat16),
-            pltpu.SemaphoreType.DMA((instances + 1,)),
+            pltpu.SemaphoreType.DMA((instances,)),
         ],
         compiler_params=pltpu.CompilerParams(vmem_limit_bytes=24 << 20),
         cost_estimate=pl.CostEstimate(flops=1 << 29, bytes_accessed=2 << 20, transcendentals=1 << 19),
         name="attend_rest",
-    )(me, *got[:2], *got[instances:], half, allowed, keys_rest, vals_rest)
+    )(me, *got[:2], *got[instances:], attended, allowed, keys_rest, vals_rest)
     return (attended, key_cache, value_cache)
 
 

time: 30.8 us -> 31.1 us (level)
  Pallas kernels: 4.52 us -> 5.46 us
  waiting for transfers between devices: 9.05 us -> 8.41 us
    pallas_call x1, Pallas kernels: 2.39 us -> 3.33 us  [few_instances(): pl.pallas_call(functools.partial(lead_kernel, instances, capacity, heads)...]
    ppermute x8, waiting for transfers between devices: 9.05 us -> 8.41 us  [swap(): return lax.ppermute(array, 'seq', [(i, i ^ k) for i in range(instances)])]
  transfers between devices with their start and end apart: 8 -> 8, of which waited for: 4 -> 3; matrix products, arithmetic and copies ran while one was open for 0% -> 0% of each run, Pallas kernels for 10% -> 13%
where the time goes in v14:
time: 31.1 us; the launch traced here: 30.9 us
  starting transfers between devices  13.8 us (44%)
  waiting for transfers between devices  8.41 us (27%)
  Pallas kernels  5.46 us (18%)
  local copies, waits for them, and re-layouts  2.6 us (8%)
  between operations  0.69 us (2%)
    ppermute x8, starting transfers between devices, swap(): return lax.ppermute(array, 'seq', [(i, i ^ k) for i in range(instances)])  13.8 us
    ppermute x8, waiting for transfers between devices, swap(): return lax.ppermute(array, 'seq', [(i, i ^ k) for i in range(instances)])  8.41 us
    pallas_call x1, Pallas kernels, few_instances(): pl.pallas_call(functools.partial(lead_kernel, instances, capacity, heads)...  3.33 us
    unnamed x9, local copies, waits for them, and re-layouts  2.59 us
    pallas_call x1, Pallas kernels, few_instances(): pl.pallas_call(functools.partial(rest_kernel, instances, capacity, heads)...  1.58 us
  transfers between devices with their start and end apart: 8, of which 3 were waited for; matrix products, arithmetic and copies ran while one was open for 0% of the time, Pallas kernels for 13%

profile of v14, /device:TPU:0, one launch (start us, length us, event | category | flops | bytes accessed | tf_op | source)
XLA Modules:
  0.0 30.9 jit_solution(16918420000201393524)
XLA Ops:
  0.6 0.0 copy-start.3
  0.6 0.9 %constant_dynamic-update-slice_fusion.1 = bf16[128,512]{1,0:T(8,128)(2,1)S(1)} fusion(bf16[128,256]{1,0:T(8,128)(2,1)} %param.6), kind=kLoop, calls=%fused_computation.1 | loop fusion | bytes 131072
  1.5 0.0 copy-done.3
  1.5 4.1 %collective-permute-start.6 = (bf16[128,512]{1,0:T(8,128)(2,1)S(1)}, bf16[128,512]{1,0:T(8,128)(2,1)S(1)}, u32[]{:S(2)}, u32[]{:S(2)}) collective-permute-start(bf16[128,512]{1,0:T(8,128)(2,1)S(1)} %constant_dynamic-update-slice_fusion.rest_4_), channel_id=1, source_target_pairs={{0,8},{4,12},{8,0},{12,4},{1,9},{5,13},{9,1},{13,5},{2,10},{6,14},... | collective-permute-start | bytes 393224 | tf_op jit(solution)/shard_map/ppermute | solution.py:320
  5.6 1.6 %collective-permute-start.5 = (bf16[128,512]{1,0:T(8,128)(2,1)S(1)}, bf16[128,512]{1,0:T(8,128)(2,1)S(1)}, u32[]{:S(2)}, u32[]{:S(2)}) collective-permute-start(bf16[128,512]{1,0:T(8,128)(2,1)S(1)} %constant_dynamic-update-slice_fusion.rest_4_), channel_id=1, source_target_pairs={{0,4},{4,0},{8,12},{12,8},{1,5},{5,1},{9,13},{13,9},{2,6},{6,2},{1... | collective-permute-start | bytes 393224 | tf_op jit(solution)/shard_map/ppermute | solution.py:320
  7.2 0.0 copy-start.1
  7.2 0.0 copy-start.2
  7.2 0.7 %copy-done.1 = s32[128,1]{0,1:T(1,128)S(1)} copy-done((s32[128,1]{0,1:T(1,128)S(1)}, s32[128,1]{0,1:T(1,128)}, u32[]{:S(2)}) %copy-start.1) | copy-done | bytes 536
  7.9 0.0 copy-done.2
  7.9 0.0 copy-start
  7.9 1.0 %copy-done = bf16[128,2048]{1,0:T(8,128)(2,1)S(1)} copy-done((bf16[128,2048]{1,0:T(8,128)(2,1)S(1)}, bf16[128,2048]{1,0:T(8,128)(2,1)}, u32[]{:S(2)}) %copy-start) | copy-done | bytes 524312
  8.9 0.5 %pack.1 = (bf16[784,128]{1,0:T(8,128)(2,1)S(1)}, bf16[784,128]{1,0:T(8,128)(2,1)S(1)}, bf16[544,128]{1,0:T(8,128)(2,1)S(1)}, bf16[544,128]{1,0:T(8,128)(2,1)S(1)...) custom-call(s32[1]{0:T(128)} %bitcast.me_ref, bf16[128,2048]{1,0:T(8,128)(2,1)S(1)} %copy-done, ...), custom_call_target="tpu_custom_call" | custom-call | flops 134217728 | bytes 2097152 | tf_op jit(solution)/shard_map/pack/pallas_call | solution.py:330
  9.5 0.5 %collective-permute-start = (bf16[784,128]{1,0:T(8,128)(2,1)S(1)}, bf16[784,128]{1,0:T(8,128)(2,1)S(1)}, u32[]{:S(2)}, u32[]{:S(2)}) collective-permute-start(bf16[784,128]{1,0:T(8,128)(2,1)S(1)} %get-tuple-element.16), channel_id=1, source_target_pairs={{0,4},{4,0},{8,12},{12,8},{1,5},{5,1},{9,13},{13,9},{2,6},{6,2},{1... | collective-permute-start | bytes 602120 | tf_op jit(solution)/shard_map/ppermute | solution.py:320
  10.0 0.1 collective-permute-start.3
  10.1 3.9 %collective-permute-start.4 = (bf16[544,128]{1,0:T(8,128)(2,1)S(1)}, bf16[544,128]{1,0:T(8,128)(2,1)S(1)}, u32[]{:S(2)}, u32[]{:S(2)}) collective-permute-start(bf16[544,128]{1,0:T(8,128)(2,1)S(1)} %get-tuple-element.20), channel_id=1, source_target_pairs={{0,12},{4,8},{8,4},{12,0},{1,13},{5,9},{9,5},{13,1},{2,14},{6,10},... | collective-permute-start | bytes 417800 | tf_op jit(solution)/shard_map/ppermute | solution.py:320
  13.9 0.0 collective-permute-done.6.far_ref
  13.9 0.0 collective-permute-done.5.near_ref.rest_5_
  13.9 0.9 %collective-permute-start.7 = (bf16[128,512]{1,0:T(8,128)(2,1)S(1)}, bf16[128,512]{1,0:T(8,128)(2,1)S(1)}, u32[]{:S(2)}, u32[]{:S(2)}) collective-permute-start(bf16[128,512]{1,0:T(8,128)(2,1)S(1)} %gate.1.rest_6_), channel_id=1, source_target_pairs={{0,4},{4,0},{8,12},{12,8},{1,5},{5,1},{9,13},{13,9},{2,6},{6,2},{1... | collective-permute-start | bytes 393224 | tf_op jit(solution)/shard_map/ppermute | solution.py:320
  14.8 1.4 %collective-permute-start.1 = (bf16[240,128]{1,0:T(8,128)(2,1)S(1)}, bf16[240,128]{1,0:T(8,128)(2,1)S(1)}, u32[]{:S(2)}, u32[]{:S(2)}) collective-permute-start(bf16[240,128]{1,0:T(8,128)(2,1)S(1)} %get-tuple-element.17), channel_id=1, source_target_pairs={{0,8},{4,12},{8,0},{12,4},{1,9},{5,13},{9,1},{13,5},{2,10},{6,14},... | collective-permute-start | bytes 184328 | tf_op jit(solution)/shard_map/ppermute | solution.py:320
  16.2 3.4 %collective-permute-done.3.rest_2_ = bf16[544,128]{1,0:T(8,128)(2,1)S(1)} collective-permute-done((bf16[544,128]{1,0:T(8,128)(2,1)S(1)}, bf16[544,128]{1,0:T(8,128)(2,1)S(1)}, u32[]{:S(2)}, u32[]{:S(2)}) %collective-permute-start.3) | collective-permute-done | bytes 139296 | tf_op jit(solution)/shard_map/ppermute | solution.py:320
  19.7 1.3 %collective-permute-start.2 = (bf16[240,128]{1,0:T(8,128)(2,1)S(1)}, bf16[240,128]{1,0:T(8,128)(2,1)S(1)}, u32[]{:S(2)}, u32[]{:S(2)}) collective-permute-start(bf16[240,128]{1,0:T(8,128)(2,1)S(1)} %get-tuple-element.18), channel_id=1, source_target_pairs={{0,12},{4,8},{8,4},{12,0},{1,13},{5,9},{9,5},{13,1},{2,14},{6,10},... | collective-permute-start | bytes 184328 | tf_op jit(solution)/shard_map/ppermute | solution.py:320
  21.0 3.4 %collective-permute-done.4.rest_3_ = bf16[544,128]{1,0:T(8,128)(2,1)S(1)} collective-permute-done((bf16[544,128]{1,0:T(8,128)(2,1)S(1)}, bf16[544,128]{1,0:T(8,128)(2,1)S(1)}, u32[]{:S(2)}, u32[]{:S(2)}) %collective-permute-start.4) | collective-permute-done | bytes 139296 | tf_op jit(solution)/shard_map/ppermute | solution.py:320
  24.5 0.0 collective-permute-done.rest_1_
  24.5 1.5 %collective-permute-done.7.rest_7_ = bf16[128,512]{1,0:T(8,128)(2,1)S(1)} collective-permute-done((bf16[128,512]{1,0:T(8,128)(2,1)S(1)}, bf16[128,512]{1,0:T(8,128)(2,1)S(1)}, u32[]{:S(2)}, u32[]{:S(2)}) %collective-permute-start.7) | collective-permute-done | bytes 131104 | tf_op jit(solution)/shard_map/ppermute | solution.py:320
  26.0 3.3 %attend_lead.1 = (bf16[192,2048]{1,0:T(8,128)(2,1)}, bf16[192,256]{1,0:T(8,128)(2,1)S(1)}, bf16[512,128]{1,0:T(8,128)(2,1)S(1)}, bf16[512,256]{1,0:T(8,128)(2,1)...) custom-call(s32[1]{0:T(128)} %bitcast.me_ref, bf16[784,128]{1,0:T(8,128)(2,1)S(1)} %get-tuple-element.15.rest_0_, ...), custom_call_target="tpu_custom_call" | custom-call | flops 536870912 | bytes 2097152 | tf_op jit(solution)/shard_map/attend_lead/pallas_call | solution.py:356
  29.3 0.0 collective-permute-done.1.rest_2_
  29.3 0.0 collective-permute-done.2.rest_3_
  29.3 1.6 %attend_rest.1 = bf16[192,2048]{1,0:T(8,128)(2,1)} custom-call(s32[1]{0:T(128)} %bitcast.me_ref, bf16[784,128]{1,0:T(8,128)(2,1)S(1)} %get-tuple-element.15.rest_0_, bf16[784,128]{1,0:T(8,128)(2,1)S(1)} %collective-permute-done.rest_1_, bf16[240,128]{1,0:T(8,128)(2,1)S(1)} %collective-permute-done.1.rest_2_, ...), custom_call_target="tpu_custom_call", output_to_operand_aliasing={{}: (5, {})} | custom-call | flops 536870912 | bytes 2097152 | tf_op jit(solution)/shard_map/attend_rest/pallas_call | solution.py:379
  (2 shorter events, 0.0 us)
Async XLA Ops:
  0.6 0.9 %copy-start.3 = (bf16[128,256]{1,0:T(8,128)(2,1)S(1)}, bf16[128,256]{1,0:T(8,128)(2,1)}, u32[]{:S(2)}) copy-start(bf16[128,256]{1,0:T(8,128)(2,1)} %param.7) | copy-start | bytes 196612
  1.5 12.4 %collective-permute-start.6 = (bf16[128,512]{1,0:T(8,128)(2,1)S(1)}, bf16[128,512]{1,0:T(8,128)(2,1)S(1)}, u32[]{:S(2)}, u32[]{:S(2)}) collective-permute-start(bf16[128,512]{1,0:T(8,128)(2,1)S(1)} %constant_dynamic-update-slice_fusion.rest_4_), channel_id=1, source_target_pairs={{0,8},{4,12},{8,0},{12,4},{1,9},{5,13},{9,1},{13,5},{2,10},{6,14},... | collective-permute-start | bytes 393224 | tf_op jit(solution)/shard_map/ppermute | solution.py:320
  5.6 8.3 %collective-permute-start.5 = (bf16[128,512]{1,0:T(8,128)(2,1)S(1)}, bf16[128,512]{1,0:T(8,128)(2,1)S(1)}, u32[]{:S(2)}, u32[]{:S(2)}) collective-permute-start(bf16[128,512]{1,0:T(8,128)(2,1)S(1)} %constant_dynamic-update-slice_fusion.rest_4_), channel_id=1, source_target_pairs={{0,4},{4,0},{8,12},{12,8},{1,5},{5,1},{9,13},{13,9},{2,6},{6,2},{1... | collective-permute-start | bytes 393224 | tf_op jit(solution)/shard_map/ppermute | solution.py:320
  7.2 0.7 %copy-start.1 = (s32[128,1]{0,1:T(1,128)S(1)}, s32[128,1]{0,1:T(1,128)}, u32[]{:S(2)}) copy-start(s32[128,1]{0,1:T(1,128)} %param.8) | copy-start | bytes 1540
  7.2 0.7 %copy-start.2 = (s32[128,1]{0,1:T(1,128)S(1)}, s32[128,1]{0,1:T(1,128)}, u32[]{:S(2)}) copy-start(s32[128,1]{0,1:T(1,128)} %param.9) | copy-start | bytes 1540
  7.9 1.0 %copy-start = (bf16[128,2048]{1,0:T(8,128)(2,1)S(1)}, bf16[128,2048]{1,0:T(8,128)(2,1)}, u32[]{:S(2)}) copy-start(bf16[128,2048]{1,0:T(8,128)(2,1)} %q_hbm.1) | copy-start | bytes 1572868
  9.5 15.0 %collective-permute-start = (bf16[784,128]{1,0:T(8,128)(2,1)S(1)}, bf16[784,128]{1,0:T(8,128)(2,1)S(1)}, u32[]{:S(2)}, u32[]{:S(2)}) collective-permute-start(bf16[784,128]{1,0:T(8,128)(2,1)S(1)} %get-tuple-element.16), channel_id=1, source_target_pairs={{0,4},{4,0},{8,12},{12,8},{1,5},{5,1},{9,13},{13,9},{2,6},{6,2},{1... | collective-permute-start | bytes 602120 | tf_op jit(solution)/shard_map/ppermute | solution.py:320
  10.0 9.7 %collective-permute-start.3 = (bf16[544,128]{1,0:T(8,128)(2,1)S(1)}, bf16[544,128]{1,0:T(8,128)(2,1)S(1)}, u32[]{:S(2)}, u32[]{:S(2)}) collective-permute-start(bf16[544,128]{1,0:T(8,128)(2,1)S(1)} %get-tuple-element.19), channel_id=1, source_target_pairs={{0,8},{4,12},{8,0},{12,4},{1,9},{5,13},{9,1},{13,5},{2,10},{6,14},... | collective-permute-start | bytes 417800 | tf_op jit(solution)/shard_map/ppermute | solution.py:320
  10.1 14.4 %collective-permute-start.4 = (bf16[544,128]{1,0:T(8,128)(2,1)S(1)}, bf16[544,128]{1,0:T(8,128)(2,1)S(1)}, u32[]{:S(2)}, u32[]{:S(2)}) collective-permute-start(bf16[544,128]{1,0:T(8,128)(2,1)S(1)} %get-tuple-element.20), channel_id=1, source_target_pairs={{0,12},{4,8},{8,4},{12,0},{1,13},{5,9},{9,5},{13,1},{2,14},{6,10},... | collective-permute-start | bytes 417800 | tf_op jit(solution)/shard_map/ppermute | solution.py:320
  13.9 12.0 %collective-permute-start.7 = (bf16[128,512]{1,0:T(8,128)(2,1)S(1)}, bf16[128,512]{1,0:T(8,128)(2,1)S(1)}, u32[]{:S(2)}, u32[]{:S(2)}) collective-permute-start(bf16[128,512]{1,0:T(8,128)(2,1)S(1)} %gate.1.rest_6_), channel_id=1, source_target_pairs={{0,4},{4,0},{8,12},{12,8},{1,5},{5,1},{9,13},{13,9},{2,6},{6,2},{1... | collective-permute-start | bytes 393224 | tf_op jit(solution)/shard_map/ppermute | solution.py:320
  14.8 14.5 %collective-permute-start.1 = (bf16[240,128]{1,0:T(8,128)(2,1)S(1)}, bf16[240,128]{1,0:T(8,128)(2,1)S(1)}, u32[]{:S(2)}, u32[]{:S(2)}) collective-permute-start(bf16[240,128]{1,0:T(8,128)(2,1)S(1)} %get-tuple-element.17), channel_id=1, source_target_pairs={{0,8},{4,12},{8,0},{12,4},{1,9},{5,13},{9,1},{13,5},{2,10},{6,14},... | collective-permute-start | bytes 184328 | tf_op jit(solution)/shard_map/ppermute | solution.py:320
  19.7 9.7 %collective-permute-start.2 = (bf16[240,128]{1,0:T(8,128)(2,1)S(1)}, bf16[240,128]{1,0:T(8,128)(2,1)S(1)}, u32[]{:S(2)}, u32[]{:S(2)}) collective-permute-start(bf16[240,128]{1,0:T(8,128)(2,1)S(1)} %get-tuple-element.18), channel_id=1, source_target_pairs={{0,12},{4,8},{8,4},{12,0},{1,13},{5,9},{9,5},{13,1},{2,14},{6,10},... | collective-permute-start | bytes 184328 | tf_op jit(solution)/shard_map/ppermute | solution.py:320
